TPU v7x, 32 devices: a whole 2x2x4 slice. The times are simulated.
32 devices in a mesh: fsdp: 16 (over z, y, x), tp: 2 (over core).
Axes of the slice: x: 2, y: 2, z: 4, core: 2. Of those that a mesh axis runs over, the one named last changes fastest.
Arguments:
- hidden: bfloat16 [8192, 1536], P(('fsdp', 'tp')), may hold values from -6 to 6
- document_index: int32 [8192], replicated, may hold values from 0 to 8192, as said below
- attn_gain: bfloat16 [1, 1536], P(None, 'fsdp'), may hold values from 0.25 to 1.75
- q_weight: bfloat16 [1, 1536, 1536], P(None, 'fsdp', 'tp'), may hold values from -0.21875 to 0.21875
- key_matrix: bfloat16 [1, 1536, 768], P(None, 'fsdp', 'tp'), may hold values from -0.21875 to 0.21875
- value_matrix: bfloat16 [1, 1536, 768], P(None, 'fsdp', 'tp'), may hold values from -0.15625 to 0.15625
- out_weight: bfloat16 [1, 1536, 1536], P(None, 'fsdp', 'tp'), may hold values from -0.625 to 0.625
- mlp_gain: bfloat16 [1, 1536], P(None, 'fsdp'), may hold values from 0.25 to 1.75
- gate_weight: bfloat16 [1, 1536, 4096], P(None, 'fsdp', 'tp'), may hold values from -0.15625 to 0.15625
- up_weight: bfloat16 [1, 1536, 4096], P(None, 'fsdp', 'tp'), may hold values from -0.15625 to 0.15625
- down_weight: bfloat16 [1, 1536, 4096], P(None, 'fsdp', 'tp'), may hold values from -0.125 to 0.125
- cotangent: bfloat16 [8192, 1536], P(('fsdp', 'tp')), may hold values from -6 to 6
Outputs:
- output: bfloat16 [8192, 1536], P(('fsdp', 'tp'))
- input_grad: float32 [8192, 1536], P(('fsdp', 'tp'))
- attn_gain_grad: float32 [1, 1536], P(None, 'fsdp')
- q_grad: float32 [1, 1536, 1536], P(None, 'fsdp', 'tp')
- k_grad: float32 [1, 1536, 768], P(None, 'fsdp', 'tp')
- v_grad: float32 [1, 1536, 768], P(None, 'fsdp', 'tp')
- out_grad: float32 [1, 1536, 1536], P(None, 'fsdp', 'tp')
- mlp_gain_grad: float32 [1, 1536], P(None, 'fsdp')
- gate_grad: float32 [1, 1536, 4096], P(None, 'fsdp', 'tp')
- up_grad: float32 [1, 1536, 4096], P(None, 'fsdp', 'tp')
- down_grad: float32 [1, 1536, 4096], P(None, 'fsdp', 'tp')
Inputs may be any that keep to these rules, and one draw needn't show every extreme that they name: `document_index`: sequence s holds ids 0 and ids in (s * 4096, (s + 1) * 4096]; its last document has id (s + 1) * 4096. A document is a run of one nonzero id, and ids never fall inside a sequence except to 0. Every sequence ends with 1 to 128 padding tokens of id 0. In every sequence one document starts within its first 257 tokens and ends within its last 512 tokens; the others start at random places.
All inputs are finite; a program needn't handle non-finite values.
Results may differ from a plain program's by a relative error of at most 0.015.
The roundings to bfloat16 on the way count: a program that leaves them out, or rounds other values in their place, can miss the bound.
Values may be sent and summed in bfloat16 or wider, within the bound.
No kernel may reach another device: no remote copies, remote signals or barrier semaphores. Data moves between devices by JAX's collectives and lax.ppermute only.
A program may use at most 256 MiB of HBM per device.

v0:
```python
import jax
import jax.numpy as jnp
from jax import lax
from jax.sharding import PartitionSpec as P

HEAD_SIZE = 96
SPANS = 8
PACKED_LENGTH = 4096


rope_base = 100000.0
norm_eps = 1e-05
masked_score = -1000000000.0


def passed_along(value, axis, steps):
    count = lax.axis_size(axis)
    leading, last = (max(0, -steps), min(count, count - steps))
    return lax.ppermute(value, axis, [(source, source + steps) for source in range(leading, last)])


def rms_factor(stream):
    return lax.rsqrt(jnp.mean(stream * stream, axis=-1, keepdims=True) + norm_eps)


def apply_rotary(values_in, token_positions, direction):
    half = values_in.shape[-1] // 2
    freq = rope_base ** (-2.0 * jnp.arange(half, dtype=jnp.float32) / values_in.shape[-1])
    angle = token_positions.astype(jnp.float32)[:, None] * freq[None, :]
    cosine = jnp.cos(angle)[:, None, :]
    sine = direction * jnp.sin(angle)[:, None, :]
    first = values_in[..., :half]
    second = values_in[..., half:]
    return jnp.concatenate(
        [first * cosine - second * sine, second * cosine + first * sine], axis=-1
    )


def matmul(left, right):
    return jnp.dot(left, right, preferred_element_type=jnp.float32)


def matmul_nt(left, right):
    return lax.dot_general(
        left, right, (((1,), (1,)), ((), ())), preferred_element_type=jnp.float32
    )


def matmul_tn(left, right):
    return lax.dot_general(
        left, right, (((0,), (0,)), ((), ())), preferred_element_type=jnp.float32
    )


def widen(rows_low):
    return lax.all_gather(rows_low, "tp", axis=0, tiled=True)


def narrow(term_fn, own_rows):
    return lax.psum_scatter(
        term_fn(jnp.int32(0), own_rows * lax.axis_size("tp")), "tp", scatter_dimension=0, tiled=True
    )


def block_scores(query_rows, keys_block, allowed, scale):
    raw = jnp.einsum("qkgd,skd->kgqs", query_rows, keys_block, preferred_element_type=jnp.float32)
    return jnp.where(allowed[None, None], raw * scale, masked_score)


def total_step(query_rows, keys_block, allowed, scale, carry):
    best, total = carry
    scores = block_scores(query_rows, keys_block, allowed, scale)
    larger = jnp.maximum(best, jnp.max(scores, axis=-1))
    total = total * jnp.exp(best - larger) + jnp.sum(jnp.exp(scores - larger[..., None]), axis=-1)
    return (larger, total)


def output_step(query_rows, keys_block, values_block, allowed, scale, lse, carry):
    scores = block_scores(query_rows, keys_block, allowed, scale)
    probs = jnp.exp(scores - lse[..., None]).astype(jnp.bfloat16)
    return carry + jnp.einsum(
        "kgqs,skd->qkgd", probs, values_block, preferred_element_type=jnp.float32
    )


def gradient_step(query_rows, keys_block, values_block, allowed, scale, lse, dout, delta, carry):
    scores = block_scores(query_rows, keys_block, allowed, scale)
    probs = jnp.exp(scores - lse[..., None])
    dprobs = jnp.einsum("qkgd,skd->kgqs", dout, values_block, preferred_element_type=jnp.float32)
    dscores = (probs * (dprobs - delta[..., None])).astype(jnp.bfloat16)
    carry = carry + jnp.einsum(
        "kgqs,skd->qkgd", dscores, keys_block, preferred_element_type=jnp.float32
    )
    dkey_block = (
        jnp.einsum("kgqs,qkgd->skd", dscores, query_rows, preferred_element_type=jnp.float32)
        * scale
    )
    dvalue_block = jnp.einsum(
        "kgqs,qkgd->skd", probs.astype(jnp.bfloat16), dout, preferred_element_type=jnp.float32
    )
    return (carry, dkey_block, dvalue_block)


def attend(query_rows, blocks, masks, scale):
    stat_shape = (query_rows.shape[1], query_rows.shape[2], query_rows.shape[0])
    carry = (jnp.full(stat_shape, masked_score, jnp.float32), jnp.zeros(stat_shape, jnp.float32))
    for kv_pair, allowed in zip(blocks, masks):
        carry = total_step(query_rows, kv_pair[0], allowed, scale, carry)
    lse = carry[0] + jnp.log(carry[1])
    result = jnp.zeros(query_rows.shape, jnp.float32)
    for kv_pair, allowed in zip(blocks, masks):
        result = output_step(query_rows, kv_pair[0], kv_pair[1], allowed, scale, lse, result)
    return (lse, result)


def norm_backward(stream, factor, gain, dnormed):
    gain_full = gain.astype(jnp.float32)
    gain_part = jnp.sum(dnormed * stream * factor, axis=0)
    scaled = dnormed * gain_full
    dstream = factor * scaled - stream * factor**3 * jnp.mean(
        scaled * stream, axis=-1, keepdims=True
    )
    return (dstream, gain_part)


def attention_block(stream, weights, token_positions, masks, scale):
    gain, q_part, k_part, v_part, o_part = weights
    factor = rms_factor(stream)
    normalized_input = widen((stream * factor * gain.astype(jnp.float32)).astype(jnp.bfloat16))
    token_row_count = normalized_input.shape[0]
    q_heads = q_part.shape[1] // HEAD_SIZE
    kv_heads = k_part.shape[1] // HEAD_SIZE
    query_rows = apply_rotary(
        matmul(normalized_input, q_part).reshape(token_row_count, q_heads, HEAD_SIZE),
        token_positions,
        1.0,
    )
    query_rows = query_rows.astype(jnp.bfloat16).reshape(
        token_row_count, kv_heads, q_heads // kv_heads, HEAD_SIZE
    )
    keys_own = apply_rotary(
        matmul(normalized_input, k_part).reshape(token_row_count, kv_heads, HEAD_SIZE),
        token_positions,
        1.0,
    ).astype(jnp.bfloat16)
    values_own = (
        matmul(normalized_input, v_part)
        .astype(jnp.bfloat16)
        .reshape(token_row_count, kv_heads, HEAD_SIZE)
    )
    blocks = [(keys_own, values_own)]
    for offset in range(1, len(masks)):
        blocks.append(passed_along((keys_own, values_own), "fsdp", offset))
    lse, out_full = attend(query_rows, blocks, masks, scale)
    attended = out_full.astype(jnp.bfloat16).reshape(token_row_count, q_heads * HEAD_SIZE)

    def out_term(start, count):
        return matmul_nt(attended, o_part)

    mixed_heads = stream + narrow(out_term, stream.shape[0])
    return (mixed_heads, (factor, normalized_input, query_rows, blocks, lse, out_full, attended))


def attention_backward(stream, weights, saved, masks, token_positions, scale, dstream):
    gain, q_part, k_part, v_part, o_part = weights
    factor, normalized_input, query_rows, blocks, lse, out_full, attended = saved
    token_row_count = normalized_input.shape[0]
    q_heads = q_part.shape[1] // HEAD_SIZE
    dmixed = widen(dstream.astype(jnp.bfloat16))
    grad_out = matmul_tn(dmixed, attended)
    dout = matmul(dmixed, o_part).astype(jnp.bfloat16).reshape(query_rows.shape)
    delta = jnp.transpose(jnp.sum(dout.astype(jnp.float32) * out_full, axis=-1), (1, 2, 0))
    dquery = jnp.zeros(query_rows.shape, jnp.float32)
    dkeys = None
    dvalues = None
    for offset in range(len(blocks)):
        keys_block, values_block = blocks[offset]
        dquery, dkey_block, dvalue_block = gradient_step(
            query_rows, keys_block, values_block, masks[offset], scale, lse, dout, delta, dquery
        )
        if offset == 0:
            dkeys = dkey_block
            dvalues = dvalue_block
        else:
            returned = passed_along((dkey_block, dvalue_block), "fsdp", -offset)
            dkeys = dkeys + returned[0]
            dvalues = dvalues + returned[1]
    dq_low = (
        apply_rotary(
            (dquery * scale).reshape(token_row_count, q_heads, HEAD_SIZE), token_positions, -1.0
        )
        .astype(jnp.bfloat16)
        .reshape(token_row_count, q_heads * HEAD_SIZE)
    )
    dk_low = (
        apply_rotary(dkeys, token_positions, -1.0).astype(jnp.bfloat16).reshape(token_row_count, -1)
    )
    dv_low = dvalues.astype(jnp.bfloat16).reshape(token_row_count, -1)

    def attention_back_term(start, count):
        total = matmul_nt(dq_low, q_part)
        total = total + matmul_nt(dk_low, k_part)
        return total + matmul_nt(dv_low, v_part)

    dnormed = narrow(attention_back_term, stream.shape[0])
    dstream_norm, gain_part = norm_backward(stream, factor, gain, dnormed)
    parts = (
        gain_part,
        matmul_tn(normalized_input, dq_low),
        matmul_tn(normalized_input, dk_low),
        matmul_tn(normalized_input, dv_low),
        grad_out,
    )
    return (dstream + dstream_norm, parts)


def mlp_block(stream, weights, finish):
    gain, gate_part, up_weights, down_part = weights
    factor = rms_factor(stream)
    normalized_input = widen((stream * factor * gain.astype(jnp.float32)).astype(jnp.bfloat16))
    gate = matmul(normalized_input, gate_part)
    up_part = matmul(normalized_input, up_weights)
    act = (gate / (1.0 + jnp.exp(-gate)) * up_part).astype(jnp.bfloat16)
    saved = (factor, normalized_input, gate, up_part, act)
    if not finish:
        return (stream, saved)

    def down_term(start, count):
        return matmul_nt(act, down_part)

    return (stream + narrow(down_term, stream.shape[0]), saved)


def mlp_backward(stream, weights, saved, dstream):
    gain, gate_part, up_weights, down_part = weights
    factor, normalized_input, gate, up_part, act = saved
    dmixed = widen(dstream.astype(jnp.bfloat16))
    dact = matmul(dmixed, down_part)
    grad_down = matmul_tn(dmixed, act)
    sigma = 1.0 / (1.0 + jnp.exp(-gate))
    dgate = (dact * up_part * sigma * (1.0 + gate * (1.0 - sigma))).astype(jnp.bfloat16)
    dup = (dact * gate * sigma).astype(jnp.bfloat16)

    def mlp_back_term(start, count):
        total = matmul_nt(dgate, gate_part)
        return total + matmul_nt(dup, up_weights)

    dnormed = narrow(mlp_back_term, stream.shape[0])
    dstream_norm, gain_part = norm_backward(stream, factor, gain, dnormed)
    parts = (
        gain_part,
        matmul_tn(normalized_input, dgate),
        matmul_tn(normalized_input, dup),
        grad_down,
    )
    return (dstream + dstream_norm, parts)


def body(
    hidden,
    document_index,
    attn_gain,
    q_weight,
    key_matrix,
    value_matrix,
    out_weight,
    mlp_gain,
    gate_weight,
    up_weight,
    down_weight,
    cotangent,
):
    own_rows = hidden.shape[0]
    span_len = own_rows * lax.axis_size("tp")
    shard = lax.axis_index("fsdp")
    place = shard % SPANS
    seq_ids = lax.dynamic_slice_in_dim(
        document_index, shard // SPANS * PACKED_LENGTH, PACKED_LENGTH
    )
    seq_index = jnp.arange(PACKED_LENGTH, dtype=jnp.int32)
    before = jnp.concatenate([jnp.full((1,), -1, jnp.int32), seq_ids[:-1]])
    starts = lax.cummax(jnp.where(seq_ids != before, seq_index, 0), axis=0)
    seq_pos = seq_index - starts
    query_at = place * span_len
    query_ids = lax.dynamic_slice_in_dim(seq_ids, query_at, span_len)
    token_positions = lax.dynamic_slice_in_dim(seq_pos, query_at, span_len)
    query_index = query_at + jnp.arange(span_len, dtype=jnp.int32)
    masks = []
    for offset in range(SPANS):
        key_at = jnp.maximum(place - offset, 0) * span_len
        key_ids = lax.dynamic_slice_in_dim(seq_ids, key_at, span_len)
        key_index = key_at + jnp.arange(span_len, dtype=jnp.int32)
        allowed = (
            (query_ids[:, None] == key_ids[None, :])
            & (key_index[None, :] <= query_index[:, None])
            & (place >= offset)
        )
        masks.append(allowed)
    row_ids = lax.dynamic_slice_in_dim(query_ids, lax.axis_index("tp") * own_rows, own_rows)
    scale = HEAD_SIZE ** (-0.5)
    layer_count = q_weight.shape[0]

    def fetch_attention(decoder_layer_index):
        return (
            lax.all_gather(attn_gain[decoder_layer_index], "fsdp", axis=0, tiled=True),
            lax.all_gather(q_weight[decoder_layer_index], "fsdp", axis=0, tiled=True),
            lax.all_gather(key_matrix[decoder_layer_index], "fsdp", axis=0, tiled=True),
            lax.all_gather(value_matrix[decoder_layer_index], "fsdp", axis=0, tiled=True),
            lax.all_gather(out_weight[decoder_layer_index], "fsdp", axis=0, tiled=True),
        )

    def fetch_mlp(decoder_layer_index):
        return (
            lax.all_gather(mlp_gain[decoder_layer_index], "fsdp", axis=0, tiled=True),
            lax.all_gather(gate_weight[decoder_layer_index], "fsdp", axis=0, tiled=True),
            lax.all_gather(up_weight[decoder_layer_index], "fsdp", axis=0, tiled=True),
            lax.all_gather(down_weight[decoder_layer_index], "fsdp", axis=0, tiled=True),
        )

    stream = hidden.astype(jnp.float32)
    kept = []
    decoder_layer_index = 0
    inputs = [stream]
    attn_set = fetch_attention(decoder_layer_index)
    stream, unused_attn = attention_block(stream, attn_set, token_positions, masks, scale)
    mlp_set = fetch_mlp(decoder_layer_index)
    stream, unused_mlp = mlp_block(stream, mlp_set, True)
    kept.append((attn_set, mlp_set))
    output = stream.astype(jnp.bfloat16)
    dstream = cotangent.astype(jnp.float32) * (row_ids != 0).astype(jnp.float32)[:, None]
    attn_sums = [None] * layer_count
    mlp_sums = [None] * layer_count
    for decoder_layer_index in reversed(range(layer_count)):
        attn_set = fetch_attention(decoder_layer_index)
        mlp_set = fetch_mlp(decoder_layer_index)
        middle, attn_saved = attention_block(
            inputs[decoder_layer_index], attn_set, token_positions, masks, scale
        )
        unused_stream, mlp_saved = mlp_block(middle, mlp_set, False)
        dstream, mlp_parts = mlp_backward(middle, mlp_set, mlp_saved, dstream)
        mlp_sums[decoder_layer_index] = (
            lax.psum_scatter(mlp_parts[0], "fsdp", scatter_dimension=0, tiled=True),
            lax.psum_scatter(mlp_parts[1], "fsdp", scatter_dimension=0, tiled=True),
            lax.psum_scatter(mlp_parts[2], "fsdp", scatter_dimension=0, tiled=True),
            lax.psum_scatter(mlp_parts[3], "fsdp", scatter_dimension=0, tiled=True),
        )
        dstream, attn_parts = attention_backward(
            inputs[decoder_layer_index],
            attn_set,
            attn_saved,
            masks,
            token_positions,
            scale,
            dstream,
        )
        attn_sums[decoder_layer_index] = (
            lax.psum_scatter(attn_parts[0], "fsdp", scatter_dimension=0, tiled=True),
            lax.psum_scatter(attn_parts[1], "fsdp", scatter_dimension=0, tiled=True),
            lax.psum_scatter(attn_parts[2], "fsdp", scatter_dimension=0, tiled=True),
            lax.psum_scatter(attn_parts[3], "fsdp", scatter_dimension=0, tiled=True),
            lax.psum_scatter(attn_parts[4], "fsdp", scatter_dimension=0, tiled=True),
        )
    attn_gain_part = jnp.stack([entry[0] for entry in attn_sums])
    mlp_gain_part = jnp.stack([entry[0] for entry in mlp_sums])
    attn_gain_grad, mlp_gain_grad = lax.psum((attn_gain_part, mlp_gain_part), "tp")
    q_grad = jnp.stack([entry[1] for entry in attn_sums])
    k_grad = jnp.stack([entry[2] for entry in attn_sums])
    v_grad = jnp.stack([entry[3] for entry in attn_sums])
    out_grad = jnp.stack([entry[4] for entry in attn_sums])
    gate_grad = jnp.stack([entry[1] for entry in mlp_sums])
    up_grad = jnp.stack([entry[2] for entry in mlp_sums])
    down_grad = jnp.stack([entry[3] for entry in mlp_sums])
    return (
        output,
        dstream,
        attn_gain_grad,
        q_grad,
        k_grad,
        v_grad,
        out_grad,
        mlp_gain_grad,
        gate_grad,
        up_grad,
        down_grad,
    )


def solution(mesh):
    placed = (
        P(("fsdp", "tp"), None),
        P(),
        P(None, "fsdp"),
        P(None, "fsdp", "tp"),
        P(None, "fsdp", "tp"),
        P(None, "fsdp", "tp"),
        P(None, "fsdp", "tp"),
        P(None, "fsdp"),
        P(None, "fsdp", "tp"),
        P(None, "fsdp", "tp"),
        P(None, "fsdp", "tp"),
        P(("fsdp", "tp"), None),
    )
    return jax.shard_map(
        body,
        mesh=mesh,
        in_specs=placed,
        out_specs=(
            P(("fsdp", "tp"), None),
            P(("fsdp", "tp"), None),
            P(None, "fsdp"),
            P(None, "fsdp", "tp"),
            P(None, "fsdp", "tp"),
            P(None, "fsdp", "tp"),
            P(None, "fsdp", "tp"),
            P(None, "fsdp"),
            P(None, "fsdp", "tp"),
            P(None, "fsdp", "tp"),
            P(None, "fsdp", "tp"),
        ),
        check_vma=False,
    )
```

profile of v0, /device:TPU:1, one launch (start us, length us, event | category | flops | bytes accessed | tf_op | source)
XLA Modules:
  0.0 2532.2 jit_solution(17257215712914213496)
XLA Ops:
  12.9 36.1 %all-reduce.6 = (bf16[1536]{0:T(1024)(128)(2,1)S(1)}, bf16[1536]{0:T(1024)(128)(2,1)S(1)}) all-reduce(bf16[1536]{0:T(1024)(128)(2,1)S(1)} %dynamic-update-slice, bf16[1536]{0:T(1024)(128)(2,1)S(1)} %dynamic-update-slice.1), channel_id=2, replica_groups=mesh['fsdp'=16,'tp'=2] {'fsdp'}, use_global_device_ids=true, to_apply=%add | all-reduce | flops 3072 | bytes 12288
  65.4 58.3 %all-gather.29.cloned.1.call-done = bf16[1,1536,384]{2,1,0:T(8,128)(2,1)} async-done(((bf16[1,96,384]{2,1,0:T(8,128)(2,1)}), bf16[1,1536,384]{2,1,0:T(8,128)(2,1)}) %all-gather.29.cloned.1.call-update) | async-done | bytes 1179664 | tf_op jit(solution)/shard_map/all_gather | solution.py:308
  141.2 50.3 %all-gather.31.cloned.1.call-done = bf16[1,1536,384]{2,1,0:T(8,128)(2,1)} async-done(((bf16[1,96,384]{2,1,0:T(8,128)(2,1)}), bf16[1,1536,384]{2,1,0:T(8,128)(2,1)}) %all-gather.31.cloned.1.call-update) | async-done | bytes 1179664 | tf_op jit(solution)/shard_map/all_gather | solution.py:307
  198.8 57.8 %all-gather.33.cloned.1.call-done = bf16[1,1536,768]{2,1,0:T(8,128)(2,1)} async-done(((bf16[1,96,768]{2,1,0:T(8,128)(2,1)}), bf16[1,1536,768]{2,1,0:T(8,128)(2,1)}) %all-gather.33.cloned.1.call-update) | async-done | bytes 2359312 | tf_op jit(solution)/shard_map/all_gather | solution.py:306
  308.9 18.2 collective-permute-start.5
  332.5 28.5 %collective-permute-start.6 = (bf16[512,4,96]{0,2,1:T(8,128)(2,1)}, bf16[512,4,96]{0,2,1:T(8,128)(2,1)S(1)}, u32[]{:S(2)}, u32[]{:S(2)}) collective-permute-start(bf16[512,4,96]{0,2,1:T(8,128)(2,1)} %pad_maximum_fusion.2), channel_id=1, source_target_pairs={{0,14},{2,16},{4,18},{6,20},{8,22},{10,24},{12,26},{14,28},{16,30}... | collective-permute-start | bytes 1179656 | tf_op jit(solution)/shard_map/ppermute | solution.py:19
  487.4 96.9 %all-gather.41.cloned.1.call-done = bf16[1,1536,2048]{2,1,0:T(8,128)(2,1)} async-done(((bf16[1,96,2048]{2,1,0:T(8,128)(2,1)}), bf16[1,1536,2048]{2,1,0:T(8,128)(2,1)}) %all-gather.41.cloned.1.call-update) | async-done | bytes 6291472 | tf_op jit(solution)/shard_map/all_gather | solution.py:317
  593.0 87.0 %all-gather.39.cloned.1.call-done = bf16[1,1536,2048]{2,1,0:T(8,128)(2,1)} async-done(((bf16[1,96,2048]{2,1,0:T(8,128)(2,1)}), bf16[1,1536,2048]{2,1,0:T(8,128)(2,1)}) %all-gather.39.cloned.1.call-update) | async-done | bytes 6291472 | tf_op jit(solution)/shard_map/all_gather | solution.py:316
  700.4 88.3 %all-gather.37.cloned.1.call-done = bf16[1,1536,2048]{2,1,0:T(8,128)(2,1)} async-done(((bf16[1,96,2048]{2,1,0:T(8,128)(2,1)}), bf16[1,1536,2048]{2,1,0:T(8,128)(2,1)}) %all-gather.37.cloned.1.call-update) | async-done | bytes 6291472 | tf_op jit(solution)/shard_map/all_gather | solution.py:315
  980.2 18.1 collective-permute-done.16
  999.5 37.3 %collective-permute-done.17 = f32[512,4,96]{0,2,1:T(8,128)} collective-permute-done((f32[512,4,96]{0,2,1:T(8,128)}, f32[512,4,96]{0,2,1:T(8,128)}, u32[]{:S(2)}, u32[]{:S(2)}) %collective-permute-start.17) | collective-permute-done | bytes 786464 | tf_op jit(solution)/shard_map/ppermute | solution.py:19
  1067.7 57.8 %collective-permute-done.23 = f32[512,4,96]{0,2,1:T(8,128)S(1)} collective-permute-done((f32[512,4,96]{0,2,1:T(8,128)}, f32[512,4,96]{0,2,1:T(8,128)S(1)}, u32[]{:S(2)}, u32[]{:S(2)}) %collective-permute-start.23) | collective-permute-done | bytes 786464 | tf_op jit(solution)/shard_map/ppermute | solution.py:19
  1125.5 71.1 %collective-permute-done.24 = f32[512,4,96]{0,2,1:T(8,128)S(1)} collective-permute-done((f32[512,4,96]{0,2,1:T(8,128)S(1)}, f32[512,4,96]{0,2,1:T(8,128)S(1)}, u32[]{:S(2)}, u32[]{:S(2)}) %collective-permute-start.24) | collective-permute-done | bytes 786464 | tf_op jit(solution)/shard_map/ppermute | solution.py:19
  1196.6 38.7 %collective-permute-done.26 = f32[512,4,96]{0,2,1:T(8,128)S(1)} collective-permute-done((f32[512,4,96]{0,2,1:T(8,128)S(1)}, f32[512,4,96]{0,2,1:T(8,128)S(1)}, u32[]{:S(2)}, u32[]{:S(2)}) %collective-permute-start.26) | collective-permute-done | bytes 786464 | tf_op jit(solution)/shard_map/ppermute | solution.py:19
  1282.7 61.4 %reduce-scatter.18.cloned.1.call-done = f32[256,1536]{1,0:T(8,128)} async-done(((f32[512,1536]{1,0:T(8,128)}), f32[256,1536]{1,0:T(8,128)}) %reduce-scatter.18.cloned.1.call-update) | async-done | bytes 1572880 | tf_op jit(solution)/shard_map/reduce_scatter | solution.py:60
  1345.9 93.0 %all-reduce.4 = (f32[1536]{0:T(1024)S(1)}, f32[1536]{0:T(1024)S(1)}) all-reduce(f32[1536]{0:T(1024)S(1)} %get-tuple-element.13, f32[1536]{0:T(1024)S(1)} %copy-done.69), channel_id=15, replica_groups=mesh['fsdp'=16,'tp'=2] {'fsdp'}, use_global_device_ids=true, to_apply=%region_28.29.clone | all-reduce | flops 3072 | bytes 24576
  1439.1 17.6 all-reduce.5
  1459.6 16.9 reduce-scatter.24.cloned.1.call-done
  1476.6 132.7 %reduce-scatter.22.cloned.1.call-done = f32[96,384]{1,0:T(8,128)} async-done(((f32[1536,384]{1,0:T(8,128)}), f32[96,384]{1,0:T(8,128)}) %reduce-scatter.22.cloned.1.call-update) | async-done | bytes 147472 | tf_op jit(solution)/shard_map/reduce_scatter | solution.py:359
  1609.3 141.6 %reduce-scatter.20.cloned.1.call-done = f32[96,768]{1,0:T(8,128)} async-done(((f32[1536,768]{1,0:T(8,128)}), f32[96,768]{1,0:T(8,128)}) %reduce-scatter.20.cloned.1.call-update) | async-done | bytes 294928 | tf_op jit(solution)/shard_map/reduce_scatter | solution.py:358
  1750.9 142.8 %reduce-scatter.26.cloned.1.call-done = f32[96,768]{1,0:T(8,128)} async-done(((f32[1536,768]{1,0:T(8,128)}), f32[96,768]{1,0:T(8,128)}) %reduce-scatter.26.cloned.1.call-update) | async-done | bytes 294928 | tf_op jit(solution)/shard_map/reduce_scatter | solution.py:361
  1893.7 210.7 %reduce-scatter.28.cloned.1.call-done = f32[96,2048]{1,0:T(8,128)} async-done(((f32[1536,2048]{1,0:T(8,128)}), f32[96,2048]{1,0:T(8,128)}) %reduce-scatter.28.cloned.1.call-update) | async-done | bytes 786448 | tf_op jit(solution)/shard_map/reduce_scatter | solution.py:343
  2104.4 210.8 %reduce-scatter.30.cloned.1.call-done = f32[96,2048]{1,0:T(8,128)} async-done(((f32[1536,2048]{1,0:T(8,128)}), f32[96,2048]{1,0:T(8,128)}) %reduce-scatter.30.cloned.1.call-update) | async-done | bytes 786448 | tf_op jit(solution)/shard_map/reduce_scatter | solution.py:344
  2315.2 209.7 %reduce-scatter.32.cloned.1.call-done = f32[96,2048]{1,0:T(8,128)} async-done(((f32[1536,2048]{1,0:T(8,128)}), f32[96,2048]{1,0:T(8,128)}) %reduce-scatter.32.cloned.1.call-update) | async-done | bytes 786448 | tf_op jit(solution)/shard_map/reduce_scatter | solution.py:345
  (461 shorter events, 532.7 us)
Async XLA Ops:
  52.6 138.8 %all-gather.31.cloned.1.call-start = ((), (), s32[]{:S(2)}) async-start(), calls=%async_computation.27 | async-start | bytes 1253376 | tf_op jit(solution)/shard_map/all_gather | solution.py:307
  53.4 203.3 %all-gather.33.cloned.1.call-start = ((), (), s32[]{:S(2)}) async-start(), calls=%async_computation.28 | async-start | bytes 2506752 | tf_op jit(solution)/shard_map/all_gather | solution.py:306
  54.0 399.4 %all-gather.35.cloned.1.call-start = ((), (), s32[]{:S(2)}) async-start(), calls=%async_computation.29 | async-start | bytes 2506752 | tf_op jit(solution)/shard_map/all_gather | solution.py:309
  54.5 419.7 %reduce-scatter.12.cloned.1.call-start = ((), (), s32[]{:S(2)}) async-start(), calls=%async_computation.12 | async-start | bytes 4718592 | tf_op jit(solution)/shard_map/reduce_scatter | solution.py:60
  127.0 316.2 %collective-permute-start.12 = (bf16[512,4,96]{0,2,1:T(8,128)(2,1)}, bf16[512,4,96]{0,2,1:T(8,128)(2,1)}, u32[]{:S(2)}, u32[]{:S(2)}) collective-permute-start(bf16[512,4,96]{0,2,1:T(8,128)(2,1)} %bitcast.3), channel_id=1, source_target_pairs={{0,12},{2,14},{4,16},{6,18},{8,20},{10,22},{12,24},{14,26},{16,28}... | collective-permute-start | bytes 1179656 | tf_op jit(solution)/shard_map/ppermute | solution.py:19
  131.0 307.6 %collective-permute-start.11 = (bf16[512,4,96]{0,2,1:T(8,128)(2,1)}, bf16[512,4,96]{0,2,1:T(8,128)(2,1)}, u32[]{:S(2)}, u32[]{:S(2)}) collective-permute-start(bf16[512,4,96]{0,2,1:T(8,128)(2,1)} %bitcast.3), channel_id=1, source_target_pairs={{0,10},{2,12},{4,14},{6,16},{8,18},{10,20},{12,22},{14,24},{16,26}... | collective-permute-start | bytes 1179656 | tf_op jit(solution)/shard_map/ppermute | solution.py:19
  134.3 299.5 %collective-permute-start.10 = (bf16[512,4,96]{0,2,1:T(8,128)(2,1)}, bf16[512,4,96]{0,2,1:T(8,128)(2,1)}, u32[]{:S(2)}, u32[]{:S(2)}) collective-permute-start(bf16[512,4,96]{0,2,1:T(8,128)(2,1)} %bitcast.3), channel_id=1, source_target_pairs={{0,8},{2,10},{4,12},{6,14},{8,16},{10,18},{12,20},{14,22},{16,24},... | collective-permute-start | bytes 1179656 | tf_op jit(solution)/shard_map/ppermute | solution.py:19
  137.3 291.6 %collective-permute-start.9 = (bf16[512,4,96]{0,2,1:T(8,128)(2,1)}, bf16[512,4,96]{0,2,1:T(8,128)(2,1)}, u32[]{:S(2)}, u32[]{:S(2)}) collective-permute-start(bf16[512,4,96]{0,2,1:T(8,128)(2,1)} %bitcast.3), channel_id=1, source_target_pairs={{0,6},{2,8},{4,10},{6,12},{8,14},{10,16},{12,18},{14,20},{16,22},{... | collective-permute-start | bytes 1179656 | tf_op jit(solution)/shard_map/ppermute | solution.py:19
  460.5 219.5 %all-gather.39.cloned.1.call-start = ((), (), s32[]{:S(2)}) async-start(), calls=%async_computation.31 | async-start | bytes 6684672 | tf_op jit(solution)/shard_map/all_gather | solution.py:316
  461.2 230.5 %all-gather.23.cloned.1.call-start = ((), (), s32[]{:S(2)}) async-start(), calls=%async_computation.13 | async-start | bytes 2359296 | tf_op jit(solution)/shard_map/all_gather | solution.py:56
  477.0 311.6 %all-gather.37.cloned.1.call-start = ((), (), s32[]{:S(2)}) async-start(), calls=%async_computation.30 | async-start | bytes 6684672 | tf_op jit(solution)/shard_map/all_gather | solution.py:315
  477.8 343.5 %reduce-scatter.16.cloned.1.call-start = ((), (), s32[]{:S(2)}) async-start(), calls=%async_computation.16 | async-start | bytes 4718592 | tf_op jit(solution)/shard_map/reduce_scatter | solution.py:60
  839.7 504.4 %reduce-scatter.18.cloned.1.call-start = ((), (), s32[]{:S(2)}) async-start(), calls=%async_computation.18 | async-start | bytes 4718592 | tf_op jit(solution)/shard_map/reduce_scatter | solution.py:60
  1044.3 152.3 %collective-permute-start.24 = (f32[512,4,96]{0,2,1:T(8,128)S(1)}, f32[512,4,96]{0,2,1:T(8,128)S(1)}, u32[]{:S(2)}, u32[]{:S(2)}) collective-permute-start(f32[512,4,96]{0,2,1:T(8,128)S(1)} %copy-done.81), channel_id=1, source_target_pairs={{8,0},{10,2},{12,4},{14,6},{16,8},{18,10},{20,12},{22,14},{24,16},... | collective-permute-start | bytes 2359304 | tf_op jit(solution)/shard_map/ppermute | solution.py:19
  1047.2 149.5 %collective-permute-start.25 = (f32[512,4,96]{0,2,1:T(8,128)S(1)}, f32[512,4,96]{0,2,1:T(8,128)S(1)}, u32[]{:S(2)}, u32[]{:S(2)}) collective-permute-start(f32[512,4,96]{0,2,1:T(8,128)S(1)} %copy-done.80), channel_id=1, source_target_pairs={{10,0},{12,2},{14,4},{16,6},{18,8},{20,10},{22,12},{24,14},{26,16}... | collective-permute-start | bytes 2359304 | tf_op jit(solution)/shard_map/ppermute | solution.py:19
  1056.5 178.8 %collective-permute-start.26 = (f32[512,4,96]{0,2,1:T(8,128)S(1)}, f32[512,4,96]{0,2,1:T(8,128)S(1)}, u32[]{:S(2)}, u32[]{:S(2)}) collective-permute-start(f32[512,4,96]{0,2,1:T(8,128)S(1)} %copy-done.79), channel_id=1, source_target_pairs={{12,0},{14,2},{16,4},{18,6},{20,8},{22,10},{24,12},{26,14},{28,16}... | collective-permute-start | bytes 2359304 | tf_op jit(solution)/shard_map/ppermute | solution.py:19
  1065.2 170.2 %collective-permute-start.27 = (f32[512,4,96]{0,2,1:T(8,128)S(1)}, f32[512,4,96]{0,2,1:T(8,128)S(1)}, u32[]{:S(2)}, u32[]{:S(2)}) collective-permute-start(f32[512,4,96]{0,2,1:T(8,128)S(1)} %copy-done.78), channel_id=1, source_target_pairs={{14,0},{16,2},{18,4},{20,6},{22,8},{24,10},{26,12},{28,14},{30,16}... | collective-permute-start | bytes 2359304 | tf_op jit(solution)/shard_map/ppermute | solution.py:19
  1240.7 235.9 %reduce-scatter.24.cloned.1.call-start = ((), (), s32[]{:S(2)}) async-start(), calls=%async_computation.21 | async-start | bytes 2506752 | tf_op jit(solution)/shard_map/reduce_scatter | solution.py:360
  1243.2 366.1 %reduce-scatter.22.cloned.1.call-start = ((), (), s32[]{:S(2)}) async-start(), calls=%async_computation.20 | async-start | bytes 2506752 | tf_op jit(solution)/shard_map/reduce_scatter | solution.py:359
  1245.8 505.1 %reduce-scatter.20.cloned.1.call-start = ((), (), s32[]{:S(2)}) async-start(), calls=%async_computation.19 | async-start | bytes 5013504 | tf_op jit(solution)/shard_map/reduce_scatter | solution.py:358
  1249.7 644.0 %reduce-scatter.26.cloned.1.call-start = ((), (), s32[]{:S(2)}) async-start(), calls=%async_computation.22 | async-start | bytes 5013504 | tf_op jit(solution)/shard_map/reduce_scatter | solution.py:361
  1255.0 849.4 %reduce-scatter.28.cloned.1.call-start = ((), (), s32[]{:S(2)}) async-start(), calls=%async_computation.23 | async-start | bytes 13369344 | tf_op jit(solution)/shard_map/reduce_scatter | solution.py:343
  1264.4 1050.9 %reduce-scatter.30.cloned.1.call-start = ((), (), s32[]{:S(2)}) async-start(), calls=%async_computation.24 | async-start | bytes 13369344 | tf_op jit(solution)/shard_map/reduce_scatter | solution.py:344
  1272.5 1252.4 %reduce-scatter.32.cloned.1.call-start = ((), (), s32[]{:S(2)}) async-start(), calls=%async_computation.25 | async-start | bytes 13369344 | tf_op jit(solution)/shard_map/reduce_scatter | solution.py:345
  (136 other events, 5493.9 us)
Sparse Core Ops, SparseCore 0:
  52.0 13.3 all-gather.20
  68.2 55.4 all-gather.28
  126.4 64.9 all-gather.30
  194.1 62.5 all-gather.32
  259.3 71.2 all-gather.34
  458.6 15.5 reduce-scatter.11
  476.4 10.9 all-gather.24
  490.6 93.7 all-gather.40
  587.5 92.4 all-gather.38
  682.0 9.6 all-gather.22
  694.8 93.7 all-gather.36
  810.5 10.7 reduce-scatter.15
  823.5 12.0 reduce-scatter.13
  839.8 10.9 all-gather.26
  1240.8 103.1 reduce-scatter.17
  1349.4 127.1 reduce-scatter.23
  1482.7 126.5 reduce-scatter.21
  1614.9 135.9 reduce-scatter.19
  1757.5 136.1 reduce-scatter.25
  1899.8 204.5 reduce-scatter.27
  2111.6 203.6 reduce-scatter.29
  2321.4 203.4 reduce-scatter.31
where the time goes:
time: 2540 us; the launch traced here: 2530 us
  waiting for transfers between devices  1890 us (74%)
  matrix products  288 us (11%)
  blocking collectives  147 us (6%)
  starting transfers between devices  121 us (5%)
  other arithmetic  57.1 us (2%)
    ppermute x28, waiting for transfers between devices, passed_along(): lax.ppermute(value, axis, [(source, source + steps) for source in range(l...  255 us
    reduce_scatter x1, waiting for transfers between devices, body(): lax.psum_scatter(mlp_parts[2], 'fsdp', scatter_dimension=0, tiled=True)  211 us
    reduce_scatter x1, waiting for transfers between devices, body(): lax.psum_scatter(mlp_parts[1], 'fsdp', scatter_dimension=0, tiled=True)  211 us
    reduce_scatter x1, waiting for transfers between devices, body(): lax.psum_scatter(mlp_parts[3], 'fsdp', scatter_dimension=0, tiled=True)  210 us
    reduce_scatter x1, waiting for transfers between devices, body(): lax.psum_scatter(attn_parts[4], 'fsdp', scatter_dimension=0, tiled=True)  143 us
    reduce_scatter x1, waiting for transfers between devices, body(): lax.psum_scatter(attn_parts[1], 'fsdp', scatter_dimension=0, tiled=True)  142 us
    reduce_scatter x1, waiting for transfers between devices, body(): lax.psum_scatter(attn_parts[2], 'fsdp', scatter_dimension=0, tiled=True)  133 us
    unnamed x2, blocking collectives  129 us
  transfers between devices with their start and end apart: 50, of which 37 were waited for; matrix products, arithmetic and copies ran while one was open for 9% of the time, Pallas kernels for 0%

commit v1 on v0

v1 whole, which is shorter than its diff:
```python
import functools
import math

import jax
import jax.numpy as jnp
from jax import lax
from jax.experimental import pallas as pl
from jax.experimental.pallas import tpu as pltpu
from jax.sharding import PartitionSpec as P

HEAD_SIZE = 96
HALF = HEAD_SIZE // 2
SPANS = 8
PLANE = 4
PACKED_LENGTH = 4096
SPAN = PACKED_LENGTH // SPANS

rope_base = 100000.0
norm_eps = 1e-05
masked_score = -1000000000.0
scale = HEAD_SIZE ** (-0.5)
scale_log2 = scale * math.log2(math.e)
bf16 = jnp.bfloat16
f32 = jnp.float32


def dot(left, right, left_dim=1, right_dim=0):
    return lax.dot_general(
        left, right, (((left_dim,), (right_dim,)), ((), ())), preferred_element_type=f32
    )


def hop(value, distance):
    count = lax.axis_size("fsdp")
    return lax.ppermute(value, "fsdp", [(i, i ^ distance) for i in range(count)])


def swap(value):
    return lax.ppermute(value, "tp", [(0, 1), (1, 0)])


def groups_of(size):
    count = lax.axis_size("fsdp")
    return [list(range(first, first + size)) for first in range(0, count, size)]


def exchange(value, size):
    groups = None if size == lax.axis_size("fsdp") else groups_of(size)
    return lax.all_to_all(value, "fsdp", 0, 0, axis_index_groups=groups)


def project_kernel(place_ref, hidden_ref, gain_ref, weight_ref, cos_ref, sin_ref,
                   normed_ref, q_t_ref, k_t_ref, v_t_ref, q_ref, k_ref, v_ref):
    x = hidden_ref[0].astype(f32)
    factor = lax.rsqrt(jnp.mean(x * x, axis=-1, keepdims=True) + norm_eps)
    normed = (x * factor * gain_ref[...]).astype(bf16)
    normed_ref[0] = normed
    product = dot(normed, weight_ref[...]).T
    cosine, sine = cos_ref[...], sin_ref[...]
    for number, (t_ref, n_ref) in enumerate(((q_t_ref, q_ref), (k_t_ref, k_ref))):
        first = product[number * HEAD_SIZE:number * HEAD_SIZE + HALF]
        second = product[number * HEAD_SIZE + HALF:(number + 1) * HEAD_SIZE]
        turned = jnp.concatenate(
            [first * cosine - second * sine, second * cosine + first * sine], axis=0
        )
        t_ref[...] = turned.astype(bf16)
        n_ref[...] = turned.T.astype(bf16)
    value = product[2 * HEAD_SIZE:3 * HEAD_SIZE]
    v_t_ref[...] = value.astype(bf16)
    v_ref[...] = value.T.astype(bf16)


def project(pieces, gain, weight, places, cosine, sine):
    count, rows, width = pieces.shape
    tokens = count * rows
    wide = pl.BlockSpec((HEAD_SIZE, rows), lambda i, p: (0, p[i]))
    tall = pl.BlockSpec((rows, HEAD_SIZE), lambda i, p: (p[i], 0))
    table = pl.BlockSpec((HALF, rows), lambda i, p: (0, p[i]))
    return pl.pallas_call(
        project_kernel,
        grid_spec=pltpu.PrefetchScalarGridSpec(
            num_scalar_prefetch=1,
            grid=(count,),
            in_specs=[
                pl.BlockSpec((1, rows, width), lambda i, p: (i, 0, 0)),
                pl.BlockSpec((1, width), lambda i, p: (0, 0)),
                pl.BlockSpec(weight.shape, lambda i, p: (0, 0)),
                table,
                table,
            ],
            out_specs=[pl.BlockSpec((1, rows, width), lambda i, p: (i, 0, 0))]
            + [wide] * 3 + [tall] * 3,
        ),
        out_shape=[jax.ShapeDtypeStruct(pieces.shape, bf16)]
        + [jax.ShapeDtypeStruct((HEAD_SIZE, tokens), bf16)] * 3
        + [jax.ShapeDtypeStruct((tokens, HEAD_SIZE), bf16)] * 3,
        compiler_params=pltpu.CompilerParams(vmem_limit_bytes=32 * 2**20),
        cost_estimate=pl.CostEstimate(
            flops=2 * tokens * width * 3 * HEAD_SIZE,
            bytes_accessed=4 * tokens * width,
            transcendentals=0,
        ),
        name="project",
    )(places, pieces, gain, weight, cosine, sine)


def widened(column):
    return jnp.concatenate([column] * (SPAN // column.shape[1]), axis=1)


def causal_tile():
    key_at = lax.broadcasted_iota(jnp.int32, (SPAN, SPAN), 0)
    query_at = lax.broadcasted_iota(jnp.int32, (SPAN, SPAN), 1)
    return key_at <= query_at


def forward_kernel(q_t_ref, k_ref, v_t_ref, id_row_ref, id_col_ref, out_ref, out_full_ref, lse_ref):
    block = pl.program_id(0)
    query = q_t_ref[...]
    id_row = id_row_ref[...]

    def step(at, carry, diagonal):
        best, total, result = carry
        keys = pl.ds(pl.multiple_of(at * SPAN, SPAN), SPAN)
        scores = dot(k_ref[keys, :], query) * scale_log2
        allowed = widened(id_col_ref[keys, :]) == id_row
        if diagonal:
            allowed = allowed & causal_tile()
        scores = jnp.where(allowed, scores, masked_score)
        larger = jnp.maximum(best, jnp.max(scores, axis=0, keepdims=True))
        weights = jnp.exp2(scores - larger)
        faded = jnp.exp2(best - larger)
        total = total * faded + jnp.sum(weights, axis=0, keepdims=True)
        result = result * faded + dot(v_t_ref[:, keys], weights.astype(bf16))
        return larger, total, result

    carry = (
        jnp.full((1, SPAN), masked_score, f32),
        jnp.zeros((1, SPAN), f32),
        jnp.zeros((HEAD_SIZE, SPAN), f32),
    )
    carry = lax.fori_loop(0, block, lambda at, c: step(at, c, False), carry)
    best, total, result = step(block, carry, True)
    result = result / total
    out_full_ref[...] = result
    out_ref[0] = result.astype(bf16)
    lse_ref[...] = best + jnp.log2(total)


def attention_forward(q_t, k, v_t, id_row, id_col):
    tokens = k.shape[0]
    whole = lambda array: pl.BlockSpec(array.shape, lambda i: (0, 0))
    return pl.pallas_call(
        forward_kernel,
        grid=(SPANS,),
        in_specs=[
            pl.BlockSpec((HEAD_SIZE, SPAN), lambda i: (0, i)),
            whole(k),
            whole(v_t),
            pl.BlockSpec((1, SPAN), lambda i: (0, i)),
            whole(id_col),
        ],
        out_specs=[
            pl.BlockSpec((1, HEAD_SIZE, SPAN), lambda i: (i, 0, 0)),
            pl.BlockSpec((HEAD_SIZE, SPAN), lambda i: (0, i)),
            pl.BlockSpec((1, SPAN), lambda i: (0, i)),
        ],
        out_shape=[
            jax.ShapeDtypeStruct((SPANS, HEAD_SIZE, SPAN), bf16),
            jax.ShapeDtypeStruct((HEAD_SIZE, tokens), f32),
            jax.ShapeDtypeStruct((1, tokens), f32),
        ],
        compiler_params=pltpu.CompilerParams(vmem_limit_bytes=40 * 2**20),
        cost_estimate=pl.CostEstimate(
            flops=36 * SPAN * SPAN * 256 * 4 * 4, bytes_accessed=8 * 2**20, transcendentals=36 * SPAN * SPAN
        ),
        name="attention_forward",
    )(q_t, k, v_t, id_row, id_col)


def backward_kernel(q_t_ref, q_ref, k_t_ref, k_ref, v_ref, dout_ref, out_ref, lse_ref, id_row_ref, id_col_ref,
                    cos_ref, sin_ref, grad_ref, delta_ref, dout_n_ref, dq_ref):
    block = pl.program_id(0)

    @pl.when(block == 0)
    def _():
        for at in range(SPANS):
            dout = dout_ref[at]
            here = slice(at * SPAN, (at + 1) * SPAN)
            delta_ref[:, here] = jnp.sum(dout.astype(f32) * out_ref[:, here], axis=0, keepdims=True)
            dout_n_ref[here, :] = dout.astype(f32).T.astype(bf16)
        dq_ref[...] = jnp.zeros(dq_ref.shape, f32)

    key_t, key, value = k_t_ref[...], k_ref[...], v_ref[...]
    id_col = widened(id_col_ref[...])

    def step(at, carry, diagonal):
        dkey, dvalue = carry
        rows = pl.ds(pl.multiple_of(at * SPAN, SPAN), SPAN)
        scores = dot(key, q_t_ref[:, rows]) * scale_log2 - lse_ref[:, rows]
        allowed = id_col == id_row_ref[:, rows]
        if diagonal:
            allowed = allowed & causal_tile()
        probs = jnp.exp2(jnp.where(allowed, scores, masked_score))
        dprobs = dot(value, dout_ref[at])
        dscores = (probs * (dprobs - delta_ref[:, rows])).astype(bf16)
        dvalue = dvalue + dot(probs.astype(bf16), dout_n_ref[rows, :])
        dkey = dkey + dot(dscores, q_ref[rows, :])
        dq_ref[at] += dot(key_t, dscores)
        return dkey, dvalue

    zero = jnp.zeros((SPAN, HEAD_SIZE), f32)
    carry = step(block, (zero, zero), True)
    dkey, dvalue = lax.fori_loop(block + 1, SPANS, lambda at, c: step(at, c, False), carry)
    cosine, sine = cos_ref[...], sin_ref[...]
    for number, grad in enumerate((dq_ref[block], dkey.T)):
        first = grad[:HALF] * scale
        second = grad[HALF:] * scale
        turned = jnp.concatenate(
            [first * cosine + second * sine, second * cosine - first * sine], axis=0
        )
        grad_ref[0, number * HEAD_SIZE:(number + 1) * HEAD_SIZE, :] = turned.astype(bf16)
    grad_ref[0, 2 * HEAD_SIZE:, :] = dvalue.T.astype(bf16)


def attention_backward(q_t, q, k_t, k, v, dout, out, lse, id_row, id_col, cosine, sine):
    tokens = k.shape[0]
    whole = lambda array: pl.BlockSpec(array.shape, lambda i: (0,) * array.ndim)
    wide = pl.BlockSpec((HEAD_SIZE, SPAN), lambda i: (0, i))
    tall = pl.BlockSpec((SPAN, HEAD_SIZE), lambda i: (i, 0))
    table = pl.BlockSpec((HALF, SPAN), lambda i: (0, i))
    return pl.pallas_call(
        backward_kernel,
        grid=(SPANS,),
        in_specs=[
            whole(q_t), whole(q), wide, tall, tall, whole(dout), whole(out), whole(lse), whole(id_row),
            pl.BlockSpec((SPAN, id_col.shape[1]), lambda i: (i, 0)), table, table,
        ],
        out_specs=pl.BlockSpec((1, 3 * HEAD_SIZE, SPAN), lambda i: (i, 0, 0)),
        out_shape=jax.ShapeDtypeStruct((SPANS, 3 * HEAD_SIZE, SPAN), bf16),
        scratch_shapes=[
            pltpu.VMEM((1, tokens), f32),
            pltpu.VMEM((tokens, HEAD_SIZE), bf16),
            pltpu.VMEM((SPANS, HEAD_SIZE, SPAN), f32),
        ],
        compiler_params=pltpu.CompilerParams(vmem_limit_bytes=48 * 2**20),
        cost_estimate=pl.CostEstimate(
            flops=36 * SPAN * SPAN * 256 * 10 * 4, bytes_accessed=12 * 2**20, transcendentals=36 * SPAN * SPAN
        ),
        name="attention_backward",
    )(q_t, q, k_t, k, v, dout, out, lse, id_row, id_col, cosine, sine)


def head_grad_kernel(place_ref, normed_ref, grad_ref, out_ref, sum_ref):
    at = pl.program_id(0)
    product = dot(grad_ref[0], normed_ref[0])

    @pl.when(at == 0)
    def _():
        sum_ref[...] = product

    @pl.when(at > 0)
    def _():
        sum_ref[...] += product

    @pl.when(at == pl.num_programs(0) - 1)
    def _():
        out_ref[...] = sum_ref[...].T.astype(bf16)


def head_grads(normed, grads, places):
    count, rows, width = normed.shape
    return pl.pallas_call(
        head_grad_kernel,
        grid_spec=pltpu.PrefetchScalarGridSpec(
            num_scalar_prefetch=1,
            grid=(count,),
            in_specs=[
                pl.BlockSpec((1, rows, width), lambda i, p: (i, 0, 0)),
                pl.BlockSpec((1, 3 * HEAD_SIZE, rows), lambda i, p: (p[i] // 2, 0, p[i] % 2)),
            ],
            out_specs=pl.BlockSpec((width, 3 * HEAD_SIZE), lambda i, p: (0, 0)),
            scratch_shapes=[pltpu.VMEM((3 * HEAD_SIZE, width), f32)],
        ),
        out_shape=jax.ShapeDtypeStruct((width, 3 * HEAD_SIZE), bf16),
        compiler_params=pltpu.CompilerParams(vmem_limit_bytes=32 * 2**20),
        cost_estimate=pl.CostEstimate(
            flops=2 * count * rows * width * 3 * HEAD_SIZE, bytes_accessed=2 * count * rows * width, transcendentals=0
        ),
        name="head_grads",
    )(places, normed, grads)


def gather_block(own):
    rows = own.shape[0]
    cut_a, cut_b = rows // 128 * 48, rows // 128 * 88
    p1, p2, p4 = hop(own, 1), hop(own, 2), hop(own, 4)
    p3, p6, p5 = hop(p2, 1), hop(p4, 2), hop(p1, 4)
    p7 = jnp.concatenate([hop(p6[:cut_a], 1), hop(p5[cut_a:cut_b], 2), hop(p3[cut_b:], 4)], axis=0)
    pieces = []
    for piece in (own, p1, p2, p3, p4, p5, p6, p7):
        pieces += [piece, swap(piece)]
    return jnp.stack(pieces)


def gather_plane(own):
    pieces = []
    for piece in [own] + [hop(own, k) for k in range(1, PLANE)]:
        pieces += [piece, swap(piece)]
    return jnp.concatenate(pieces, axis=0)


def scatter_plane(parts, rows):
    table = parts.reshape(PLANE, 2, rows, -1)
    pair = table[:, 0] + swap(table[:, 1].astype(bf16)).astype(f32)
    low = pair.astype(bf16)
    total = pair[0]
    for k in range(1, PLANE):
        total = total + hop(low[k], k).astype(f32)
    return total


def reorder(rows, plane_at, planes):
    width = rows.shape[1] // planes
    return jnp.concatenate(
        [lax.dynamic_slice_in_dim(rows, (plane_at ^ k) * width, width, 1) for k in range(planes)], axis=1
    )


def rms_factor(stream):
    return lax.rsqrt(jnp.mean(stream * stream, axis=-1, keepdims=True) + norm_eps)


def norm_backward(stream, factor, gain, dnormed):
    scaled = dnormed * gain
    return factor * scaled - stream * factor**3 * jnp.mean(scaled * stream, axis=-1, keepdims=True)


def body(
    hidden,
    document_index,
    attn_gain,
    q_weight,
    key_matrix,
    value_matrix,
    out_weight,
    mlp_gain,
    gate_weight,
    up_weight,
    down_weight,
    cotangent,
):
    count = lax.axis_size("fsdp")
    planes = count // PLANE
    f = lax.axis_index("fsdp")
    t = lax.axis_index("tp")
    place = f % SPANS
    plane_at = f // PLANE
    own, width = hidden.shape
    shard = q_weight.shape[1]
    q_heads = q_weight.shape[2] // HEAD_SIZE
    kv_heads = key_matrix.shape[2] // HEAD_SIZE
    per_kv = q_heads // kv_heads
    units = gate_weight.shape[2] // PLANE

    def by_head(weight, heads, copies):
        cut = weight[0].reshape(shard, heads, HEAD_SIZE).transpose(1, 0, 2)
        return jnp.repeat(cut, copies, axis=0)

    gains_own = jnp.stack([attn_gain[0], mlp_gain[0]], axis=-1)
    sent = jnp.concatenate(
        [
            by_head(q_weight, q_heads, 1),
            by_head(key_matrix, kv_heads, per_kv),
            by_head(value_matrix, kv_heads, per_kv),
            jnp.broadcast_to(gains_own[None], (SPANS, shard, 2)),
        ],
        axis=-1,
    )
    sent = jnp.tile(sent, (count // SPANS, 1, 1))
    head_set = exchange(sent, count).reshape(width, -1)
    head_weight = head_set[:, :3 * HEAD_SIZE]
    gains = head_set[:, 3 * HEAD_SIZE:].T.astype(f32)
    gain_a, gain_m = gains[0:1], gains[1:2]

    pieces = gather_block(hidden)

    unit_set = jnp.concatenate(
        [w[0].reshape(shard, PLANE, units).transpose(1, 0, 2) for w in (gate_weight, up_weight, down_weight)],
        axis=-1,
    )
    unit_own = exchange(unit_set, PLANE).reshape(PLANE * shard, 3 * units)
    unit_weight = jnp.concatenate(
        [unit_own] + [hop(unit_own, PLANE * k) for k in range(1, planes)], axis=0
    )
    out_part = lax.all_gather(out_weight[0], "fsdp", axis=0, tiled=True)
    in_part = lax.all_gather(
        jnp.concatenate([q_weight[0], key_matrix[0], value_matrix[0]], axis=1), "fsdp", axis=0, tiled=True
    )

    seq_ids = lax.dynamic_slice_in_dim(document_index, f // SPANS * PACKED_LENGTH, PACKED_LENGTH)
    seq_index = jnp.arange(PACKED_LENGTH, dtype=jnp.int32)
    before = jnp.concatenate([jnp.full((1,), -1, jnp.int32), seq_ids[:-1]])
    starts = lax.cummax(jnp.where(seq_ids != before, seq_index, 0), axis=0)
    positions = (seq_index - starts).astype(f32)
    freq = rope_base ** (-2.0 * jnp.arange(HALF, dtype=f32) / HEAD_SIZE)
    angle = freq[:, None] * positions[None, :]
    cosine, sine = jnp.cos(angle), jnp.sin(angle)
    id_row = seq_ids[None, :]
    id_col = jnp.broadcast_to(seq_ids[:, None], (PACKED_LENGTH, 128))
    own_ids = lax.dynamic_slice_in_dim(seq_ids, place * SPAN + t * own, own)
    places = jnp.stack([(place ^ k) * 2 + (t ^ c) for k in range(SPANS) for c in range(2)]).astype(jnp.int32)

    dstream = cotangent.astype(f32) * (own_ids != 0).astype(f32)[:, None]
    dmlp = gather_plane(reorder(dstream.astype(bf16), plane_at, planes))

    normed, q_t, k_t, v_t, q, k, v = project(pieces, gain_a, head_weight, places, cosine, sine)
    out_t, out_full, lse = attention_forward(q_t, k, v_t, id_row, id_col)
    attended = exchange(out_t, SPANS).reshape(q_heads * HEAD_SIZE, SPAN)

    stream = hidden.astype(f32)
    mine = lax.dynamic_slice_in_dim(attended, t * own, own, 1)
    other = lax.dynamic_slice_in_dim(attended, (1 - t) * own, own, 1)
    mid = stream + dot(mine, out_part, 0, 1) + swap(dot(other, out_part, 0, 1))

    factor_m = rms_factor(mid)
    normed_m = gather_plane(reorder((mid * factor_m * gain_m).astype(bf16), plane_at, planes))
    gate = dot(normed_m, unit_weight[:, :units])
    up = dot(normed_m, unit_weight[:, units:2 * units])
    dact = dot(dmlp, unit_weight[:, 2 * units:])
    sigma = 1.0 / (1.0 + jnp.exp(-gate))
    act = (gate * sigma * up).astype(bf16)
    dgate = (dact * up * sigma * (1.0 + gate * (1.0 - sigma))).astype(bf16)
    dup = (dact * gate * sigma).astype(bf16)
    dgate_up = jnp.concatenate([dgate, dup], axis=1)
    dnormed_m = reorder(
        scatter_plane(dot(dgate_up, unit_weight[:, :2 * units], 1, 1), own), plane_at, planes
    )
    dmid = dstream + norm_backward(mid, factor_m, gain_m, dnormed_m)

    dattn = dmid.astype(bf16)
    dattn_other = swap(dattn)
    dattn = jnp.where(
        t == 0,
        jnp.concatenate([dattn, dattn_other], axis=0),
        jnp.concatenate([dattn_other, dattn], axis=0),
    )
    dout = exchange(
        dot(out_part, dattn, 0, 1).astype(bf16).reshape(SPANS, HEAD_SIZE, SPAN), SPANS
    )
    out_grad = lax.psum_scatter(
        dot(dattn, attended, 0, 1).astype(bf16), "fsdp", scatter_dimension=0, tiled=True
    ).astype(f32)
    grads = attention_backward(q_t, q, k_t, k, v, dout, out_full, lse, id_row, id_col, cosine, sine)

    back = exchange(grads, SPANS)
    dq = back[:, :HEAD_SIZE].reshape(q_heads * HEAD_SIZE, SPAN)
    dkv = back[:, HEAD_SIZE:].reshape(kv_heads, per_kv, 2, HEAD_SIZE, SPAN).astype(f32).sum(axis=1)
    dkv = dkv.astype(bf16).transpose(1, 0, 2, 3).reshape(2 * kv_heads * HEAD_SIZE, SPAN)
    din = jnp.concatenate([dq, dkv], axis=0)
    mine = lax.dynamic_slice_in_dim(din, t * own, own, 1)
    other = lax.dynamic_slice_in_dim(din, (1 - t) * own, own, 1)
    dnormed_a = dot(mine, in_part, 0, 1) + swap(dot(other, in_part, 0, 1))
    input_grad = dmid + norm_backward(stream, rms_factor(stream), gain_a, dnormed_a)

    head_sums = exchange(head_grads(normed, grads, places).reshape(count, shard, 3 * HEAD_SIZE), count)
    head_sums = head_sums.reshape(count // SPANS, SPANS, shard, 3 * HEAD_SIZE).astype(f32).sum(axis=0)
    q_grad = head_sums[..., :HEAD_SIZE].transpose(1, 0, 2).reshape(shard, -1)
    kv_sums = head_sums.reshape(kv_heads, per_kv, shard, 3 * HEAD_SIZE).sum(axis=1)
    k_grad = kv_sums[..., HEAD_SIZE:2 * HEAD_SIZE].transpose(1, 0, 2).reshape(shard, -1)
    v_grad = kv_sums[..., 2 * HEAD_SIZE:].transpose(1, 0, 2).reshape(shard, -1)

    output = (
        mid + reorder(scatter_plane(dot(act, unit_weight[:, 2 * units:], 1, 1), own), plane_at, planes)
    ).astype(bf16)
    unit_grad = jnp.concatenate([dot(normed_m, dgate_up, 0, 0), dot(dmlp, act, 0, 0)], axis=1)
    unit_grad = unit_grad.reshape(planes, PLANE * shard, 3 * units)
    low = unit_grad.astype(bf16)
    unit_sum = unit_grad[0]
    for step in range(1, planes):
        unit_sum = unit_sum + hop(low[step], PLANE * step).astype(f32)
    unit_back = exchange(unit_sum.astype(bf16).reshape(PLANE, shard, 3 * units), PLANE)
    unit_back = unit_back.transpose(1, 0, 2).astype(f32)
    gate_grad, up_grad, down_grad = (
        unit_back[..., part * units:(part + 1) * units].reshape(shard, -1) for part in range(3)
    )

    def row_products(pairs):
        return sum(jnp.sum(grad * weight[0].astype(f32), axis=1) for grad, weight in pairs)

    gain_parts = jnp.stack([
        row_products([(q_grad, q_weight), (k_grad, key_matrix), (v_grad, value_matrix)]),
        row_products([(gate_grad, gate_weight), (up_grad, up_weight)]),
    ])
    gain_grads = (gain_parts + swap(gain_parts)) / jnp.stack([attn_gain[0], mlp_gain[0]]).astype(f32)
    return (
        output,
        input_grad,
        gain_grads[0:1],
        q_grad[None],
        k_grad[None],
        v_grad[None],
        out_grad[None],
        gain_grads[1:2],
        gate_grad[None],
        up_grad[None],
        down_grad[None],
    )


def solution(mesh):
    rows = P(("fsdp", "tp"), None)
    gain = P(None, "fsdp")
    weight = P(None, "fsdp", "tp")
    return jax.shard_map(
        body,
        mesh=mesh,
        in_specs=(rows, P(), gain, weight, weight, weight, weight, gain, weight, weight, weight, rows),
        out_specs=(rows, rows, gain, weight, weight, weight, weight, gain, weight, weight, weight),
        check_vma=False,
    )
```

time: 2540 us -> 935 us (0.37)
  waiting for transfers between devices: 1890 us -> 471 us
  matrix products: 288 us -> 79.3 us
  blocking collectives: 147 us -> 33.3 us
  Pallas kernels: 0 us -> 92.4 us
  local copies, waits for them, and re-layouts: 13.5 us -> 101 us
  starting transfers between devices: 121 us -> 80 us
    reduce_scatter x11 -> x1, waiting for transfers between devices: 1150 us -> 96.4 us  [body(): lax.psum_scatter(dot(dattn, attended, 0, 1).astype(bf16), 'fsdp', scatter...]
    all_gather x11 -> x2, waiting for transfers between devices: 474 us -> 0.02 us  [the longest x1 0.02 us: body(): lax.all_gather(jnp.concatenate([q_weight[0], key_matrix[0], value_matrix[...]
    dot_general x69 -> x13, matrix products: 288 us -> 79.3 us  [dot(): lax.dot_general(left, right, (((left_dim,), (right_dim,)), ((), ())), pre...]
    unnamed x2 -> x0, blocking collectives: 129 us -> none
    pallas_call x0 -> x4, Pallas kernels: none -> 92.4 us  [the longest x1 36.3 us: attention_backward(): pl.pallas_call(backward_kernel, grid=(SPANS,), in_specs=[whole(q_t), whol...]
    ppermute x28 -> x49, waiting for transfers between devices: 255 us -> 336 us  [the longest x27 335 us: hop(): lax.ppermute(value, 'fsdp', [(i, i ^ distance) for i in range(count)])]
    ppermute x28 -> x49, starting transfers between devices: 120 us -> 55.5 us  [the longest x22 28.7 us: swap(): return lax.ppermute(value, 'tp', [(0, 1), (1, 0)])]
    unnamed x225 -> x149, local copies, waits for them, and re-layouts: 12 us -> 56.6 us
  transfers between devices with their start and end apart: 50 -> 58, of which waited for: 37 -> 21; matrix products, arithmetic and copies ran while one was open for 9% -> 18% of each run, Pallas kernels for 0% -> 10%
where the time goes in v1:
time: 935 us; the launch traced here: 922 us
  waiting for transfers between devices  471 us (50%)
  local copies, waits for them, and re-layouts  101 us (11%)
  Pallas kernels  92.4 us (10%)
  starting transfers between devices  80 us (9%)
  matrix products  79.3 us (8%)
  other arithmetic  50.2 us (5%)
  blocking collectives  33.3 us (4%)
  between operations  15.3 us (2%)
    ppermute x27, waiting for transfers between devices, hop(): lax.ppermute(value, 'fsdp', [(i, i ^ distance) for i in range(count)])  335 us
    reduce_scatter x1, waiting for transfers between devices, body(): lax.psum_scatter(dot(dattn, attended, 0, 1).astype(bf16), 'fsdp', scatter...  96.4 us
    dot_general x13, matrix products, dot(): lax.dot_general(left, right, (((left_dim,), (right_dim,)), ((), ())), pre...  79.3 us
    unnamed x149, local copies, waits for them, and re-layouts  56.6 us
    all_to_all x6, waiting for transfers between devices, exchange(): return lax.all_to_all(value, 'fsdp', 0, 0, axis_index_groups=groups)  38.2 us
    pallas_call x1, Pallas kernels, attention_backward(): pl.pallas_call(backward_kernel, grid=(SPANS,), in_specs=[whole(q_t), whol...  36.3 us
    all_to_all x1, blocking collectives, exchange(): return lax.all_to_all(value, 'fsdp', 0, 0, axis_index_groups=groups)  33.3 us
    ppermute x22, starting transfers between devices, swap(): return lax.ppermute(value, 'tp', [(0, 1), (1, 0)])  28.7 us
  transfers between devices with their start and end apart: 58, of which 21 were waited for; matrix products, arithmetic and copies ran while one was open for 18% of the time, Pallas kernels for 10%

profile of v1, /device:TPU:1, one launch (start us, length us, event | category | flops | bytes accessed | tf_op | source)
XLA Modules:
  0.0 922.5 jit_solution(3253292362522505460)
XLA Ops:
  45.0 30.9 %collective-permute-done.9 = bf16[256,1536]{1,0:T(8,128)(2,1)S(1)} collective-permute-done((bf16[256,1536]{1,0:T(8,128)(2,1)}, bf16[256,1536]{1,0:T(8,128)(2,1)S(1)}, u32[]{:S(2)}, u32[]{:S(2)}) %collective-permute-start.9) | collective-permute-done | bytes 786464 | tf_op jit(solution)/shard_map/ppermute | solution.py:35
  108.5 18.9 %project.1 = (bf16[16,256,1536]{2,1,0:T(8,128)(2,1)S(1)}, bf16[96,4096]{1,0:T(8,128)(2,1)S(1)}, bf16[96,4096]{1,0:T(8,128)(2,1)S(1)}, bf16[96,4096]{1,0:T(8,128)...) custom-call(s32[16]{0:T(128)S(1)} %stack.129.place_ref, ...), custom_call_target="tpu_custom_call" | custom-call | flops 3623878656 | bytes 25165824 | tf_op jit(solution)/shard_map/project/pallas_call | solution.py:79
  134.4 23.5 %attention_forward.1 = (bf16[8,96,512]{2,1,0:T(8,128)(2,1)}, f32[96,4096]{1,0:T(8,128)S(1)}, f32[1,4096]{1,0:T(1,128)S(1)}) custom-call(bf16[96,4096]{1,0:T(8,128)(2,1)S(1)} %get-tuple-element.21.q_t_ref, bf16[4096,96]{1,0:T(8,128)(2,1)S(1)} %get-tuple-element.22.k_ref, bf16[96,4096]{1,0:T(8,128)(2,1)S(1)} %get-tuple-element.23.v_t_ref, ...), custom_call_target="tpu_custom_call" | custom-call | flops 38654705664 | bytes 8388608 | tf_op jit(solution)/shard_map/attention_forward/pallas_call | solution.py:153
  163.0 11.3 %all-to-all-done.1 = bf16[8,96,512]{2,1,0:T(8,128)(2,1)S(1)} async-done(((bf16[8,96,512]{2,1,0:T(8,128)(2,1)}), bf16[8,96,512]{2,1,0:T(8,128)(2,1)S(1)}, u32[]{:S(2)}, u32[]{:S(2)}) %all-to-all-start.1) | async-done | bytes 786464 | tf_op jit(solution)/shard_map/all_to_all | solution.py:49
  190.7 14.0 %all-to-all-done.2 = bf16[4,96,1536]{2,1,0:T(8,128)(2,1)} async-done(((bf16[4,96,1536]{2,1,0:T(8,128)(2,1)}), bf16[4,96,1536]{2,1,0:T(8,128)(2,1)}, u32[]{:S(2)}, u32[]{:S(2)}) %all-to-all-start.2) | async-done | bytes 1179680 | tf_op jit(solution)/shard_map/all_to_all | solution.py:49
  217.7 17.9 %collective-permute-done.27 = bf16[384,1536]{1,0:T(8,128)(2,1)} collective-permute-done((bf16[384,1536]{1,0:T(8,128)(2,1)}, bf16[384,1536]{1,0:T(8,128)(2,1)}, u32[]{:S(2)}, u32[]{:S(2)}) %collective-permute-start.27) | collective-permute-done | bytes 1179680 | tf_op jit(solution)/shard_map/ppermute | solution.py:35
  238.0 72.5 %collective-permute-done.26 = bf16[384,1536]{1,0:T(8,128)(2,1)} collective-permute-done((bf16[384,1536]{1,0:T(8,128)(2,1)}, bf16[384,1536]{1,0:T(8,128)(2,1)}, u32[]{:S(2)}, u32[]{:S(2)}) %collective-permute-start.26) | collective-permute-done | bytes 1179680 | tf_op jit(solution)/shard_map/ppermute | solution.py:35
  320.0 8.5 collective-permute-done.19
  336.4 9.8 %collective-permute-done.37 = bf16[256,1536]{1,0:T(8,128)(2,1)S(1)} collective-permute-done((bf16[256,1536]{1,0:T(8,128)(2,1)}, bf16[256,1536]{1,0:T(8,128)(2,1)S(1)}, u32[]{:S(2)}, u32[]{:S(2)}) %collective-permute-start.37) | collective-permute-done | bytes 786464 | tf_op jit(solution)/shard_map/ppermute | solution.py:35
  350.4 20.9 %collective-permute-done.21 = bf16[256,1536]{1,0:T(8,128)(2,1)S(1)} collective-permute-done((bf16[256,1536]{1,0:T(8,128)(2,1)}, bf16[256,1536]{1,0:T(8,128)(2,1)S(1)}, u32[]{:S(2)}, u32[]{:S(2)}) %collective-permute-start.21) | collective-permute-done | bytes 786464 | tf_op jit(solution)/shard_map/ppermute | solution.py:35
  388.6 11.0 %multiply_convert_fusion.1 = (bf16[2048,512]{0,1:T(8,128)(2,1)S(1)}, bf16[2048,512]{0,1:T(8,128)(2,1)S(1)}, bf16[2048,512]{0,1:T(8,128)(2,1)}) fusion(f32[2048,512]{0,1:T(8,128)} %fusion.40, f32[2048,512]{0,1:T(8,128)} %fusion.31, bf16[2048,1536]{1,0:T(8,128)(2,1)} %copy-done.49, bf16[1536,1536]{1,0:T(8,128)(2,1)S(1)} %pad_maximum_fusion.1), kind=kOutput, calls=%fused_computation.13 | convolution fusion | flops 3238002688 | bytes 22544384 | tf_op jit(solution)/shard_map/dot_general | solution.py:28
  399.6 10.0 %fusion.5 = f32[2048,1536]{1,0:T(8,128)S(1)} fusion(bf16[1536,1536]{1,0:T(8,128)(2,1)S(1)} %pad_maximum_fusion.1, bf16[2048,512]{0,1:T(8,128)(2,1)} %get-tuple-element.49, bf16[2048,512]{0,1:T(8,128)(2,1)S(1)} %get-tuple-element.47), kind=kOutput, calls=%fused_computation.19 | convolution fusion | flops 6450839552 | bytes 19922944 | tf_op jit(solution)/shard_map/dot_general | solution.py:28
  429.1 12.2 %fusion.9 = f32[1536,1024]{0,1:T(8,128)} fusion(bf16[2048,1536]{1,0:T(8,128)(2,1)} %copy-done.49, bf16[2048,512]{0,1:T(8,128)(2,1)} %get-tuple-element.49, bf16[2048,512]{0,1:T(8,128)(2,1)S(1)} %copy-done.59), kind=kOutput, calls=%fused_computation.28 | convolution fusion | flops 6450839552 | bytes 16777216 | tf_op jit(solution)/shard_map/dot_general | solution.py:28
  467.1 16.6 %collective-permute-done.42 = bf16[256,1536]{1,0:T(8,128)(2,1)} collective-permute-done((bf16[256,1536]{1,0:T(8,128)(2,1)}, bf16[256,1536]{1,0:T(8,128)(2,1)}, u32[]{:S(2)}, u32[]{:S(2)}) %collective-permute-start.42) | collective-permute-done | bytes 786464 | tf_op jit(solution)/shard_map/ppermute | solution.py:35
  486.3 14.1 %collective-permute-done.29 = bf16[256,1536]{1,0:T(8,128)(2,1)S(1)} collective-permute-done((bf16[256,1536]{1,0:T(8,128)(2,1)S(1)}, bf16[256,1536]{1,0:T(8,128)(2,1)S(1)}, u32[]{:S(2)}, u32[]{:S(2)}) %collective-permute-start.29) | collective-permute-done | bytes 786464 | tf_op jit(solution)/shard_map/ppermute | solution.py:35
  500.4 16.9 %collective-permute-done.31 = bf16[256,1536]{1,0:T(8,128)(2,1)S(1)} collective-permute-done((bf16[256,1536]{1,0:T(8,128)(2,1)S(1)}, bf16[256,1536]{1,0:T(8,128)(2,1)S(1)}, u32[]{:S(2)}, u32[]{:S(2)}) %collective-permute-start.31) | collective-permute-done | bytes 786464 | tf_op jit(solution)/shard_map/ppermute | solution.py:35
  545.1 15.8 %collective-permute-done.45 = bf16[384,1536]{0,1:T(8,128)(2,1)} collective-permute-done((bf16[384,1536]{0,1:T(8,128)(2,1)}, bf16[384,1536]{0,1:T(8,128)(2,1)}, u32[]{:S(2)}, u32[]{:S(2)}) %collective-permute-start.45) | collective-permute-done | bytes 1179680 | tf_op jit(solution)/shard_map/ppermute | solution.py:35
  560.9 29.6 %collective-permute-done.47 = bf16[384,1536]{0,1:T(8,128)(2,1)} collective-permute-done((bf16[384,1536]{0,1:T(8,128)(2,1)}, bf16[384,1536]{0,1:T(8,128)(2,1)}, u32[]{:S(2)}, u32[]{:S(2)}) %collective-permute-start.47) | collective-permute-done | bytes 1179680 | tf_op jit(solution)/shard_map/ppermute | solution.py:35
  590.5 66.0 %collective-permute-done.46 = bf16[384,1536]{0,1:T(8,128)(2,1)} collective-permute-done((bf16[384,1536]{0,1:T(8,128)(2,1)}, bf16[384,1536]{0,1:T(8,128)(2,1)}, u32[]{:S(2)}, u32[]{:S(2)}) %collective-permute-start.46) | collective-permute-done | bytes 1179680 | tf_op jit(solution)/shard_map/ppermute | solution.py:35
  672.5 36.3 %attention_backward.1.grad_ref = bf16[8,288,512]{2,1,0:T(8,128)(2,1)} custom-call(bf16[96,4096]{1,0:T(8,128)(2,1)S(1)} %copy-done.9, bf16[4096,96]{1,0:T(8,128)(2,1)S(1)} %copy-done.4, bf16[96,4096]{1,0:T(8,128)(2,1)S(1)} %copy-done.11, bf16[4096,96]{1,0:T(8,128)(2,1)S(1)} %copy-done.6, bf16[4096,96]{1,0:T(8,128)(2,1)} %copy-done.7, ...), custom_call_target="tpu_custom_call" | custom-call | flops 96636764160 | bytes 12582912 | tf_op jit(solution)/shard_map/attention_backward/pallas_call | solution.py:232
  713.4 13.6 %head_grads.1 = bf16[1536,288]{1,0:T(8,128)(2,1)S(1)} custom-call(s32[16]{0:T(128)S(1)} %stack.129.place_ref, bf16[16,256,1536]{2,1,0:T(8,128)(2,1)S(1)} %copy-done.1, bf16[8,288,512]{2,1,0:T(8,128)(2,1)} %attention_backward.1.grad_ref), custom_call_target="tpu_custom_call" | custom-call | flops 3623878656 | bytes 12582912 | tf_op jit(solution)/shard_map/head_grads/pallas_call | solution.py:273
  727.0 33.3 %all_to_all.35 = bf16[16,96,288]{2,1,0:T(8,128)(2,1)S(1)} all-to-all(bf16[16,96,288]{2,1,0:T(8,128)(2,1)S(1)} %bitcast.178), channel_id=1, replica_groups=mesh['fsdp'=16,'tp'=2] {'fsdp'}, dimensions={0} | all-to-all | bytes 1769472 | tf_op jit(solution)/shard_map/all_to_all | solution.py:49
  780.5 12.9 %all-to-all-done.4 = bf16[8,288,512]{2,1,0:T(8,128)(2,1)} async-done(((bf16[8,288,512]{2,1,0:T(8,128)(2,1)}), bf16[8,288,512]{2,1,0:T(8,128)(2,1)}, u32[]{:S(2)}, u32[]{:S(2)}) %all-to-all-start.4) | async-done | bytes 2359328 | tf_op jit(solution)/shard_map/all_to_all | solution.py:49
  811.2 96.4 %reduce-scatter.2.cloned.1.call-done = bf16[96,768]{1,0:T(8,128)(2,1)} async-done(((bf16[1536,768]{1,0:T(8,128)(2,1)}), bf16[96,768]{1,0:T(8,128)(2,1)}) %reduce-scatter.2.cloned.1.call-update) | async-done | bytes 147472 | tf_op jit(solution)/shard_map/reduce_scatter | solution.py:451
  (359 shorter events, 293.9 us)
Async XLA Ops:
  7.2 167.2 %all-gather.6.cloned.1.call-start = ((), (), s32[]{:S(2)}) async-start(), calls=%async_computation.10 | async-start | bytes 2506752 | tf_op jit(solution)/shard_map/all_gather | solution.py:396
  19.2 70.8 %all-to-all-start = ((bf16[16,96,290]{2,1,0:T(8,128)(2,1)}), bf16[16,96,290]{2,1,0:T(8,128)(2,1)S(1)}, u32[]{:S(2)}, u32[]{:S(2)}) async-start(bf16[16,96,290]{2,1,0:T(8,128)(2,1)} %bitcast.186), calls=%async_computation | async-start | bytes 2359296 | tf_op jit(solution)/shard_map/all_to_all | solution.py:49
  28.0 47.9 %collective-permute-start.9 = (bf16[256,1536]{1,0:T(8,128)(2,1)}, bf16[256,1536]{1,0:T(8,128)(2,1)S(1)}, u32[]{:S(2)}, u32[]{:S(2)}) collective-permute-start(bf16[256,1536]{1,0:T(8,128)(2,1)} %collective-permute-done.1), channel_id=1, source_target_pairs={{0,8},{2,10},{4,12},{6,14},{8,0},{10,2},{12,4},{14,6},{16,24},{18,... | collective-permute-start | bytes 2359304 | tf_op jit(solution)/shard_map/ppermute | solution.py:35
  29.2 51.9 %collective-permute-start.2 = (bf16[256,1536]{1,0:T(8,128)(2,1)}, bf16[256,1536]{1,0:T(8,128)(2,1)S(1)}, u32[]{:S(2)}, u32[]{:S(2)}) collective-permute-start(bf16[256,1536]{1,0:T(8,128)(2,1)} %collective-permute-done.1), channel_id=1, source_target_pairs={{0,1},{1,0},{2,3},{3,2},{4,5},{5,4},{6,7},{7,6},{8,9},{9,8},{10,11... | collective-permute-start | bytes 2359304 | tf_op jit(solution)/shard_map/ppermute | solution.py:39
  39.6 61.1 %collective-permute-start.8 = (bf16[256,1536]{1,0:T(8,128)(2,1)}, bf16[256,1536]{1,0:T(8,128)(2,1)}, u32[]{:S(2)}, u32[]{:S(2)}) collective-permute-start(bf16[256,1536]{1,0:T(8,128)(2,1)} %collective-permute-done.7), channel_id=1, source_target_pairs={{0,1},{1,0},{2,3},{3,2},{4,5},{5,4},{6,7},{7,6},{8,9},{9,8},{10,11... | collective-permute-start | bytes 2359304 | tf_op jit(solution)/shard_map/ppermute | solution.py:39
  209.7 100.9 %collective-permute-start.26 = (bf16[384,1536]{1,0:T(8,128)(2,1)}, bf16[384,1536]{1,0:T(8,128)(2,1)}, u32[]{:S(2)}, u32[]{:S(2)}) collective-permute-start(bf16[384,1536]{1,0:T(8,128)(2,1)} %bitcast.50), channel_id=1, source_target_pairs={{0,16},{2,18},{4,20},{6,22},{8,24},{10,26},{12,28},{14,30},{16,0},... | collective-permute-start | bytes 3538952 | tf_op jit(solution)/shard_map/ppermute | solution.py:35
  209.7 102.0 %collective-permute-start.25 = (bf16[384,1536]{1,0:T(8,128)(2,1)}, bf16[384,1536]{1,0:T(8,128)(2,1)}, u32[]{:S(2)}, u32[]{:S(2)}) collective-permute-start(bf16[384,1536]{1,0:T(8,128)(2,1)} %bitcast.50), channel_id=1, source_target_pairs={{0,8},{2,10},{4,12},{6,14},{8,0},{10,2},{12,4},{14,6},{16,24},{18,... | collective-permute-start | bytes 3538952 | tf_op jit(solution)/shard_map/ppermute | solution.py:35
  215.0 102.3 %collective-permute-start.35 = (bf16[256,1536]{1,0:T(8,128)(2,1)}, bf16[256,1536]{1,0:T(8,128)(2,1)}, u32[]{:S(2)}, u32[]{:S(2)}) collective-permute-start(bf16[256,1536]{1,0:T(8,128)(2,1)} %get-tuple-element.71), channel_id=1, source_target_pairs={{0,4},{2,6},{4,0},{6,2},{8,12},{10,14},{12,8},{14,10},{16,20},{18,... | collective-permute-start | bytes 2359304 | tf_op jit(solution)/shard_map/ppermute | solution.py:35
  216.2 102.4 %collective-permute-start.33 = (bf16[256,1536]{1,0:T(8,128)(2,1)}, bf16[256,1536]{1,0:T(8,128)(2,1)}, u32[]{:S(2)}, u32[]{:S(2)}) collective-permute-start(bf16[256,1536]{1,0:T(8,128)(2,1)} %get-tuple-element.71), channel_id=1, source_target_pairs={{0,2},{2,0},{4,6},{6,4},{8,10},{10,8},{12,14},{14,12},{16,18},{18,... | collective-permute-start | bytes 2359304 | tf_op jit(solution)/shard_map/ppermute | solution.py:35
  235.6 83.2 %collective-permute-start.32 = (bf16[256,1536]{1,0:T(8,128)(2,1)}, bf16[256,1536]{1,0:T(8,128)(2,1)}, u32[]{:S(2)}, u32[]{:S(2)}) collective-permute-start(bf16[256,1536]{1,0:T(8,128)(2,1)} %get-tuple-element.71), channel_id=1, source_target_pairs={{0,1},{1,0},{2,3},{3,2},{4,5},{5,4},{6,7},{7,6},{8,9},{9,8},{10,11... | collective-permute-start | bytes 2359304 | tf_op jit(solution)/shard_map/ppermute | solution.py:39
  318.6 52.8 %collective-permute-start.21 = (bf16[256,1536]{1,0:T(8,128)(2,1)}, bf16[256,1536]{1,0:T(8,128)(2,1)S(1)}, u32[]{:S(2)}, u32[]{:S(2)}) collective-permute-start(bf16[256,1536]{1,0:T(8,128)(2,1)} %get-tuple-element.77), channel_id=1, source_target_pairs={{0,4},{2,6},{4,0},{6,2},{8,12},{10,14},{12,8},{14,10},{16,20},{18,... | collective-permute-start | bytes 2359304 | tf_op jit(solution)/shard_map/ppermute | solution.py:35
  318.9 53.6 %collective-permute-start.23 = (bf16[256,1536]{1,0:T(8,128)(2,1)}, bf16[256,1536]{1,0:T(8,128)(2,1)S(1)}, u32[]{:S(2)}, u32[]{:S(2)}) collective-permute-start(bf16[256,1536]{1,0:T(8,128)(2,1)} %get-tuple-element.77), channel_id=1, source_target_pairs={{0,6},{2,4},{4,2},{6,0},{8,14},{10,12},{12,10},{14,8},{16,22},{18,... | collective-permute-start | bytes 2359304 | tf_op jit(solution)/shard_map/ppermute | solution.py:35
  328.5 44.0 %collective-permute-start.34 = (bf16[256,1536]{1,0:T(8,128)(2,1)}, bf16[256,1536]{1,0:T(8,128)(2,1)S(1)}, u32[]{:S(2)}, u32[]{:S(2)}) collective-permute-start(bf16[256,1536]{1,0:T(8,128)(2,1)} %collective-permute-done.33), channel_id=1, source_target_pairs={{0,1},{1,0},{2,3},{3,2},{4,5},{5,4},{6,7},{7,6},{8,9},{9,8},{10,11... | collective-permute-start | bytes 2359304 | tf_op jit(solution)/shard_map/ppermute | solution.py:39
  335.1 39.2 %collective-permute-start.36 = (bf16[256,1536]{1,0:T(8,128)(2,1)}, bf16[256,1536]{1,0:T(8,128)(2,1)S(1)}, u32[]{:S(2)}, u32[]{:S(2)}) collective-permute-start(bf16[256,1536]{1,0:T(8,128)(2,1)} %collective-permute-done.35), channel_id=1, source_target_pairs={{0,1},{1,0},{2,3},{3,2},{4,5},{5,4},{6,7},{7,6},{8,9},{9,8},{10,11... | collective-permute-start | bytes 2359304 | tf_op jit(solution)/shard_map/ppermute | solution.py:39
  458.7 41.7 %collective-permute-start.29 = (bf16[256,1536]{1,0:T(8,128)(2,1)S(1)}, bf16[256,1536]{1,0:T(8,128)(2,1)S(1)}, u32[]{:S(2)}, u32[]{:S(2)}) collective-permute-start(bf16[256,1536]{1,0:T(8,128)(2,1)S(1)} %get-tuple-element.56), channel_id=1, source_target_pairs={{0,2},{2,0},{4,6},{6,4},{8,10},{10,8},{12,14},{14,12},{16,18},{18,... | collective-permute-start | bytes 2359304 | tf_op jit(solution)/shard_map/ppermute | solution.py:35
  459.0 58.3 %collective-permute-start.31 = (bf16[256,1536]{1,0:T(8,128)(2,1)S(1)}, bf16[256,1536]{1,0:T(8,128)(2,1)S(1)}, u32[]{:S(2)}, u32[]{:S(2)}) collective-permute-start(bf16[256,1536]{1,0:T(8,128)(2,1)S(1)} %get-tuple-element.57), channel_id=1, source_target_pairs={{0,6},{2,4},{4,2},{6,0},{8,14},{10,12},{12,10},{14,8},{16,22},{18,... | collective-permute-start | bytes 2359304 | tf_op jit(solution)/shard_map/ppermute | solution.py:35
  466.8 51.4 %collective-permute-start.30 = (bf16[256,1536]{1,0:T(8,128)(2,1)S(1)}, bf16[256,1536]{1,0:T(8,128)(2,1)S(1)}, u32[]{:S(2)}, u32[]{:S(2)}) collective-permute-start(bf16[256,1536]{1,0:T(8,128)(2,1)S(1)} %get-tuple-element.58), channel_id=1, source_target_pairs={{0,4},{2,6},{4,0},{6,2},{8,12},{10,14},{12,8},{14,10},{16,20},{18,... | collective-permute-start | bytes 2359304 | tf_op jit(solution)/shard_map/ppermute | solution.py:35
  532.9 57.6 %collective-permute-start.47 = (bf16[384,1536]{0,1:T(8,128)(2,1)}, bf16[384,1536]{0,1:T(8,128)(2,1)}, u32[]{:S(2)}, u32[]{:S(2)}) collective-permute-start(bf16[384,1536]{0,1:T(8,128)(2,1)} %get-tuple-element.51), channel_id=1, source_target_pairs={{0,24},{2,26},{4,28},{6,30},{8,16},{10,18},{12,20},{14,22},{16,8},... | collective-permute-start | bytes 3538952 | tf_op jit(solution)/shard_map/ppermute | solution.py:35
  534.6 122.0 %collective-permute-start.46 = (bf16[384,1536]{0,1:T(8,128)(2,1)}, bf16[384,1536]{0,1:T(8,128)(2,1)}, u32[]{:S(2)}, u32[]{:S(2)}) collective-permute-start(bf16[384,1536]{0,1:T(8,128)(2,1)} %get-tuple-element.52), channel_id=1, source_target_pairs={{0,16},{2,18},{4,20},{6,22},{8,24},{10,26},{12,28},{14,30},{16,0},... | collective-permute-start | bytes 3538952 | tf_op jit(solution)/shard_map/ppermute | solution.py:35
  540.5 122.9 %all-to-all-start.3 = ((bf16[8,96,512]{2,1,0:T(8,128)(2,1)}), bf16[8,96,512]{2,1,0:T(8,128)(2,1)S(1)}, u32[]{:S(2)}, u32[]{:S(2)}) async-start(bf16[8,96,512]{2,1,0:T(8,128)(2,1)} %bitcast.66), calls=%async_computation.3 | async-start | bytes 1572864 | tf_op jit(solution)/shard_map/all_to_all | solution.py:49
  544.1 254.7 %all-gather.4.cloned.1.call-start = ((), (), s32[]{:S(2)}) async-start(), calls=%async_computation.8 | async-start | bytes 5013504 | tf_op jit(solution)/shard_map/all_gather | solution.py:397
  663.5 63.6 %all-to-all-start.6 = ((bf16[4,96,1536]{2,1,0:T(8,128)(2,1)}), bf16[4,96,1536]{2,1,0:T(8,128)(2,1)}, u32[]{:S(2)}, u32[]{:S(2)}) async-start(bf16[4,96,1536]{2,1,0:T(8,128)(2,1)} %bitcast.188), calls=%async_computation.6 | async-start | bytes 2359296 | tf_op jit(solution)/shard_map/all_to_all | solution.py:49
  764.9 142.8 %reduce-scatter.2.cloned.1.call-start = ((), (), s32[]{:S(2)}) async-start(), calls=%async_computation.9 | async-start | bytes 2506752 | tf_op jit(solution)/shard_map/reduce_scatter | solution.py:451
  804.7 104.5 %collective-permute-start.44 = (f32[256,1536]{1,0:T(8,128)}, f32[256,1536]{1,0:T(8,128)}, u32[]{:S(2)}, u32[]{:S(2)}) collective-permute-start(f32[256,1536]{1,0:T(8,128)} %fusion.48), channel_id=1, source_target_pairs={{0,1},{1,0},{2,3},{3,2},{4,5},{5,4},{6,7},{7,6},{8,9},{9,8},{10,11... | collective-permute-start | bytes 4718600 | tf_op jit(solution)/shard_map/ppermute | solution.py:39
  (94 other events, 1452.3 us)
Sparse Core Ops, SparseCore 0:
  13.0 81.3 all-gather.5
  548.3 155.2 all-gather.3
  770.6 136.9 reduce-scatter.1

commit v2 on v1

v2 whole, which is shorter than its diff:
```python
import functools
import math

import jax
import jax.numpy as jnp
from jax import lax
from jax.experimental import pallas as pl
from jax.experimental.pallas import tpu as pltpu
from jax.sharding import PartitionSpec as P

HEAD_SIZE = 96
HALF = HEAD_SIZE // 2
SPANS = 8
PLANE = 4
PACKED_LENGTH = 4096
SPAN = PACKED_LENGTH // SPANS

rope_base = 100000.0
norm_eps = 1e-05
masked_score = -1000000000.0
scale = HEAD_SIZE ** (-0.5)
scale_log2 = scale * math.log2(math.e)
bf16 = jnp.bfloat16
f32 = jnp.float32


def dot(left, right, left_dim=1, right_dim=0):
    return lax.dot_general(
        left, right, (((left_dim,), (right_dim,)), ((), ())), preferred_element_type=f32
    )


def hop(value, distance):
    count = lax.axis_size("fsdp")
    return lax.ppermute(value, "fsdp", [(i, i ^ distance) for i in range(count)])


def swap(value):
    return lax.ppermute(value, "tp", [(0, 1), (1, 0)])


def groups_of(size):
    count = lax.axis_size("fsdp")
    return [list(range(first, first + size)) for first in range(0, count, size)]


def exchange(value, size):
    groups = None if size == lax.axis_size("fsdp") else groups_of(size)
    return lax.all_to_all(value, "fsdp", 0, 0, axis_index_groups=groups)


def project_kernel(*refs):
    pieces, (place_ref, head_ref, cos_ref, sin_ref) = refs[:2 * SPANS], refs[2 * SPANS:2 * SPANS + 4]
    normed_ref, gain_ref, q_t_ref, k_t_ref, v_t_ref, q_ref, k_ref, v_ref = refs[2 * SPANS + 4:2 * SPANS + 12]
    in_buf, out_buf, in_sem, out_sem = refs[2 * SPANS + 12:]
    rows = pieces[0].shape[0]
    place, core = place_ref[0], place_ref[1]

    def fetch(pair, part):
        return pltpu.make_async_copy(
            pieces[2 * pair + part],
            in_buf.at[pair % 3, pl.ds(pl.multiple_of((core ^ part) * rows, rows), rows)],
            in_sem.at[pair % 3, part],
        )

    def store(pair):
        return pltpu.make_async_copy(out_buf.at[pair % 2], normed_ref.at[place ^ pair], out_sem.at[pair % 2])

    for pair in range(2):
        for part in range(2):
            fetch(pair, part).start()
    row = lax.broadcasted_iota(jnp.int32, (8, head_ref.shape[1]), 0)
    column = lax.broadcasted_iota(jnp.int32, (8, head_ref.shape[1]), 1)
    pick = (column == row + 3 * HEAD_SIZE).astype(f32).astype(bf16)
    gains = dot(pick, head_ref[...], 1, 1)
    gain = gains[0:1]
    gain_ref[...] = gains
    for pair in range(SPANS):
        for part in range(2):
            fetch(pair, part).wait()
        if pair + 2 < SPANS:
            for part in range(2):
                fetch(pair + 2, part).start()
        if pair >= 2:
            store(pair - 2).wait()
        x = in_buf[pair % 3].astype(f32)
        factor = lax.rsqrt(jnp.mean(x * x, axis=-1, keepdims=True) + norm_eps)
        normed = (x * factor * gain).astype(bf16)
        out_buf[pair % 2] = normed
        store(pair).start()
        product = dot(normed, head_ref[:, :3 * HEAD_SIZE]).T
        here = pl.ds(pl.multiple_of((place ^ pair) * 2 * rows, 2 * rows), 2 * rows)
        cosine, sine = cos_ref[:, here], sin_ref[:, here]
        for number, (t_ref, n_ref) in enumerate(((q_t_ref, q_ref), (k_t_ref, k_ref))):
            first = product[number * HEAD_SIZE:number * HEAD_SIZE + HALF]
            second = product[number * HEAD_SIZE + HALF:(number + 1) * HEAD_SIZE]
            turned = jnp.concatenate(
                [first * cosine - second * sine, second * cosine + first * sine], axis=0
            )
            t_ref[:, here] = turned.astype(bf16)
            n_ref[here, :] = turned.T.astype(bf16)
        value = product[2 * HEAD_SIZE:3 * HEAD_SIZE]
        v_t_ref[:, here] = value.astype(bf16)
        v_ref[here, :] = value.T.astype(bf16)
    for pair in range(SPANS - 2, SPANS):
        store(pair).wait()


def project(pieces, head_set, places, cosine, sine):
    rows, width = pieces[0].shape
    tokens = 2 * SPANS * rows
    vmem = pl.BlockSpec(memory_space=pltpu.VMEM)
    anywhere = pl.BlockSpec(memory_space=pl.ANY)
    return pl.pallas_call(
        project_kernel,
        in_specs=[anywhere] * len(pieces) + [pl.BlockSpec(memory_space=pltpu.SMEM), vmem, vmem, vmem],
        out_specs=[anywhere] + [vmem] * 7,
        out_shape=[
            jax.ShapeDtypeStruct((SPANS, 2 * rows, width), bf16),
            jax.ShapeDtypeStruct((8, width), f32),
        ]
        + [jax.ShapeDtypeStruct((HEAD_SIZE, tokens), bf16)] * 3
        + [jax.ShapeDtypeStruct((tokens, HEAD_SIZE), bf16)] * 3,
        scratch_shapes=[
            pltpu.VMEM((3, 2 * rows, width), bf16),
            pltpu.VMEM((2, 2 * rows, width), bf16),
            pltpu.SemaphoreType.DMA((3, 2)),
            pltpu.SemaphoreType.DMA((2,)),
        ],
        compiler_params=pltpu.CompilerParams(vmem_limit_bytes=56 * 2**20),
        cost_estimate=pl.CostEstimate(
            flops=2 * tokens * width * 3 * HEAD_SIZE,
            bytes_accessed=4 * tokens * width,
            transcendentals=0,
        ),
        name="project",
    )(*pieces, places, head_set, cosine, sine)


def widened(column):
    return jnp.concatenate([column] * (SPAN // column.shape[1]), axis=1)


def causal_tile():
    key_at = lax.broadcasted_iota(jnp.int32, (SPAN, SPAN), 0)
    query_at = lax.broadcasted_iota(jnp.int32, (SPAN, SPAN), 1)
    return key_at <= query_at


def forward_kernel(q_t_ref, k_ref, v_t_ref, id_row_ref, id_col_ref, out_ref, out_full_ref, lse_ref):
    block = pl.program_id(0)
    query = q_t_ref[...]
    id_row = id_row_ref[...]

    def step(at, carry, diagonal):
        best, total, result = carry
        keys = pl.ds(pl.multiple_of(at * SPAN, SPAN), SPAN)
        scores = dot(k_ref[keys, :], query) * scale_log2
        allowed = widened(id_col_ref[keys, :]) == id_row
        if diagonal:
            allowed = allowed & causal_tile()
        scores = jnp.where(allowed, scores, masked_score)
        larger = jnp.maximum(best, jnp.max(scores, axis=0, keepdims=True))
        weights = jnp.exp2(scores - larger)
        faded = jnp.exp2(best - larger)
        total = total * faded + jnp.sum(weights, axis=0, keepdims=True)
        result = result * faded + dot(v_t_ref[:, keys], weights.astype(bf16))
        return larger, total, result

    carry = (
        jnp.full((1, SPAN), masked_score, f32),
        jnp.zeros((1, SPAN), f32),
        jnp.zeros((HEAD_SIZE, SPAN), f32),
    )
    carry = lax.fori_loop(0, block, lambda at, c: step(at, c, False), carry)
    best, total, result = step(block, carry, True)
    result = result / total
    out_full_ref[...] = result
    out_ref[0] = result.astype(bf16)
    lse_ref[...] = best + jnp.log2(total)


def attention_forward(q_t, k, v_t, id_row, id_col):
    tokens = k.shape[0]
    whole = lambda array: pl.BlockSpec(array.shape, lambda i: (0, 0))
    return pl.pallas_call(
        forward_kernel,
        grid=(SPANS,),
        in_specs=[
            pl.BlockSpec((HEAD_SIZE, SPAN), lambda i: (0, i)),
            whole(k),
            whole(v_t),
            pl.BlockSpec((1, SPAN), lambda i: (0, i)),
            whole(id_col),
        ],
        out_specs=[
            pl.BlockSpec((1, HEAD_SIZE, SPAN), lambda i: (i, 0, 0)),
            pl.BlockSpec((HEAD_SIZE, SPAN), lambda i: (0, i)),
            pl.BlockSpec((1, SPAN), lambda i: (0, i)),
        ],
        out_shape=[
            jax.ShapeDtypeStruct((SPANS, HEAD_SIZE, SPAN), bf16),
            jax.ShapeDtypeStruct((HEAD_SIZE, tokens), f32),
            jax.ShapeDtypeStruct((1, tokens), f32),
        ],
        compiler_params=pltpu.CompilerParams(vmem_limit_bytes=40 * 2**20),
        cost_estimate=pl.CostEstimate(
            flops=36 * SPAN * SPAN * 256 * 4 * 4, bytes_accessed=8 * 2**20, transcendentals=36 * SPAN * SPAN
        ),
        name="attention_forward",
    )(q_t, k, v_t, id_row, id_col)


def backward_kernel(cubes, q_t_ref, q_ref, k_t_ref, k_ref, v_ref, dout_ref, out_ref, lse_ref, id_row_ref, id_col_ref,
                    cos_ref, sin_ref, normed_ref, grad_ref, delta_ref, dout_n_ref, dq_ref, sum_ref):
    block = pl.program_id(0)

    @pl.when(block == 0)
    def _():
        for at in range(SPANS):
            dout = dout_ref[at]
            here = slice(at * SPAN, (at + 1) * SPAN)
            delta_ref[:, here] = jnp.sum(dout.astype(f32) * out_ref[:, here], axis=0, keepdims=True)
            dout_n_ref[here, :] = dout.astype(f32).T.astype(bf16)
        dq_ref[...] = jnp.zeros(dq_ref.shape, f32)
        sum_ref[...] = jnp.zeros(sum_ref.shape, f32)

    key_t, key, value = k_t_ref[...], k_ref[...], v_ref[...]
    id_col = widened(id_col_ref[...])

    def step(at, carry, diagonal):
        dkey, dvalue = carry
        rows = pl.ds(pl.multiple_of(at * SPAN, SPAN), SPAN)
        scores = dot(key, q_t_ref[:, rows]) * scale_log2 - lse_ref[:, rows]
        allowed = id_col == id_row_ref[:, rows]
        if diagonal:
            allowed = allowed & causal_tile()
        probs = jnp.exp2(jnp.where(allowed, scores, masked_score))
        dprobs = dot(value, dout_ref[at])
        dscores = (probs * (dprobs - delta_ref[:, rows])).astype(bf16)
        dvalue = dvalue + dot(probs.astype(bf16), dout_n_ref[rows, :])
        dkey = dkey + dot(dscores, q_ref[rows, :])
        dq_ref[at] += dot(key_t, dscores)
        return dkey, dvalue

    zero = jnp.zeros((SPAN, HEAD_SIZE), f32)
    carry = step(block, (zero, zero), True)
    dkey, dvalue = lax.fori_loop(block + 1, SPANS, lambda at, c: step(at, c, False), carry)
    cosine, sine = cos_ref[...], sin_ref[...]
    for number, grad in enumerate((dq_ref[block], dkey.T)):
        first = grad[:HALF] * scale
        second = grad[HALF:] * scale
        turned = jnp.concatenate(
            [first * cosine + second * sine, second * cosine - first * sine], axis=0
        )
        grad_ref[block, number * HEAD_SIZE:(number + 1) * HEAD_SIZE, :SPAN] = turned.astype(bf16)
    grad_ref[block, 2 * HEAD_SIZE:, :SPAN] = dvalue.T.astype(bf16)
    sum_ref[...] += dot(grad_ref[block, :, :SPAN], normed_ref[0])

    @pl.when(block == SPANS - 1)
    def _():
        part = sum_ref.shape[1] // SPANS
        shard = part // cubes
        for place in range(SPANS):
            pieces = [
                sum_ref[:, (cube * SPANS + place) * shard:(cube * SPANS + place + 1) * shard] for cube in range(cubes)
            ]
            grad_ref[place, :, SPAN:] = jnp.concatenate(pieces, axis=1).astype(bf16)


def attention_backward(q_t, q, k_t, k, v, dout, out, lse, id_row, id_col, cosine, sine, normed, cubes):
    tokens = k.shape[0]
    width = normed.shape[2]
    whole = lambda array: pl.BlockSpec(array.shape, lambda i: (0,) * array.ndim)
    wide = pl.BlockSpec((HEAD_SIZE, SPAN), lambda i: (0, i))
    tall = pl.BlockSpec((SPAN, HEAD_SIZE), lambda i: (i, 0))
    table = pl.BlockSpec((HALF, SPAN), lambda i: (0, i))
    return pl.pallas_call(
        functools.partial(backward_kernel, cubes),
        grid=(SPANS,),
        in_specs=[
            whole(q_t), whole(q), wide, tall, tall, whole(dout), whole(out), whole(lse), whole(id_row),
            pl.BlockSpec((SPAN, id_col.shape[1]), lambda i: (i, 0)), table, table,
            pl.BlockSpec((1, SPAN, width), lambda i: (i, 0, 0)),
        ],
        out_specs=pl.BlockSpec((SPANS, 3 * HEAD_SIZE, SPAN + width // SPANS), lambda i: (0, 0, 0)),
        out_shape=jax.ShapeDtypeStruct((SPANS, 3 * HEAD_SIZE, SPAN + width // SPANS), bf16),
        scratch_shapes=[
            pltpu.VMEM((1, tokens), f32),
            pltpu.VMEM((tokens, HEAD_SIZE), bf16),
            pltpu.VMEM((SPANS, HEAD_SIZE, SPAN), f32),
            pltpu.VMEM((3 * HEAD_SIZE, width), f32),
        ],
        compiler_params=pltpu.CompilerParams(vmem_limit_bytes=56 * 2**20),
        cost_estimate=pl.CostEstimate(
            flops=36 * SPAN * SPAN * 256 * 10 * 4, bytes_accessed=12 * 2**20, transcendentals=36 * SPAN * SPAN
        ),
        name="attention_backward",
    )(q_t, q, k_t, k, v, dout, out, lse, id_row, id_col, cosine, sine, normed)


def head_finish_kernel(*refs):
    sum_refs, (q_ref, k_ref, v_ref, q_out, k_out, v_out, product_ref) = refs[:-7], refs[-7:]
    total = sum_refs[0][...].astype(f32)
    for ref in sum_refs[1:]:
        total = total + ref[...].astype(f32)
    total = total.T
    product = jnp.zeros(product_ref.shape, f32)
    at = 0
    for ref, out in ((q_ref, q_out), (k_ref, k_out), (v_ref, v_out)):
        grad = total[:, at:at + out.shape[1]]
        at += out.shape[1]
        out[...] = grad
        product = product + jnp.sum(grad * ref[...].astype(f32), axis=1, keepdims=True)
    product_ref[...] = product


def head_finish(sums, q_weight, k_weight, v_weight):
    vmem = pl.BlockSpec(memory_space=pltpu.VMEM)
    return pl.pallas_call(
        head_finish_kernel,
        in_specs=[vmem] * (len(sums) + 3),
        out_specs=[vmem] * 4,
        out_shape=[jax.ShapeDtypeStruct(w.shape, f32) for w in (q_weight, k_weight, v_weight)]
        + [jax.ShapeDtypeStruct((q_weight.shape[0], 1), f32)],
        compiler_params=pltpu.CompilerParams(vmem_limit_bytes=32 * 2**20),
        name="head_finish",
    )(*sums, q_weight, k_weight, v_weight)


def unit_finish_kernel(place_ref, *refs):
    piece_refs, (gate_w_ref, up_w_ref, gate_out, up_out, down_out, product_ref) = refs[:PLANE], refs[PLANE:]
    units = gate_out.shape[1] // PLANE
    for link, piece_ref in enumerate(piece_refs):
        here = pl.ds(pl.multiple_of((place_ref[0] ^ link) * units, units), units)
        for number, out in enumerate((gate_out, up_out, down_out)):
            out[:, here] = piece_ref[:, number * units:(number + 1) * units].astype(f32)
    product_ref[...] = jnp.sum(
        gate_out[...] * gate_w_ref[...].astype(f32) + up_out[...] * up_w_ref[...].astype(f32), axis=1, keepdims=True
    )


def unit_finish(place, pieces, gate_weight, up_weight):
    vmem = pl.BlockSpec(memory_space=pltpu.VMEM)
    return pl.pallas_call(
        unit_finish_kernel,
        in_specs=[pl.BlockSpec(memory_space=pltpu.SMEM)] + [vmem] * (PLANE + 2),
        out_specs=[vmem] * 4,
        out_shape=[jax.ShapeDtypeStruct(gate_weight.shape, f32)] * 3
        + [jax.ShapeDtypeStruct((gate_weight.shape[0], 1), f32)],
        compiler_params=pltpu.CompilerParams(vmem_limit_bytes=32 * 2**20),
        name="unit_finish",
    )(place, *pieces, gate_weight, up_weight)


def unit_grad_kernel(*refs):
    tables, out_ref = (refs[:3 * PLANE], refs[3 * PLANE:6 * PLANE]), refs[6 * PLANE]
    column = 0
    for table in tables:
        total = None
        for k, right in enumerate(table[2 * PLANE:]):
            left = jnp.concatenate([table[2 * k][...], table[2 * k + 1][...]], axis=0)
            term = dot(left, right[...], 0, 0)
            total = term if total is None else total + term
        out_ref[:, column:column + total.shape[1]] = total.astype(bf16)
        column += total.shape[1]


def unit_grads(normed, dgate_up, dout, act):
    tokens, width = normed[0].shape
    rows = width // 4
    whole = lambda array: pl.BlockSpec(array.shape, lambda i: (0, 0))
    left = [pl.BlockSpec((tokens, rows), lambda i: (0, i))] * (2 * PLANE)
    columns = dgate_up[0].shape[1] + act[0].shape[1]
    return pl.pallas_call(
        unit_grad_kernel,
        grid=(width // rows,),
        in_specs=left + [whole(part) for part in dgate_up] + left + [whole(part) for part in act],
        out_specs=pl.BlockSpec((rows, columns), lambda i: (i, 0)),
        out_shape=jax.ShapeDtypeStruct((width, columns), bf16),
        compiler_params=pltpu.CompilerParams(vmem_limit_bytes=48 * 2**20),
        cost_estimate=pl.CostEstimate(
            flops=2 * 2 * tokens * PLANE * width * columns, bytes_accessed=24 * 2**20, transcendentals=0
        ),
        name="unit_grads",
    )(*normed, *dgate_up, *dout, *act)


def feed_kernel(pairs, *refs):
    ins, weight_ref, refs = refs[:4 * pairs], refs[4 * pairs], refs[4 * pairs + 1:]
    units = weight_ref.shape[1] // 3
    weight = weight_ref[:, :2 * units]
    down_weight = weight_ref[:, 2 * units:]
    for pair in range(pairs):
        own_ref, other_ref, d_own_ref, d_other_ref = ins[4 * pair:4 * pair + 4]
        kept_ref, sent_ref, out_kept_ref, out_sent_ref, dgate_up_ref, act_ref = refs[6 * pair:6 * pair + 6]
        rows = own_ref.shape[0]
        gate_up = dot(jnp.concatenate([own_ref[...], other_ref[...]], axis=0), weight)
        dact = dot(jnp.concatenate([d_own_ref[...], d_other_ref[...]], axis=0), down_weight)
        gate, up = gate_up[:, :units], gate_up[:, units:]
        sigma = 1.0 / (1.0 + jnp.exp(-gate))
        silu = gate * sigma
        dgate_up_ref[:, :units] = (dact * up * sigma * (1.0 + gate * (1.0 - sigma))).astype(bf16)
        dgate_up_ref[:, units:] = (dact * silu).astype(bf16)
        act_ref[...] = (silu * up).astype(bf16)
        dnormed = dot(dgate_up_ref[...], weight, 1, 1)
        kept_ref[...] = dnormed[:rows]
        sent_ref[...] = dnormed[rows:].astype(bf16)
        out = dot(act_ref[...], down_weight, 1, 1)
        out_kept_ref[...] = out[:rows]
        out_sent_ref[...] = out[rows:].astype(bf16)


def feed(rows_list, weight):
    pairs = len(rows_list)
    rows, width = rows_list[0][0].shape
    units = weight.shape[1] // 3
    vmem = pl.BlockSpec(memory_space=pltpu.VMEM)
    halves = [jax.ShapeDtypeStruct((rows, width), f32), jax.ShapeDtypeStruct((rows, width), bf16)]
    shapes = (
        halves * 2 + [jax.ShapeDtypeStruct((2 * rows, 2 * units), bf16), jax.ShapeDtypeStruct((2 * rows, units), bf16)]
    ) * pairs
    ins = [part for group in rows_list for part in group]
    outs = pl.pallas_call(
        functools.partial(feed_kernel, pairs),
        in_specs=[vmem] * (len(ins) + 1),
        out_specs=[vmem] * len(shapes),
        out_shape=shapes,
        compiler_params=pltpu.CompilerParams(vmem_limit_bytes=48 * 2**20),
        cost_estimate=pl.CostEstimate(
            flops=pairs * 2 * 2 * rows * width * units * 6, bytes_accessed=8 * 2**20, transcendentals=2 * rows * units
        ),
        name="feed",
    )(*ins, weight)
    return [outs[6 * pair:6 * pair + 6] for pair in range(pairs)]


def back_kernel(core_ref, back_ref, weight_ref, mine_ref, other_ref, head_ref, table_ref):
    heads = back_ref.shape[0]
    kv_heads = (table_ref.shape[0] // HEAD_SIZE - heads) // 2
    per_kv = heads // kv_heads
    cubes, _, shard = head_ref.shape

    def put(at, value):
        table_ref[at:at + HEAD_SIZE, :] = value[:, :SPAN]
        for cube in range(cubes):
            head_ref[cube, at:at + HEAD_SIZE, :] = value[:, SPAN + cube * shard:SPAN + (cube + 1) * shard]

    for head in range(heads):
        put(head * HEAD_SIZE, back_ref[head, :HEAD_SIZE, :])
    for number in range(2):
        here = slice((number + 1) * HEAD_SIZE, (number + 2) * HEAD_SIZE)
        for head in range(kv_heads):
            total = back_ref[head * per_kv, here, :].astype(f32)
            for copy in range(1, per_kv):
                total = total + back_ref[head * per_kv + copy, here, :].astype(f32)
            put((heads + number * kv_heads + head) * HEAD_SIZE, total.astype(bf16))
    rows = mine_ref.shape[0]
    both = dot(weight_ref[...], table_ref[...])
    low, high = both[:, :rows].T, both[:, rows:].T
    first = core_ref[0] == 0
    mine_ref[...] = jnp.where(first, low, high)
    other_ref[...] = jnp.where(first, high, low)


def input_terms(back, weight, core, cubes):
    vmem = pl.BlockSpec(memory_space=pltpu.VMEM)
    width, features = weight.shape
    rows = SPAN // 2
    shard = (back.shape[2] - SPAN) // cubes
    return pl.pallas_call(
        back_kernel,
        in_specs=[pl.BlockSpec(memory_space=pltpu.SMEM), vmem, vmem],
        out_specs=[vmem] * 3,
        out_shape=[jax.ShapeDtypeStruct((rows, width), f32)] * 2
        + [jax.ShapeDtypeStruct((cubes, features, shard), bf16)],
        scratch_shapes=[pltpu.VMEM((features, SPAN), bf16)],
        compiler_params=pltpu.CompilerParams(vmem_limit_bytes=40 * 2**20),
        cost_estimate=pl.CostEstimate(
            flops=4 * width * features * rows, bytes_accessed=12 * 2**20, transcendentals=0
        ),
        name="input_terms",
    )(core, back, weight)


tie = lax.optimization_barrier


def with_swapped(pieces):
    return [part for piece in pieces for part in (piece, swap(piece))]


def rms_factor(stream):
    return lax.rsqrt(jnp.mean(stream * stream, axis=-1, keepdims=True) + norm_eps)


def norm_backward(stream, factor, gain, dnormed):
    scaled = dnormed * gain
    return factor * scaled - stream * factor**3 * jnp.mean(scaled * stream, axis=-1, keepdims=True)


def body(
    hidden,
    document_index,
    attn_gain,
    q_weight,
    key_matrix,
    value_matrix,
    out_weight,
    mlp_gain,
    gate_weight,
    up_weight,
    down_weight,
    cotangent,
):
    count = lax.axis_size("fsdp")
    planes = count // PLANE
    f = lax.axis_index("fsdp")
    t = lax.axis_index("tp")
    place = f % SPANS
    plane_at = f // PLANE
    own, width = hidden.shape
    shard = q_weight.shape[1]
    q_heads = q_weight.shape[2] // HEAD_SIZE
    kv_heads = key_matrix.shape[2] // HEAD_SIZE
    per_kv = q_heads // kv_heads
    units = gate_weight.shape[2] // PLANE

    def by_head(weight, heads, copies):
        cut = weight[0].reshape(shard, heads, HEAD_SIZE).transpose(1, 0, 2)
        return jnp.repeat(cut, copies, axis=0)

    gains_own = jnp.stack([attn_gain[0], mlp_gain[0]], axis=-1)
    sent = jnp.concatenate(
        [
            by_head(q_weight, q_heads, 1),
            by_head(key_matrix, kv_heads, per_kv),
            by_head(value_matrix, kv_heads, per_kv),
            jnp.broadcast_to(gains_own[None], (SPANS, shard, 2)),
        ],
        axis=-1,
    )
    sent = jnp.tile(sent, (count // SPANS, 1, 1))

    plane_place = f % PLANE
    cubes = count // SPANS
    cube_at = f // SPANS
    half = own // 2
    unit_set = jnp.concatenate(
        [w[0].reshape(shard, PLANE, units).transpose(1, 0, 2) for w in (gate_weight, up_weight, down_weight)],
        axis=-1,
    )
    lines = [list(range(first, count, PLANE)) for first in range(PLANE)]
    p1, p2, p4 = hop(hidden, 1), hop(hidden, 2), hop(hidden, 4)
    out_0 = lax.all_to_all(
        jnp.broadcast_to(out_weight, (planes,) + out_weight.shape[1:]), "fsdp", 0, 0, axis_index_groups=lines
    )
    sent, unit_set, p1, p2, p4, out_0 = tie((sent, unit_set, p1, p2, p4, out_0))
    p3, p6, p5 = hop(p2, 1), hop(p4, 2), hop(p1, 4)
    out_1, out_2 = hop(out_0, 1), hop(out_0, 2)
    head_set = exchange(sent, count).reshape(width, -1)

    own_ids = lax.dynamic_slice_in_dim(document_index, f * SPAN + t * own, own)
    dstream = cotangent.astype(f32) * (own_ids != 0).astype(f32)[:, None]
    dmlp_own = dstream.astype(bf16)
    unit_set, head_set, p3, p6, p5, dmlp_own, out_1, out_2 = tie(
        (unit_set, head_set, p3, p6, p5, dmlp_own, out_1, out_2)
    )
    cut_a, cut_b = own // 128 * 48, own // 128 * 88
    p7 = [hop(p6[:cut_a], 1), hop(p5[cut_a:cut_b], 2), hop(p3[cut_b:], 4)]
    out_3 = hop(out_0, 3)
    unit_own = exchange(unit_set, PLANE).reshape(PLANE * shard, 3 * units)
    dmlp_own, p7, unit_own, out_3 = tie((dmlp_own, p7, unit_own, out_3))
    pieces = with_swapped([hidden, p1, p2, p3, p4, p5, p6, jnp.concatenate(p7, axis=0)])
    dmlp_1, dmlp_2 = hop(dmlp_own, 1), hop(dmlp_own, 2)
    unit_weight = lax.all_gather(unit_own, "fsdp", axis=0, tiled=True, axis_index_groups=lines)
    out_part = jnp.zeros((planes, PLANE, shard, out_0.shape[2]), bf16)
    for k, piece in enumerate((out_0, out_1, out_2, out_3)):
        out_part = lax.dynamic_update_slice_in_dim(out_part, piece[:, None], plane_place ^ k, 1)
    out_part = out_part.reshape(width, -1)
    in_shard = jnp.concatenate([q_weight[0], key_matrix[0], value_matrix[0]], axis=1)

    seq_ids = lax.dynamic_slice_in_dim(document_index, f // SPANS * PACKED_LENGTH, PACKED_LENGTH)
    seq_index = jnp.arange(PACKED_LENGTH, dtype=jnp.int32)
    before = jnp.concatenate([jnp.full((1,), -1, jnp.int32), seq_ids[:-1]])
    starts = lax.cummax(jnp.where(seq_ids != before, seq_index, 0), axis=0)
    positions = (seq_index - starts).astype(f32)
    freq = rope_base ** (-2.0 * jnp.arange(HALF, dtype=f32) / HEAD_SIZE)
    angle = freq[:, None] * positions[None, :]
    cosine, sine = jnp.cos(angle), jnp.sin(angle)
    id_row = seq_ids[None, :]
    id_col = jnp.broadcast_to(seq_ids[:, None], (PACKED_LENGTH, 128))
    places = jnp.stack([place, t]).astype(jnp.int32)

    normed, gains, q_t, k_t, v_t, q, key, v = project(pieces, head_set, places, cosine, sine)
    gain_a, gain_m = gains[0:1], gains[1:2]
    q_t, dmlp_1, dmlp_2 = tie((q_t, dmlp_1, dmlp_2))
    dmlp_3 = [hop(dmlp_2[:half], 1), hop(dmlp_1[half:], 2)]
    out_t, out_full, lse = attention_forward(q_t, key, v_t, id_row, id_col)
    out_t, dmlp_3 = tie((out_t, dmlp_3))
    dmlp = with_swapped([dmlp_own, dmlp_1, dmlp_2, jnp.concatenate(dmlp_3, axis=0)])
    attended = exchange(out_t, SPANS).reshape(q_heads * HEAD_SIZE, SPAN)

    stream = hidden.astype(f32)
    mine = lax.dynamic_slice_in_dim(attended, t * own, own, 1)
    other = lax.dynamic_slice_in_dim(attended, (1 - t) * own, own, 1)
    mid = stream + dot(mine, out_part, 0, 1) + swap(dot(other, out_part, 0, 1))

    factor_m = rms_factor(mid)
    normed_own = (mid * factor_m * gain_m).astype(bf16)
    n1, n2 = hop(normed_own, 1), hop(normed_own, 2)
    n1, n2, normed_late, in_shard = tie((n1, n2, normed_own, in_shard))
    in_part = lax.all_gather(in_shard, "fsdp", axis=0, tiled=True)
    n3 = hop(normed_late, 3)
    normed_m = with_swapped([normed_own, n1, n2])
    results = feed([normed_m[2 * k:2 * k + 2] + dmlp[2 * k:2 * k + 2] for k in range(3)], unit_weight)
    results, n3 = tie((results, n3))
    n3 = with_swapped([n3])
    dn_got = [swap(result[1]) for result in results]
    n3, dn_got = tie((n3, dn_got))
    normed_m += n3
    results += feed([n3 + dmlp[6:8]], unit_weight)
    dn_last, acts = tie((swap(results[3][1]), [result[5] for result in results]))
    dn_got += [dn_last]
    dn_pair = [result[0] + got.astype(f32) for result, got in zip(results, dn_got)]
    dn_far = [dn_pair[0]] + [hop(dn_pair[k].astype(bf16), k) for k in range(1, PLANE)]
    out_pair = [result[2] + swap(result[3]).astype(f32) for result in results]
    out_low = [out_pair[k].astype(bf16) for k in range(1, PLANE)]
    unit_term = unit_grads(normed_m, [result[4] for result in results], dmlp, acts)
    dn_far, out_low, unit_term = tie((dn_far, out_low, unit_term))
    unit_sum = lax.psum_scatter(unit_term, "fsdp", scatter_dimension=0, tiled=True, axis_index_groups=lines)

    dnormed_m = dn_far[0]
    for far in dn_far[1:]:
        dnormed_m = dnormed_m + far.astype(f32)
    dmid = dstream + norm_backward(mid, factor_m, gain_m, dnormed_m)

    dattn = dmid.astype(bf16)
    dattn_other = swap(dattn)
    dattn = jnp.where(
        t == 0,
        jnp.concatenate([dattn, dattn_other], axis=0),
        jnp.concatenate([dattn_other, dattn], axis=0),
    )
    dout = dot(out_part, dattn, 0, 1).astype(bf16)
    dout = exchange(dout.reshape(SPANS, HEAD_SIZE, SPAN), SPANS)
    out_term = dot(dattn, attended, 0, 1).astype(bf16).reshape(planes, PLANE, shard, -1).transpose(1, 0, 2, 3)
    dout, out_term, out_low = tie((dout, out_term, out_low))
    out_term = exchange(out_term.reshape(PLANE, planes * shard, -1), PLANE)
    out_far = [hop(out_low[2], 3)]
    grads = attention_backward(
        q_t, q, k_t, key, v, dout, out_full, lse, id_row, id_col, cosine, sine, normed, cubes
    )
    grads, out_term, out_far, out_low = tie((grads, out_term, out_far, out_low))

    back = exchange(grads, SPANS)
    out_term = out_term.astype(f32).sum(axis=0).reshape(planes, shard, -1)
    out_grad = lax.dynamic_index_in_dim(out_term, plane_at, 0, keepdims=False)
    out_sums = []
    for k in range(1, planes):
        far = lax.dynamic_index_in_dim(out_term, plane_at ^ k, 0, keepdims=False)
        out_sums.append(hop(far.astype(bf16), PLANE * k))
    back, out_low, unit_sum, in_part, out_sums = tie((back, out_low, unit_sum, in_part, out_sums))
    for far in out_sums:
        out_grad = out_grad + far.astype(f32)
    unit_sum = unit_sum.reshape(PLANE, shard, 3 * units)
    unit_back = [lax.dynamic_index_in_dim(unit_sum, plane_place ^ k, 0, keepdims=False) for k in range(PLANE)]
    unit_back = [piece if k == 0 else hop(piece, k) for k, piece in enumerate(unit_back)]
    out_far += [hop(low, k) for k, low in enumerate(out_low[:2], 1)]
    mine, other, head_terms = input_terms(back, in_part, t.reshape(1).astype(jnp.int32), cubes)
    head_sums = [lax.dynamic_index_in_dim(head_terms, cube_at ^ k, 0, keepdims=False) for k in range(cubes)]
    head_sums = [piece if k == 0 else hop(piece, SPANS * k) for k, piece in enumerate(head_sums)]
    dnormed_a = mine + swap(other)
    input_grad = dmid + norm_backward(stream, rms_factor(stream), gain_a, dnormed_a)

    q_grad, k_grad, v_grad, gain_a_part = head_finish(head_sums, q_weight[0], key_matrix[0], value_matrix[0])

    out_total = out_pair[0]
    for far in out_far:
        out_total = out_total + far.astype(f32)
    output = (mid + out_total).astype(bf16)
    gate_grad, up_grad, down_grad, gain_m_part = unit_finish(
        plane_place.reshape(1).astype(jnp.int32), unit_back, gate_weight[0], up_weight[0]
    )

    gain_parts = jnp.concatenate([gain_a_part, gain_m_part], axis=1).T
    gain_grads = (gain_parts + swap(gain_parts)) / jnp.stack([attn_gain[0], mlp_gain[0]]).astype(f32)
    return (
        output,
        input_grad,
        gain_grads[0:1],
        q_grad[None],
        k_grad[None],
        v_grad[None],
        out_grad[None],
        gain_grads[1:2],
        gate_grad[None],
        up_grad[None],
        down_grad[None],
    )


def solution(mesh):
    rows = P(("fsdp", "tp"), None)
    gain = P(None, "fsdp")
    weight = P(None, "fsdp", "tp")
    return jax.shard_map(
        body,
        mesh=mesh,
        in_specs=(rows, P(), gain, weight, weight, weight, weight, gain, weight, weight, weight, rows),
        out_specs=(rows, rows, gain, weight, weight, weight, weight, gain, weight, weight, weight),
        check_vma=False,
    )
```

time: 935 us -> 584 us (0.62)
  waiting for transfers between devices: 471 us -> 231 us
  matrix products: 79.3 us -> 13 us
  Pallas kernels: 92.4 us -> 143 us
  local copies, waits for them, and re-layouts: 101 us -> 50.5 us
  blocking collectives: 33.3 us -> 0 us
  other arithmetic: 50.2 us -> 37.8 us
    ppermute x27 -> x32, waiting for transfers between devices: 335 us -> 175 us  [hop(): lax.ppermute(value, 'fsdp', [(i, i ^ distance) for i in range(count)])]
    reduce_scatter x1, waiting for transfers between devices: 96.4 us -> 0.01 us  [body(): lax.psum_scatter(unit_term, 'fsdp', scatter_dimension=0, tiled=True, axis...]
    dot_general x13 -> x4, matrix products: 79.3 us -> 13 us  [dot(): lax.dot_general(left, right, (((left_dim,), (right_dim,)), ((), ())), pre...]
    pallas_call x3 -> x8, Pallas kernels: 68.9 us -> 120 us  [the longest x1 43.5 us: attention_backward(): pl.pallas_call(functools.partial(backward_kernel, cubes), grid=(SPANS,),...]
    all_to_all x1 -> x0, blocking collectives: 33.3 us -> none  [exchange(): return lax.all_to_all(value, 'fsdp', 0, 0, axis_index_groups=groups)]
    unnamed x149 -> x167, local copies, waits for them, and re-layouts: 56.6 us -> 24 us
    convert_element_type x8 -> x9, other arithmetic: 24.4 us -> 13.7 us  [the longest x3 4.82 us: body(): dn_pair[k].astype(bf16)]
    ppermute x22 -> x28, starting transfers between devices: 28.7 us -> 21.3 us  [swap(): return lax.ppermute(value, 'tp', [(0, 1), (1, 0)])]
  transfers between devices with their start and end apart: 58 -> 70, of which waited for: 21 -> 19; matrix products, arithmetic and copies ran while one was open for 18% -> 12% of each run, Pallas kernels for 10% -> 25%
where the time goes in v2:
time: 584 us; the launch traced here: 578 us
  waiting for transfers between devices  231 us (40%)
  Pallas kernels  143 us (24%)
  starting transfers between devices  85.4 us (15%)
  local copies, waits for them, and re-layouts  50.5 us (9%)
  other arithmetic  37.8 us (6%)
  between operations  16.8 us (3%)
  matrix products  13 us (2%)
    ppermute x32, waiting for transfers between devices, hop(): lax.ppermute(value, 'fsdp', [(i, i ^ distance) for i in range(count)])  175 us
    all_to_all x6, waiting for transfers between devices, exchange(): return lax.all_to_all(value, 'fsdp', 0, 0, axis_index_groups=groups)  46.9 us
    pallas_call x1, Pallas kernels, attention_backward(): pl.pallas_call(functools.partial(backward_kernel, cubes), grid=(SPANS,),...  43.5 us
    ppermute x32, starting transfers between devices, hop(): lax.ppermute(value, 'fsdp', [(i, i ^ distance) for i in range(count)])  33.8 us
    pallas_call x2, Pallas kernels, feed(): pl.pallas_call(functools.partial(feed_kernel, pairs), in_specs=[vmem] * (...  33.6 us
    all_to_all x6, starting transfers between devices, exchange(): return lax.all_to_all(value, 'fsdp', 0, 0, axis_index_groups=groups)  24.4 us
    unnamed x167, local copies, waits for them, and re-layouts  24 us
    pallas_call x1, Pallas kernels, attention_forward(): pl.pallas_call(forward_kernel, grid=(SPANS,), in_specs=[pl.BlockSpec((HEA...  23.4 us
  transfers between devices with their start and end apart: 70, of which 19 were waited for; matrix products, arithmetic and copies ran while one was open for 12% of the time, Pallas kernels for 25%

profile of v2, /device:TPU:1, one launch (start us, length us, event | category | flops | bytes accessed | tf_op | source)
XLA Modules:
  0.0 577.7 jit_solution(6405014406433467926)
XLA Ops:
  9.9 5.4 all-to-all-start
  26.5 7.0 %collective-permute-done.1.refs_2_ = bf16[256,1536]{1,0:T(8,128)(2,1)} collective-permute-done((bf16[256,1536]{1,0:T(8,128)(2,1)S(1)}, bf16[256,1536]{1,0:T(8,128)(2,1)}, u32[]{:S(2)}, u32[]{:S(2)}) %collective-permute-start.1) | collective-permute-done | bytes 786464 | tf_op jit(solution)/shard_map/ppermute | solution.py:35
  34.5 9.0 %collective-permute-done.3.refs_8_ = bf16[256,1536]{1,0:T(8,128)(2,1)} collective-permute-done((bf16[256,1536]{1,0:T(8,128)(2,1)S(1)}, bf16[256,1536]{1,0:T(8,128)(2,1)}, u32[]{:S(2)}, u32[]{:S(2)}) %collective-permute-start.3) | collective-permute-done | bytes 786464 | tf_op jit(solution)/shard_map/ppermute | solution.py:35
  45.4 5.4 all-to-all-start.1
  56.2 36.9 %collective-permute-done.9 = bf16[4,96,768]{2,1,0:T(8,128)(2,1)S(1)} collective-permute-done((bf16[4,96,768]{2,1,0:T(8,128)(2,1)}, bf16[4,96,768]{2,1,0:T(8,128)(2,1)S(1)}, u32[]{:S(2)}, u32[]{:S(2)}) %collective-permute-start.9) | collective-permute-done | bytes 589856 | tf_op jit(solution)/shard_map/ppermute | solution.py:35
  108.9 17.8 %collective-permute-done.18 = bf16[4,96,768]{2,1,0:T(8,128)(2,1)} collective-permute-done((bf16[4,96,768]{2,1,0:T(8,128)(2,1)}, bf16[4,96,768]{2,1,0:T(8,128)(2,1)}, u32[]{:S(2)}, u32[]{:S(2)}) %collective-permute-start.18) | collective-permute-done | bytes 589856 | tf_op jit(solution)/shard_map/ppermute | solution.py:35
  126.7 4.1 collective-permute-start.4
  145.3 18.5 %project.1 = (bf16[8,512,1536]{2,1,0:T(8,128)(2,1)}, f32[8,1536]{1,0:T(8,128)}, bf16[96,4096]{1,0:T(8,128)(2,1)}, bf16[96,4096]{1,0:T(8,128)(2,1)}, bf16[96,4096...) custom-call(bf16[256,1536]{1,0:T(8,128)(2,1)} %refs_0_.1, ...), custom_call_target="tpu_custom_call" | custom-call | flops 3623878656 | bytes 25165824 | tf_op jit(solution)/shard_map/project/pallas_call | solution.py:114
  168.3 23.4 %attention_forward.1 = (bf16[8,96,512]{2,1,0:T(8,128)(2,1)}, f32[96,4096]{1,0:T(8,128)S(1)}, f32[1,4096]{1,0:T(1,128)S(1)}) custom-call(bf16[96,4096]{1,0:T(8,128)(2,1)S(1)} %copy-done.20, bf16[4096,96]{1,0:T(8,128)(2,1)S(1)} %copy-done.18, bf16[96,4096]{1,0:T(8,128)(2,1)S(1)} %copy-done.33, s32[1,4096]{1,0:T(1,128)S(1)} %bitcast.107, ...), custom_call_target="tpu_custom_call" | custom-call | flops 38654705664 | bytes 8388608 | tf_op jit(solution)/shard_map/attention_forward/pallas_call | solution.py:186
  200.4 34.0 %all-to-all-done.3 = bf16[8,96,512]{2,1,0:T(8,128)(2,1)S(1)} async-done(((bf16[8,96,512]{2,1,0:T(8,128)(2,1)}), bf16[8,96,512]{2,1,0:T(8,128)(2,1)S(1)}, u32[]{:S(2)}, u32[]{:S(2)}) %all-to-all-start.3) | async-done | bytes 786464 | tf_op jit(solution)/shard_map/all_to_all | solution.py:49
  250.2 14.4 %collective-permute-done.27.refs_4_.refs_2_ = bf16[256,1536]{1,0:T(8,128)(2,1)S(1)} collective-permute-done((bf16[256,1536]{1,0:T(8,128)(2,1)S(1)}, bf16[256,1536]{1,0:T(8,128)(2,1)S(1)}, u32[]{:S(2)}, u32[]{:S(2)}) %collective-permute-start.27) | collective-permute-done | bytes 786464 | tf_op jit(solution)/shard_map/ppermute | solution.py:35
  270.2 24.0 %feed.2 = (f32[256,1536]{1,0:T(8,128)}, bf16[256,1536]{1,0:T(8,128)(2,1)}, f32[256,1536]{1,0:T(8,128)}, bf16[256,1536]{1,0:T(8,128)(2,1)S(1)}, bf16[512,1024]{1,...) custom-call(bf16[256,1536]{1,0:T(8,128)(2,1)} %copy-done.9, ...), custom_call_target="tpu_custom_call" | custom-call | flops 14495514624 | bytes 8388608 | tf_op jit(solution)/shard_map/feed/pallas_call | solution.py:424
  312.4 9.6 %feed.3 = (f32[256,1536]{1,0:T(8,128)}, bf16[256,1536]{1,0:T(8,128)(2,1)S(1)}, f32[256,1536]{1,0:T(8,128)}, bf16[256,1536]{1,0:T(8,128)(2,1)S(1)}, bf16[512,1024...) custom-call(bf16[256,1536]{1,0:T(8,128)(2,1)} %collective-permute-done.33.refs_0_.refs_6_, ...), custom_call_target="tpu_custom_call" | custom-call | flops 4831838208 | bytes 8388608 | tf_op jit(solution)/shard_map/feed/pallas_call | solution.py:424
  330.5 15.2 %unit_grads.1 = bf16[1536,1536]{1,0:T(8,128)(2,1)} custom-call(bf16[256,1536]{1,0:T(8,128)(2,1)S(1)} %copy-done.10, bf16[256,1536]{1,0:T(8,128)(2,1)S(1)} %copy-done.26, bf16[256,1536]{1,0:T(8,128)(2,1)S(1)} %copy-done.22, bf16[256,1536]{1,0:T(8,128)(2,1)S(1)} %copy-done.28, bf16[256,1536]{1,0:T(8,128)(2,1)S(1)} %copy-done.24, ...), custom_call_target="tpu_custom_call" | custom-call | flops 9663676416 | bytes 25165824 | tf_op jit(solution)/shard_map/unit_grads/pallas_call | solution.py:375
  345.7 10.5 %collective-permute-done.43 = bf16[256,1536]{1,0:T(8,128)(2,1)} collective-permute-done((bf16[256,1536]{1,0:T(8,128)(2,1)}, bf16[256,1536]{1,0:T(8,128)(2,1)}, u32[]{:S(2)}, u32[]{:S(2)}) %collective-permute-start.43) | collective-permute-done | bytes 786464 | tf_op jit(solution)/shard_map/ppermute | solution.py:35
  365.7 4.4 convolution_convert_fusion.1
  379.6 12.9 %all-to-all-done.4.dout_ref = bf16[8,96,512]{2,1,0:T(8,128)(2,1)S(1)} async-done(((bf16[8,96,512]{2,1,0:T(8,128)(2,1)}), bf16[8,96,512]{2,1,0:T(8,128)(2,1)S(1)}, u32[]{:S(2)}, u32[]{:S(2)}) %all-to-all-start.4) | async-done | bytes 786464 | tf_op jit(solution)/shard_map/all_to_all | solution.py:49
  393.4 4.5 all-to-all-start.5
  401.2 43.5 %attention_backward.1 = bf16[8,288,704]{2,1,0:T(8,128)(2,1)} custom-call(bf16[96,4096]{1,0:T(8,128)(2,1)} %get-tuple-element.159.q_t_ref, bf16[4096,96]{1,0:T(8,128)(2,1)} %get-tuple-element.194.q_ref, bf16[96,4096]{1,0:T(8,128)(2,1)} %get-tuple-element.195.k_t_ref, bf16[4096,96]{1,0:T(8,128)(2,1)} %get-tuple-element.160.k_ref, ...), custom_call_target="tpu_custom_call" | custom-call | flops 96636764160 | bytes 12582912 | tf_op jit(solution)/shard_map/attention_backward/pallas_call | solution.py:278
  455.9 59.7 %collective-permute-done.49 = bf16[96,768]{1,0:T(8,128)(2,1)} collective-permute-done((bf16[96,768]{1,0:T(8,128)(2,1)}, bf16[96,768]{1,0:T(8,128)(2,1)}, u32[]{:S(2)}, u32[]{:S(2)}) %collective-permute-start.49) | collective-permute-done | bytes 147488 | tf_op jit(solution)/shard_map/ppermute | solution.py:35
  515.6 4.4 collective-permute-done.51
  531.0 4.4 input_terms.1
  543.5 12.0 %collective-permute-done.55.refs_1_ = bf16[1536,96]{1,0:T(8,128)(2,1)} collective-permute-done((bf16[1536,96]{1,0:T(8,128)(2,1)}, bf16[1536,96]{1,0:T(8,128)(2,1)}, u32[]{:S(2)}, u32[]{:S(2)}) %collective-permute-start.55) | collective-permute-done | bytes 294944 | tf_op jit(solution)/shard_map/ppermute | solution.py:35
  560.6 4.3 add_convert_fusion
  (372 shorter events, 175.7 us)
Async XLA Ops:
  9.9 33.5 %all-to-all-start = ((bf16[4,96,768]{2,1,0:T(8,128)(2,1)}), bf16[4,96,768]{2,1,0:T(8,128)(2,1)S(1)}, u32[]{:S(2)}, u32[]{:S(2)}) async-start(bf16[4,96,768]{2,1,0:T(8,128)(2,1)} %broadcast_in_dim.79), calls=%async_computation | async-start | bytes 1179648 | tf_op jit(solution)/shard_map/all_to_all | solution.py:555
  45.4 50.3 %all-to-all-start.1 = ((bf16[16,96,290]{2,1,0:T(8,128)(2,1)}), bf16[16,96,290]{2,1,0:T(8,128)(2,1)S(1)}, u32[]{:S(2)}, u32[]{:S(2)}) async-start(bf16[16,96,290]{2,1,0:T(8,128)(2,1)} %bitcast.7), calls=%async_computation.1 | async-start | bytes 2359296 | tf_op jit(solution)/shard_map/all_to_all | solution.py:49
  50.8 44.2 %collective-permute-start.6 = (bf16[256,1536]{1,0:T(8,128)(2,1)}, bf16[256,1536]{1,0:T(8,128)(2,1)}, u32[]{:S(2)}, u32[]{:S(2)}) collective-permute-start(bf16[256,1536]{1,0:T(8,128)(2,1)} %collective-permute-done.2.refs_4_), channel_id=1, source_target_pairs={{0,2},{2,0},{4,6},{6,4},{8,10},{10,8},{12,14},{14,12},{16,18},{18,... | collective-permute-start | bytes 2359304 | tf_op jit(solution)/shard_map/ppermute | solution.py:35
  52.1 42.8 %collective-permute-start.7 = (bf16[256,1536]{1,0:T(8,128)(2,1)}, bf16[256,1536]{1,0:T(8,128)(2,1)}, u32[]{:S(2)}, u32[]{:S(2)}) collective-permute-start(bf16[256,1536]{1,0:T(8,128)(2,1)} %collective-permute-done.3.refs_8_), channel_id=1, source_target_pairs={{0,4},{2,6},{4,0},{6,2},{8,12},{10,14},{12,8},{14,10},{16,20},{18,... | collective-permute-start | bytes 2359304 | tf_op jit(solution)/shard_map/ppermute | solution.py:35
  53.3 42.4 %collective-permute-start.8 = (bf16[256,1536]{1,0:T(8,128)(2,1)}, bf16[256,1536]{1,0:T(8,128)(2,1)}, u32[]{:S(2)}, u32[]{:S(2)}) collective-permute-start(bf16[256,1536]{1,0:T(8,128)(2,1)} %collective-permute-done.1.refs_2_), channel_id=1, source_target_pairs={{0,8},{2,10},{4,12},{6,14},{8,0},{10,2},{12,4},{14,6},{16,24},{18,... | collective-permute-start | bytes 2359304 | tf_op jit(solution)/shard_map/ppermute | solution.py:35
  54.5 38.6 %collective-permute-start.9 = (bf16[4,96,768]{2,1,0:T(8,128)(2,1)}, bf16[4,96,768]{2,1,0:T(8,128)(2,1)S(1)}, u32[]{:S(2)}, u32[]{:S(2)}) collective-permute-start(bf16[4,96,768]{2,1,0:T(8,128)(2,1)} %copy-done.56), channel_id=1, source_target_pairs={{0,2},{2,0},{4,6},{6,4},{8,10},{10,8},{12,14},{14,12},{16,18},{18,... | collective-permute-start | bytes 1769480 | tf_op jit(solution)/shard_map/ppermute | solution.py:35
  54.8 40.1 %collective-permute-start.10 = (bf16[4,96,768]{2,1,0:T(8,128)(2,1)}, bf16[4,96,768]{2,1,0:T(8,128)(2,1)S(1)}, u32[]{:S(2)}, u32[]{:S(2)}) collective-permute-start(bf16[4,96,768]{2,1,0:T(8,128)(2,1)} %copy-done.56), channel_id=1, source_target_pairs={{0,4},{2,6},{4,0},{6,2},{8,12},{10,14},{12,8},{14,10},{16,20},{18,... | collective-permute-start | bytes 1769480 | tf_op jit(solution)/shard_map/ppermute | solution.py:35
  95.7 38.5 %all-to-all-start.2 = ((bf16[4,96,1536]{2,1,0:T(8,128)(2,1)}), bf16[4,96,1536]{2,1,0:T(8,128)(2,1)S(1)}, u32[]{:S(2)}, u32[]{:S(2)}) async-start(bf16[4,96,1536]{2,1,0:T(8,128)(2,1)} %pad_maximum_fusion), calls=%async_computation.2 | async-start | bytes 2359296 | tf_op jit(solution)/shard_map/all_to_all | solution.py:49
  99.3 170.8 %all-gather.3.cloned.1.call-start = ((), (), s32[]{:S(2)}) async-start(), calls=%async_computation.8 | async-start | bytes 5898240 | tf_op jit(solution)/shard_map/all_gather | solution.py:576
  101.6 34.9 %collective-permute-start = (bf16[256,1536]{1,0:T(8,128)(2,1)S(1)}, bf16[256,1536]{1,0:T(8,128)(2,1)}, u32[]{:S(2)}, u32[]{:S(2)}) collective-permute-start(bf16[256,1536]{1,0:T(8,128)(2,1)S(1)} %copy-done.45), channel_id=1, source_target_pairs={{0,1},{1,0},{2,3},{3,2},{4,5},{5,4},{6,7},{7,6},{8,9},{9,8},{10,11... | collective-permute-start | bytes 2359304 | tf_op jit(solution)/shard_map/ppermute | solution.py:39
  193.6 40.8 %all-to-all-start.3 = ((bf16[8,96,512]{2,1,0:T(8,128)(2,1)}), bf16[8,96,512]{2,1,0:T(8,128)(2,1)S(1)}, u32[]{:S(2)}, u32[]{:S(2)}) async-start(bf16[8,96,512]{2,1,0:T(8,128)(2,1)} %get-tuple-element.165), calls=%async_computation.3 | async-start | bytes 1572864 | tf_op jit(solution)/shard_map/all_to_all | solution.py:49
  197.2 322.9 %all-gather.5.cloned.1.call-start = ((), (), s32[]{:S(2)}) async-start(), calls=%async_computation.10 | async-start | bytes 5013504 | tf_op jit(solution)/shard_map/all_gather | solution.py:613
  267.0 31.4 %collective-permute-start.33 = (bf16[256,1536]{1,0:T(8,128)(2,1)S(1)}, bf16[256,1536]{1,0:T(8,128)(2,1)}, u32[]{:S(2)}, u32[]{:S(2)}) collective-permute-start(bf16[256,1536]{1,0:T(8,128)(2,1)S(1)} %multiply_convert_fusion.refs_0_), channel_id=1, source_target_pairs={{0,6},{2,4},{4,2},{6,0},{8,14},{10,12},{12,10},{14,8},{16,22},{18,... | collective-permute-start | bytes 2359304 | tf_op jit(solution)/shard_map/ppermute | solution.py:35
  308.2 37.5 %collective-permute-start.39 = (bf16[256,1536]{1,0:T(8,128)(2,1)}, bf16[256,1536]{1,0:T(8,128)(2,1)}, u32[]{:S(2)}, u32[]{:S(2)}) collective-permute-start(bf16[256,1536]{1,0:T(8,128)(2,1)} %add_convert_fusion.6), channel_id=1, source_target_pairs={{0,2},{2,0},{4,6},{6,4},{8,10},{10,8},{12,14},{14,12},{16,18},{18,... | collective-permute-start | bytes 2359304 | tf_op jit(solution)/shard_map/ppermute | solution.py:35
  311.2 34.6 %collective-permute-start.40 = (bf16[256,1536]{1,0:T(8,128)(2,1)}, bf16[256,1536]{1,0:T(8,128)(2,1)}, u32[]{:S(2)}, u32[]{:S(2)}) collective-permute-start(bf16[256,1536]{1,0:T(8,128)(2,1)} %add_convert_fusion.5), channel_id=1, source_target_pairs={{0,4},{2,6},{4,0},{6,2},{8,12},{10,14},{12,8},{14,10},{16,20},{18,... | collective-permute-start | bytes 2359304 | tf_op jit(solution)/shard_map/ppermute | solution.py:35
  328.1 28.1 %collective-permute-start.43 = (bf16[256,1536]{1,0:T(8,128)(2,1)}, bf16[256,1536]{1,0:T(8,128)(2,1)}, u32[]{:S(2)}, u32[]{:S(2)}) collective-permute-start(bf16[256,1536]{1,0:T(8,128)(2,1)} %add_convert_fusion.4), channel_id=1, source_target_pairs={{0,6},{2,4},{4,2},{6,0},{8,14},{10,12},{12,10},{14,8},{16,22},{18,... | collective-permute-start | bytes 2359304 | tf_op jit(solution)/shard_map/ppermute | solution.py:35
  373.9 146.1 %reduce-scatter.2.cloned.1.call-start = ((), (), s32[]{:S(2)}) async-start(), calls=%async_computation.9 | async-start | bytes 5898240 | tf_op jit(solution)/shard_map/reduce_scatter | solution.py:631
  393.4 51.2 %all-to-all-start.5 = ((bf16[4,384,768]{2,1,0:T(8,128)(2,1)}), bf16[4,384,768]{2,1,0:T(8,128)(2,1)}, u32[]{:S(2)}, u32[]{:S(2)}) async-start(bf16[4,384,768]{2,1,0:T(8,128)(2,1)} %bitcast.34), calls=%async_computation.5 | async-start | bytes 4718592 | tf_op jit(solution)/shard_map/all_to_all | solution.py:49
  397.9 46.7 %collective-permute-start.48 = (bf16[256,1536]{1,0:T(8,128)(2,1)S(1)}, bf16[256,1536]{1,0:T(8,128)(2,1)}, u32[]{:S(2)}, u32[]{:S(2)}) collective-permute-start(bf16[256,1536]{1,0:T(8,128)(2,1)S(1)} %copy-done.66), channel_id=1, source_target_pairs={{0,6},{2,4},{4,2},{6,0},{8,14},{10,12},{12,10},{14,8},{16,22},{18,... | collective-permute-start | bytes 2359304 | tf_op jit(solution)/shard_map/ppermute | solution.py:35
  444.7 75.4 %all-to-all-start.6 = ((bf16[8,288,704]{2,1,0:T(8,128)(2,1)}), bf16[8,288,704]{2,1,0:T(8,128)(2,1)S(1)}, u32[]{:S(2)}, u32[]{:S(2)}) async-start(bf16[8,288,704]{2,1,0:T(8,128)(2,1)} %attention_backward.1), calls=%async_computation.6 | async-start | bytes 7077888 | tf_op jit(solution)/shard_map/all_to_all | solution.py:49
  452.3 63.3 %collective-permute-start.49 = (bf16[96,768]{1,0:T(8,128)(2,1)}, bf16[96,768]{1,0:T(8,128)(2,1)}, u32[]{:S(2)}, u32[]{:S(2)}) collective-permute-start(bf16[96,768]{1,0:T(8,128)(2,1)} %get-tuple-element.309), channel_id=1, source_target_pairs={{0,8},{2,10},{4,12},{6,14},{8,0},{10,2},{12,4},{14,6},{16,24},{18,... | collective-permute-start | bytes 442376 | tf_op jit(solution)/shard_map/ppermute | solution.py:35
  453.7 61.9 %collective-permute-start.50 = (bf16[96,768]{1,0:T(8,128)(2,1)}, bf16[96,768]{1,0:T(8,128)(2,1)}, u32[]{:S(2)}, u32[]{:S(2)}) collective-permute-start(bf16[96,768]{1,0:T(8,128)(2,1)} %get-tuple-element.308), channel_id=1, source_target_pairs={{0,16},{2,18},{4,20},{6,22},{8,24},{10,26},{12,28},{14,30},{16,0},... | collective-permute-start | bytes 442376 | tf_op jit(solution)/shard_map/ppermute | solution.py:35
  453.7 66.3 %collective-permute-start.51 = (bf16[96,768]{1,0:T(8,128)(2,1)}, bf16[96,768]{1,0:T(8,128)(2,1)}, u32[]{:S(2)}, u32[]{:S(2)}) collective-permute-start(bf16[96,768]{1,0:T(8,128)(2,1)} %get-tuple-element.307), channel_id=1, source_target_pairs={{0,24},{2,26},{4,28},{6,30},{8,16},{10,18},{12,20},{14,22},{16,8},... | collective-permute-start | bytes 442376 | tf_op jit(solution)/shard_map/ppermute | solution.py:35
  536.2 28.7 %collective-permute-start.54 = (f32[256,1536]{1,0:T(8,128)}, f32[256,1536]{1,0:T(8,128)}, u32[]{:S(2)}, u32[]{:S(2)}) collective-permute-start(f32[256,1536]{1,0:T(8,128)} %get-tuple-element.259), channel_id=1, source_target_pairs={{0,1},{1,0},{2,3},{3,2},{4,5},{5,4},{6,7},{7,6},{8,9},{9,8},{10,11... | collective-permute-start | bytes 4718600 | tf_op jit(solution)/shard_map/ppermute | solution.py:39
  (128 other events, 1239.7 us)
Sparse Core Ops, SparseCore 0:
  144.5 95.1 all-gather.2
  377.0 114.1 reduce-scatter.1
Sparse Core Ops, SparseCore 1:
  300.7 115.6 all-gather.4

commit v3 on v2

--- a/solution.py
+++ b/solution.py
@@ -21,6 +21,7 @@
 scale = HEAD_SIZE ** (-0.5)
 scale_log2 = scale * math.log2(math.e)
 bf16 = jnp.bfloat16
+brief = pl.CostEstimate(flops=1024, bytes_accessed=1024, transcendentals=0)
 f32 = jnp.float32
 
 
@@ -128,11 +129,7 @@
             pltpu.SemaphoreType.DMA((2,)),
         ],
         compiler_params=pltpu.CompilerParams(vmem_limit_bytes=56 * 2**20),
-        cost_estimate=pl.CostEstimate(
-            flops=2 * tokens * width * 3 * HEAD_SIZE,
-            bytes_accessed=4 * tokens * width,
-            transcendentals=0,
-        ),
+        cost_estimate=brief,
         name="project",
     )(*pieces, places, head_set, cosine, sine)
 
@@ -204,9 +201,7 @@
             jax.ShapeDtypeStruct((1, tokens), f32),
         ],
         compiler_params=pltpu.CompilerParams(vmem_limit_bytes=40 * 2**20),
-        cost_estimate=pl.CostEstimate(
-            flops=36 * SPAN * SPAN * 256 * 4 * 4, bytes_accessed=8 * 2**20, transcendentals=36 * SPAN * SPAN
-        ),
+        cost_estimate=brief,
         name="attention_forward",
     )(q_t, k, v_t, id_row, id_col)
 
@@ -292,9 +287,7 @@
             pltpu.VMEM((3 * HEAD_SIZE, width), f32),
         ],
         compiler_params=pltpu.CompilerParams(vmem_limit_bytes=56 * 2**20),
-        cost_estimate=pl.CostEstimate(
-            flops=36 * SPAN * SPAN * 256 * 10 * 4, bytes_accessed=12 * 2**20, transcendentals=36 * SPAN * SPAN
-        ),
+        cost_estimate=brief,
         name="attention_backward",
     )(q_t, q, k_t, k, v, dout, out, lse, id_row, id_col, cosine, sine, normed)
 
@@ -379,9 +372,7 @@
         out_specs=pl.BlockSpec((rows, columns), lambda i: (i, 0)),
         out_shape=jax.ShapeDtypeStruct((width, columns), bf16),
         compiler_params=pltpu.CompilerParams(vmem_limit_bytes=48 * 2**20),
-        cost_estimate=pl.CostEstimate(
-            flops=2 * 2 * tokens * PLANE * width * columns, bytes_accessed=24 * 2**20, transcendentals=0
-        ),
+        cost_estimate=brief,
         name="unit_grads",
     )(*normed, *dgate_up, *dout, *act)
 
@@ -427,9 +418,7 @@
         out_specs=[vmem] * len(shapes),
         out_shape=shapes,
         compiler_params=pltpu.CompilerParams(vmem_limit_bytes=48 * 2**20),
-        cost_estimate=pl.CostEstimate(
-            flops=pairs * 2 * 2 * rows * width * units * 6, bytes_accessed=8 * 2**20, transcendentals=2 * rows * units
-        ),
+        cost_estimate=brief,
         name="feed",
     )(*ins, weight)
     return [outs[6 * pair:6 * pair + 6] for pair in range(pairs)]
@@ -475,10 +464,8 @@
         out_shape=[jax.ShapeDtypeStruct((rows, width), f32)] * 2
         + [jax.ShapeDtypeStruct((cubes, features, shard), bf16)],
         scratch_shapes=[pltpu.VMEM((features, SPAN), bf16)],
-        compiler_params=pltpu.CompilerParams(vmem_limit_bytes=40 * 2**20),
-        cost_estimate=pl.CostEstimate(
-            flops=4 * width * features * rows, bytes_accessed=12 * 2**20, transcendentals=0
-        ),
+        compiler_params=pltpu.CompilerParams(vmem_limit_bytes=56 * 2**20),
+        cost_estimate=brief,
         name="input_terms",
     )(core, back, weight)
 
@@ -551,34 +538,17 @@
         axis=-1,
     )
     lines = [list(range(first, count, PLANE)) for first in range(PLANE)]
+    lines = [list(range(first, count, PLANE)) for first in range(PLANE)]
     p1, p2, p4 = hop(hidden, 1), hop(hidden, 2), hop(hidden, 4)
-    out_0 = lax.all_to_all(
-        jnp.broadcast_to(out_weight, (planes,) + out_weight.shape[1:]), "fsdp", 0, 0, axis_index_groups=lines
-    )
-    sent, unit_set, p1, p2, p4, out_0 = tie((sent, unit_set, p1, p2, p4, out_0))
-    p3, p6, p5 = hop(p2, 1), hop(p4, 2), hop(p1, 4)
-    out_1, out_2 = hop(out_0, 1), hop(out_0, 2)
     head_set = exchange(sent, count).reshape(width, -1)
-
-    own_ids = lax.dynamic_slice_in_dim(document_index, f * SPAN + t * own, own)
-    dstream = cotangent.astype(f32) * (own_ids != 0).astype(f32)[:, None]
-    dmlp_own = dstream.astype(bf16)
-    unit_set, head_set, p3, p6, p5, dmlp_own, out_1, out_2 = tie(
-        (unit_set, head_set, p3, p6, p5, dmlp_own, out_1, out_2)
-    )
-    cut_a, cut_b = own // 128 * 48, own // 128 * 88
-    p7 = [hop(p6[:cut_a], 1), hop(p5[cut_a:cut_b], 2), hop(p3[cut_b:], 4)]
-    out_3 = hop(out_0, 3)
+    out_far = [hop(out_weight[0], PLANE * k) for k in range(1, planes)]
+    p4, document_index, cotangent = tie((p4, document_index, cotangent))
+    p5, p6 = hop(p4, 1), hop(p4, 2)
+    p3 = [hop(p2[:half], 1), hop(p1[half:], 2)]
+    p7 = [hop(p6[:half], 1), hop(p5[half:], 2)]
+    p3, p7 = jnp.concatenate(p3, axis=0), jnp.concatenate(p7, axis=0)
+    unit_set, head_set = tie((unit_set, head_set))
     unit_own = exchange(unit_set, PLANE).reshape(PLANE * shard, 3 * units)
-    dmlp_own, p7, unit_own, out_3 = tie((dmlp_own, p7, unit_own, out_3))
-    pieces = with_swapped([hidden, p1, p2, p3, p4, p5, p6, jnp.concatenate(p7, axis=0)])
-    dmlp_1, dmlp_2 = hop(dmlp_own, 1), hop(dmlp_own, 2)
-    unit_weight = lax.all_gather(unit_own, "fsdp", axis=0, tiled=True, axis_index_groups=lines)
-    out_part = jnp.zeros((planes, PLANE, shard, out_0.shape[2]), bf16)
-    for k, piece in enumerate((out_0, out_1, out_2, out_3)):
-        out_part = lax.dynamic_update_slice_in_dim(out_part, piece[:, None], plane_place ^ k, 1)
-    out_part = out_part.reshape(width, -1)
-    in_shard = jnp.concatenate([q_weight[0], key_matrix[0], value_matrix[0]], axis=1)
 
     seq_ids = lax.dynamic_slice_in_dim(document_index, f // SPANS * PACKED_LENGTH, PACKED_LENGTH)
     seq_index = jnp.arange(PACKED_LENGTH, dtype=jnp.int32)
@@ -590,16 +560,39 @@
     cosine, sine = jnp.cos(angle), jnp.sin(angle)
     id_row = seq_ids[None, :]
     id_col = jnp.broadcast_to(seq_ids[:, None], (PACKED_LENGTH, 128))
+
+    own_ids = lax.dynamic_slice_in_dim(document_index, f * SPAN + t * own, own)
+    dstream = cotangent.astype(f32) * (own_ids != 0).astype(f32)[:, None]
+    dmlp_own = dstream.astype(bf16)
+    head_set, dmlp_own, cosine, sine, id_col, p3, out_far = tie(
+        (head_set, dmlp_own, cosine, sine, id_col, p3, out_far)
+    )
+    pieces = with_swapped([hidden, p1, p2, p3, p4, p5, p6, p7])
+    out_0 = jnp.zeros((planes,) + out_weight.shape[1:], bf16)
+    for k, piece in enumerate([out_weight[0]] + out_far):
+        out_0 = lax.dynamic_update_slice_in_dim(out_0, piece[None], plane_at ^ k, 0)
+    out_1, out_2 = hop(out_0, 1), hop(out_0, 2)
+    in_shard = jnp.concatenate([q_weight[0], key_matrix[0], value_matrix[0]], axis=1)
+
     places = jnp.stack([place, t]).astype(jnp.int32)
 
     normed, gains, q_t, k_t, v_t, q, key, v = project(pieces, head_set, places, cosine, sine)
     gain_a, gain_m = gains[0:1], gains[1:2]
-    q_t, dmlp_1, dmlp_2 = tie((q_t, dmlp_1, dmlp_2))
-    dmlp_3 = [hop(dmlp_2[:half], 1), hop(dmlp_1[half:], 2)]
+    q_t, out_0, out_1, out_2, dmlp_own, unit_own = tie((q_t, out_0, out_1, out_2, dmlp_own, unit_own))
+    unit_weight = lax.all_gather(unit_own, "fsdp", axis=0, tiled=True, axis_index_groups=lines)
+    out_3 = hop(out_0, 3)
+    dmlp_1, dmlp_2 = hop(dmlp_own, 1), hop(dmlp_own, 2)
     out_t, out_full, lse = attention_forward(q_t, key, v_t, id_row, id_col)
-    out_t, dmlp_3 = tie((out_t, dmlp_3))
-    dmlp = with_swapped([dmlp_own, dmlp_1, dmlp_2, jnp.concatenate(dmlp_3, axis=0)])
-    attended = exchange(out_t, SPANS).reshape(q_heads * HEAD_SIZE, SPAN)
+    out_t, dmlp_1, dmlp_2, out_3, dmlp_late = tie((out_t, dmlp_1, dmlp_2, out_3, dmlp_own))
+    dmlp_3 = hop(dmlp_late, 3)
+    attended = exchange(out_t, SPANS)
+    attended, dmlp_3, in_shard = tie((attended, dmlp_3, in_shard))
+    in_part = lax.all_gather(in_shard, "fsdp", axis=0, tiled=True)
+    attended = attended.reshape(q_heads * HEAD_SIZE, SPAN)
+    out_part = jnp.zeros((planes, PLANE, shard, out_0.shape[2]), bf16)
+    for k, piece in enumerate((out_0, out_1, out_2, out_3)):
+        out_part = lax.dynamic_update_slice_in_dim(out_part, piece[:, None], plane_place ^ k, 1)
+    out_part = out_part.reshape(width, -1)
 
     stream = hidden.astype(f32)
     mine = lax.dynamic_slice_in_dim(attended, t * own, own, 1)
@@ -608,27 +601,27 @@
 
     factor_m = rms_factor(mid)
     normed_own = (mid * factor_m * gain_m).astype(bf16)
+    dmlp = with_swapped([dmlp_own, dmlp_1, dmlp_2, dmlp_3])
     n1, n2 = hop(normed_own, 1), hop(normed_own, 2)
-    n1, n2, normed_late, in_shard = tie((n1, n2, normed_own, in_shard))
-    in_part = lax.all_gather(in_shard, "fsdp", axis=0, tiled=True)
+    n1, n2, normed_late = tie((n1, n2, normed_own))
     n3 = hop(normed_late, 3)
     normed_m = with_swapped([normed_own, n1, n2])
-    results = feed([normed_m[2 * k:2 * k + 2] + dmlp[2 * k:2 * k + 2] for k in range(3)], unit_weight)
-    results, n3 = tie((results, n3))
-    n3 = with_swapped([n3])
-    dn_got = [swap(result[1]) for result in results]
-    n3, dn_got = tie((n3, dn_got))
-    normed_m += n3
-    results += feed([n3 + dmlp[6:8]], unit_weight)
-    dn_last, acts = tie((swap(results[3][1]), [result[5] for result in results]))
-    dn_got += [dn_last]
+    second, third = feed([normed_m[2 * k:2 * k + 2] + dmlp[2 * k:2 * k + 2] for k in (1, 2)], unit_weight)
+    second, third, n3 = tie((second, third, n3))
+    normed_m += with_swapped([n3])
+    dn_got = [swap(second[1]), swap(third[1])]
+    first, fourth = feed([normed_m[2 * k:2 * k + 2] + dmlp[2 * k:2 * k + 2] for k in (0, 3)], unit_weight)
+    first, fourth, dn_got = tie((first, fourth, dn_got))
+    results = [first, second, third, fourth]
+    dn_got = [swap(first[1])] + dn_got + [swap(fourth[1])]
     dn_pair = [result[0] + got.astype(f32) for result, got in zip(results, dn_got)]
     dn_far = [dn_pair[0]] + [hop(dn_pair[k].astype(bf16), k) for k in range(1, PLANE)]
     out_pair = [result[2] + swap(result[3]).astype(f32) for result in results]
     out_low = [out_pair[k].astype(bf16) for k in range(1, PLANE)]
-    unit_term = unit_grads(normed_m, [result[4] for result in results], dmlp, acts)
-    dn_far, out_low, unit_term = tie((dn_far, out_low, unit_term))
+    unit_term = unit_grads(normed_m, [result[4] for result in results], dmlp, [result[5] for result in results])
+    dn_far, out_low, in_part, unit_term = tie((dn_far, out_low, in_part, unit_term))
     unit_sum = lax.psum_scatter(unit_term, "fsdp", scatter_dimension=0, tiled=True, axis_index_groups=lines)
+    out_far = [hop(low, k) for k, low in enumerate(out_low[:2], 1)]
 
     dnormed_m = dn_far[0]
     for far in dn_far[1:]:
@@ -645,33 +638,33 @@
     dout = dot(out_part, dattn, 0, 1).astype(bf16)
     dout = exchange(dout.reshape(SPANS, HEAD_SIZE, SPAN), SPANS)
     out_term = dot(dattn, attended, 0, 1).astype(bf16).reshape(planes, PLANE, shard, -1).transpose(1, 0, 2, 3)
-    dout, out_term, out_low = tie((dout, out_term, out_low))
+    dout, out_term, out_low, out_far = tie((dout, out_term, out_low, out_far))
     out_term = exchange(out_term.reshape(PLANE, planes * shard, -1), PLANE)
-    out_far = [hop(out_low[2], 3)]
+    out_far += [hop(out_low[2], 3)]
     grads = attention_backward(
         q_t, q, k_t, key, v, dout, out_full, lse, id_row, id_col, cosine, sine, normed, cubes
     )
-    grads, out_term, out_far, out_low = tie((grads, out_term, out_far, out_low))
+    grads, out_term, out_far, unit_sum = tie((grads, out_term, out_far, unit_sum))
 
     back = exchange(grads, SPANS)
+    unit_sum = unit_sum.reshape(PLANE, shard, 3 * units)
+    unit_back = [lax.dynamic_index_in_dim(unit_sum, plane_place ^ k, 0, keepdims=False) for k in range(PLANE)]
+    unit_back = [piece if k == 0 else hop(piece, k) for k, piece in enumerate(unit_back)]
     out_term = out_term.astype(f32).sum(axis=0).reshape(planes, shard, -1)
     out_grad = lax.dynamic_index_in_dim(out_term, plane_at, 0, keepdims=False)
     out_sums = []
     for k in range(1, planes):
         far = lax.dynamic_index_in_dim(out_term, plane_at ^ k, 0, keepdims=False)
         out_sums.append(hop(far.astype(bf16), PLANE * k))
-    back, out_low, unit_sum, in_part, out_sums = tie((back, out_low, unit_sum, in_part, out_sums))
+    back, out_sums, unit_back = tie((back, out_sums, unit_back))
     for far in out_sums:
         out_grad = out_grad + far.astype(f32)
-    unit_sum = unit_sum.reshape(PLANE, shard, 3 * units)
-    unit_back = [lax.dynamic_index_in_dim(unit_sum, plane_place ^ k, 0, keepdims=False) for k in range(PLANE)]
-    unit_back = [piece if k == 0 else hop(piece, k) for k, piece in enumerate(unit_back)]
-    out_far += [hop(low, k) for k, low in enumerate(out_low[:2], 1)]
     mine, other, head_terms = input_terms(back, in_part, t.reshape(1).astype(jnp.int32), cubes)
     head_sums = [lax.dynamic_index_in_dim(head_terms, cube_at ^ k, 0, keepdims=False) for k in range(cubes)]
     head_sums = [piece if k == 0 else hop(piece, SPANS * k) for k, piece in enumerate(head_sums)]
     dnormed_a = mine + swap(other)
     input_grad = dmid + norm_backward(stream, rms_factor(stream), gain_a, dnormed_a)
+    input_grad, head_sums = tie((input_grad, head_sums))
 
     q_grad, k_grad, v_grad, gain_a_part = head_finish(head_sums, q_weight[0], key_matrix[0], value_matrix[0])
 

time: 584 us -> 537 us (0.920)
  waiting for transfers between devices: 231 us -> 189 us
  local copies, waits for them, and re-layouts: 50.5 us -> 44.1 us
    all_to_all x6, waiting for transfers between devices: 46.9 us -> 19.4 us  [exchange(): return lax.all_to_all(value, 'fsdp', 0, 0, axis_index_groups=groups)]
    ppermute x32 -> x34, waiting for transfers between devices: 175 us -> 161 us  [hop(): lax.ppermute(value, 'fsdp', [(i, i ^ distance) for i in range(count)])]
    unnamed x167 -> x131, local copies, waits for them, and re-layouts: 24 us -> 11.6 us
    ppermute x32 -> x34, starting transfers between devices: 33.8 us -> 33.9 us  [hop(): lax.ppermute(value, 'fsdp', [(i, i ^ distance) for i in range(count)])]
  transfers between devices with their start and end apart: 70 -> 71, of which waited for: 19 -> 21; matrix products, arithmetic and copies ran while one was open for 12% -> 17% of each run, Pallas kernels for 25% -> 27%
where the time goes in v3:
time: 537 us; the launch traced here: 528 us
  waiting for transfers between devices  189 us (35%)
  Pallas kernels  145 us (27%)
  starting transfers between devices  80.7 us (15%)
  local copies, waits for them, and re-layouts  44.1 us (8%)
  other arithmetic  41.5 us (8%)
  between operations  14.8 us (3%)
  matrix products  13.7 us (3%)
    ppermute x34, waiting for transfers between devices, hop(): lax.ppermute(value, 'fsdp', [(i, i ^ distance) for i in range(count)])  161 us
    pallas_call x1, Pallas kernels, attention_backward(): pl.pallas_call(functools.partial(backward_kernel, cubes), grid=(SPANS,),...  43.4 us
    ppermute x34, starting transfers between devices, hop(): lax.ppermute(value, 'fsdp', [(i, i ^ distance) for i in range(count)])  33.9 us
    pallas_call x2, Pallas kernels, feed(): pl.pallas_call(functools.partial(feed_kernel, pairs), in_specs=[vmem] * (...  33.8 us
    all_to_all x6, starting transfers between devices, exchange(): return lax.all_to_all(value, 'fsdp', 0, 0, axis_index_groups=groups)  23.7 us
    pallas_call x1, Pallas kernels, attention_forward(): pl.pallas_call(forward_kernel, grid=(SPANS,), in_specs=[pl.BlockSpec((HEA...  22.8 us
    ppermute x28, starting transfers between devices, swap(): return lax.ppermute(value, 'tp', [(0, 1), (1, 0)])  22.3 us
    all_to_all x6, waiting for transfers between devices, exchange(): return lax.all_to_all(value, 'fsdp', 0, 0, axis_index_groups=groups)  19.4 us
  transfers between devices with their start and end apart: 71, of which 21 were waited for; matrix products, arithmetic and copies ran while one was open for 17% of the time, Pallas kernels for 27%

profile of v3, /device:TPU:1, one launch (start us, length us, event | category | flops | bytes accessed | tf_op | source)
XLA Modules:
  0.0 528.2 jit_solution(12978667748721054985)
XLA Ops:
  17.7 3.8 all-to-all-start
  44.5 14.0 %collective-permute-done.15.refs_12_ = bf16[256,1536]{1,0:T(8,128)(2,1)} collective-permute-done((bf16[256,1536]{1,0:T(8,128)(2,1)}, bf16[256,1536]{1,0:T(8,128)(2,1)}, u32[]{:S(2)}, u32[]{:S(2)}) %collective-permute-start.15) | collective-permute-done | bytes 786464 | tf_op jit(solution)/shard_map/ppermute | solution.py:36
  65.0 6.6 %collective-permute-done.6 = bf16[128,1536]{1,0:T(8,128)(2,1)S(1)} collective-permute-done((bf16[128,1536]{1,0:T(8,128)(2,1)S(1)}, bf16[128,1536]{1,0:T(8,128)(2,1)S(1)}, u32[]{:S(2)}, u32[]{:S(2)}) %collective-permute-start.6) | collective-permute-done | bytes 393248 | tf_op jit(solution)/shard_map/ppermute | solution.py:36
  75.6 4.3 all-to-all-start.1
  93.3 18.4 %project.1 = (bf16[8,512,1536]{2,1,0:T(8,128)(2,1)}, f32[8,1536]{1,0:T(8,128)}, bf16[96,4096]{1,0:T(8,128)(2,1)}, bf16[96,4096]{1,0:T(8,128)(2,1)}, bf16[96,4096...) custom-call(bf16[256,1536]{1,0:T(8,128)(2,1)} %refs_0_.1, ...), custom_call_target="tpu_custom_call" | custom-call | flops 1024 | bytes 1024 | tf_op jit(solution)/shard_map/project/pallas_call | solution.py:115
  116.8 22.8 %attention_forward.1 = (bf16[8,96,512]{2,1,0:T(8,128)(2,1)S(1)}, f32[96,4096]{1,0:T(8,128)S(1)}, f32[1,4096]{1,0:T(1,128)S(1)}) custom-call(bf16[96,4096]{1,0:T(8,128)(2,1)S(1)} %copy-done.2, bf16[4096,96]{1,0:T(8,128)(2,1)S(1)} %copy-done.1, bf16[96,4096]{1,0:T(8,128)(2,1)S(1)} %copy-done.11, s32[1,4096]{1,0:T(1,128)S(1)} %bitcast.113, ...), custom_call_target="tpu_custom_call" | custom-call | flops 1024 | bytes 1024 | tf_op jit(solution)/shard_map/attention_forward/pallas_call | solution.py:183
  154.9 17.0 %collective-permute-done.25.refs_6_.refs_18_ = bf16[256,1536]{1,0:T(8,128)(2,1)} collective-permute-done((bf16[256,1536]{1,0:T(8,128)(2,1)}, bf16[256,1536]{1,0:T(8,128)(2,1)}, u32[]{:S(2)}, u32[]{:S(2)}) %collective-permute-start.25) | collective-permute-done | bytes 786464 | tf_op jit(solution)/shard_map/ppermute | solution.py:36
  171.9 18.7 %all-to-all-done.2 = bf16[8,96,512]{2,1,0:T(8,128)(2,1)S(1)} async-done(((bf16[8,96,512]{2,1,0:T(8,128)(2,1)}), bf16[8,96,512]{2,1,0:T(8,128)(2,1)S(1)}, u32[]{:S(2)}, u32[]{:S(2)}) %all-to-all-start.2) | async-done | bytes 786464 | tf_op jit(solution)/shard_map/all_to_all | solution.py:50
  207.5 17.2 %collective-permute-done.29.refs_0_.refs_2_ = bf16[256,1536]{1,0:T(8,128)(2,1)S(1)} collective-permute-done((bf16[256,1536]{1,0:T(8,128)(2,1)S(1)}, bf16[256,1536]{1,0:T(8,128)(2,1)S(1)}, u32[]{:S(2)}, u32[]{:S(2)}) %collective-permute-start.29) | collective-permute-done | bytes 786464 | tf_op jit(solution)/shard_map/ppermute | solution.py:36
  230.9 16.7 %feed.2 = (f32[256,1536]{1,0:T(8,128)}, bf16[256,1536]{1,0:T(8,128)(2,1)S(1)}, f32[256,1536]{1,0:T(8,128)}, bf16[256,1536]{1,0:T(8,128)(2,1)S(1)}, bf16[512,1024...) custom-call(bf16[256,1536]{1,0:T(8,128)(2,1)S(1)} %collective-permut, ...), custom_call_target="tpu_custom_call" | custom-call | flops 1024 | bytes 1024 | tf_op jit(solution)/shard_map/feed/pallas_call | solution.py:415
  247.6 5.6 %collective-permute-done.35.refs_4_.refs_6_ = bf16[256,1536]{1,0:T(8,128)(2,1)} collective-permute-done((bf16[256,1536]{1,0:T(8,128)(2,1)S(1)}, bf16[256,1536]{1,0:T(8,128)(2,1)}, u32[]{:S(2)}, u32[]{:S(2)}) %collective-permute-start.35) | collective-permute-done | bytes 786464 | tf_op jit(solution)/shard_map/ppermute | solution.py:36
  260.6 17.1 %feed.3 = (f32[256,1536]{1,0:T(8,128)}, bf16[256,1536]{1,0:T(8,128)(2,1)}, f32[256,1536]{1,0:T(8,128)}, bf16[256,1536]{1,0:T(8,128)(2,1)S(1)}, bf16[512,1024]{1,...) custom-call(bf16[256,1536]{1,0:T(8,128)(2,1)S(1)} %multiply_convert_, ...), custom_call_target="tpu_custom_call" | custom-call | flops 1024 | bytes 1024 | tf_op jit(solution)/shard_map/feed/pallas_call | solution.py:415
  286.5 15.1 %unit_grads.1 = bf16[1536,1536]{1,0:T(8,128)(2,1)} custom-call(bf16[256,1536]{1,0:T(8,128)(2,1)S(1)} %multiply_convert_fusion.refs_0_, bf16[256,1536]{1,0:T(8,128)(2,1)} %collective-permute-done.27.refs_1_, bf16[256,1536]{1,0:T(8,128)(2,1)S(1)} %collective-permute-done.29.refs_0_.refs_2_, bf16[256,1536]{1,0:T(8,128)(2,1)S(1)} %collective-permute-done.31.refs_1_.refs_3_, ...), custom_call_target="tpu_custom_call" | custom-call | flops 1024 | bytes 1024 | tf_op jit(solution)/shard_map/unit_grads/pallas_call | solution.py:368
  309.2 14.5 %collective-permute-done.45 = bf16[256,1536]{1,0:T(8,128)(2,1)S(1)} collective-permute-done((bf16[256,1536]{1,0:T(8,128)(2,1)S(1)}, bf16[256,1536]{1,0:T(8,128)(2,1)S(1)}, u32[]{:S(2)}, u32[]{:S(2)}) %collective-permute-start.45) | collective-permute-done | bytes 786464 | tf_op jit(solution)/shard_map/ppermute | solution.py:36
  333.4 4.7 convolution_convert_fusion.1
  338.1 3.9 all-to-all-start.3
  349.7 19.6 %collective-permute-done.50 = bf16[256,1536]{1,0:T(8,128)(2,1)S(1)} collective-permute-done((bf16[256,1536]{1,0:T(8,128)(2,1)}, bf16[256,1536]{1,0:T(8,128)(2,1)S(1)}, u32[]{:S(2)}, u32[]{:S(2)}) %collective-permute-start.50) | collective-permute-done | bytes 786464 | tf_op jit(solution)/shard_map/ppermute | solution.py:36
  377.8 43.4 %attention_backward.1 = bf16[8,288,704]{2,1,0:T(8,128)(2,1)} custom-call(bf16[96,4096]{1,0:T(8,128)(2,1)} %get-tuple-element.160.q_t_ref, bf16[4096,96]{1,0:T(8,128)(2,1)} %get-tuple-element.210.q_ref, bf16[96,4096]{1,0:T(8,128)(2,1)} %get-tuple-element.211.k_t_ref, bf16[4096,96]{1,0:T(8,128)(2,1)} %get-tuple-element.161.k_ref, ...), custom_call_target="tpu_custom_call" | custom-call | flops 1024 | bytes 1024 | tf_op jit(solution)/shard_map/attention_backward/pallas_call | solution.py:273
  421.2 4.5 all-to-all-start.5
  430.5 41.3 %collective-permute-done.53 = bf16[96,768]{1,0:T(8,128)(2,1)S(1)} collective-permute-done((bf16[96,768]{1,0:T(8,128)(2,1)S(1)}, bf16[96,768]{1,0:T(8,128)(2,1)S(1)}, u32[]{:S(2)}, u32[]{:S(2)}) %collective-permute-start.53) | collective-permute-done | bytes 147488 | tf_op jit(solution)/shard_map/ppermute | solution.py:36
  474.3 7.3 %collective-permute-done.55 = bf16[96,768]{1,0:T(8,128)(2,1)S(1)} collective-permute-done((bf16[96,768]{1,0:T(8,128)(2,1)S(1)}, bf16[96,768]{1,0:T(8,128)(2,1)S(1)}, u32[]{:S(2)}, u32[]{:S(2)}) %collective-permute-start.55) | collective-permute-done | bytes 147488 | tf_op jit(solution)/shard_map/ppermute | solution.py:36
  482.3 8.6 %input_terms.1 = (f32[256,1536]{1,0:T(8,128)}, f32[256,1536]{1,0:T(8,128)}, bf16[2,1536,96]{2,1,0:T(8,128)(2,1)}) custom-call(s32[1]{0:T(128)} %bitcast.16.core_ref, bf16[8,288,704]{2,1,0:T(8,128)(2,1)} %all-to-all-done.5.back_ref, bf16[1536,1536]{1,0:T(8,128)(2,1)} %all-gather.5.cloned.1.call-done.weight_ref), custom_call_target="tpu_custom_call" | custom-call | flops 1024 | bytes 1024 | tf_op jit(solution)/shard_map/input_terms/pallas_call | solution.py:460
  492.4 4.1 add_convert_fusion
  505.3 12.2 %collective-permute-done.60.refs_1_ = bf16[1536,96]{1,0:T(8,128)(2,1)S(1)} collective-permute-done((bf16[1536,96]{1,0:T(8,128)(2,1)}, bf16[1536,96]{1,0:T(8,128)(2,1)S(1)}, u32[]{:S(2)}, u32[]{:S(2)}) %collective-permute-start.60) | collective-permute-done | bytes 294944 | tf_op jit(solution)/shard_map/ppermute | solution.py:36
  (341 shorter events, 171.9 us)
Async XLA Ops:
  9.4 28.4 %collective-permute-start.3 = (bf16[256,1536]{1,0:T(8,128)(2,1)}, bf16[256,1536]{1,0:T(8,128)(2,1)S(1)}, u32[]{:S(2)}, u32[]{:S(2)}) collective-permute-start(bf16[256,1536]{1,0:T(8,128)(2,1)} %refs_0_.1), channel_id=1, source_target_pairs={{0,4},{2,6},{4,0},{6,2},{8,12},{10,14},{12,8},{14,10},{16,20},{18,... | collective-permute-start | bytes 2359304 | tf_op jit(solution)/shard_map/ppermute | solution.py:36
  17.7 55.4 %all-to-all-start = ((bf16[16,96,290]{2,1,0:T(8,128)(2,1)}), bf16[16,96,290]{2,1,0:T(8,128)(2,1)S(1)}, u32[]{:S(2)}, u32[]{:S(2)}) async-start(bf16[16,96,290]{2,1,0:T(8,128)(2,1)} %bitcast.10), calls=%async_computation | async-start | bytes 2359296 | tf_op jit(solution)/shard_map/all_to_all | solution.py:50
  21.5 51.5 %collective-permute-start.10 = (bf16[96,768]{1,0:T(8,128)(2,1)}, bf16[96,768]{1,0:T(8,128)(2,1)}, u32[]{:S(2)}, u32[]{:S(2)}) collective-permute-start(bf16[96,768]{1,0:T(8,128)(2,1)} %bitcast.132), channel_id=1, source_target_pairs={{0,24},{2,26},{4,28},{6,30},{8,16},{10,18},{12,20},{14,22},{16,8},... | collective-permute-start | bytes 442376 | tf_op jit(solution)/shard_map/ppermute | solution.py:36
  37.8 33.7 %collective-permute-start.6 = (bf16[128,1536]{1,0:T(8,128)(2,1)S(1)}, bf16[128,1536]{1,0:T(8,128)(2,1)S(1)}, u32[]{:S(2)}, u32[]{:S(2)}) collective-permute-start(bf16[128,1536]{1,0:T(8,128)(2,1)S(1)} %slice.47), channel_id=1, source_target_pairs={{0,2},{2,0},{4,6},{6,4},{8,10},{10,8},{12,14},{14,12},{16,18},{18,... | collective-permute-start | bytes 1179656 | tf_op jit(solution)/shard_map/ppermute | solution.py:36
  38.4 33.7 %collective-permute-start.7 = (bf16[128,1536]{1,0:T(8,128)(2,1)S(1)}, bf16[128,1536]{1,0:T(8,128)(2,1)S(1)}, u32[]{:S(2)}, u32[]{:S(2)}) collective-permute-start(bf16[128,1536]{1,0:T(8,128)(2,1)S(1)} %slice.48), channel_id=1, source_target_pairs={{0,4},{2,6},{4,0},{6,2},{8,12},{10,14},{12,8},{14,10},{16,20},{18,... | collective-permute-start | bytes 1179656 | tf_op jit(solution)/shard_map/ppermute | solution.py:36
  75.6 36.1 %all-to-all-start.1 = ((bf16[4,96,1536]{2,1,0:T(8,128)(2,1)}), bf16[4,96,1536]{2,1,0:T(8,128)(2,1)}, u32[]{:S(2)}, u32[]{:S(2)}) async-start(bf16[4,96,1536]{2,1,0:T(8,128)(2,1)} %pad_maximum_fusion), calls=%async_computation.1 | async-start | bytes 2359296 | tf_op jit(solution)/shard_map/all_to_all | solution.py:50
  79.9 151.0 %all-gather.3.cloned.1.call-start = ((), (), s32[]{:S(2)}) async-start(), calls=%async_computation.7 | async-start | bytes 5898240 | tf_op jit(solution)/shard_map/all_gather | solution.py:582
  111.8 31.8 %collective-permute-start.22 = (bf16[256,1536]{1,0:T(8,128)(2,1)}, bf16[256,1536]{1,0:T(8,128)(2,1)}, u32[]{:S(2)}, u32[]{:S(2)}) collective-permute-start(bf16[256,1536]{1,0:T(8,128)(2,1)} %fusion.6.refs_2_.refs_12_), channel_id=1, source_target_pairs={{0,2},{2,0},{4,6},{6,4},{8,10},{10,8},{12,14},{14,12},{16,18},{18,... | collective-permute-start | bytes 2359304 | tf_op jit(solution)/shard_map/ppermute | solution.py:36
  112.7 30.9 %collective-permute-start.23 = (bf16[256,1536]{1,0:T(8,128)(2,1)}, bf16[256,1536]{1,0:T(8,128)(2,1)}, u32[]{:S(2)}, u32[]{:S(2)}) collective-permute-start(bf16[256,1536]{1,0:T(8,128)(2,1)} %fusion.6.refs_2_.refs_12_), channel_id=1, source_target_pairs={{0,4},{2,6},{4,0},{6,2},{8,12},{10,14},{12,8},{14,10},{16,20},{18,... | collective-permute-start | bytes 2359304 | tf_op jit(solution)/shard_map/ppermute | solution.py:36
  113.6 30.0 %collective-permute-start.24 = (bf16[4,96,768]{2,1,0:T(8,128)(2,1)}, bf16[4,96,768]{2,1,0:T(8,128)(2,1)}, u32[]{:S(2)}, u32[]{:S(2)}) collective-permute-start(bf16[4,96,768]{2,1,0:T(8,128)(2,1)} %bitcast_dynamic-update-slice_fusion.4), channel_id=1, source_target_pairs={{0,6},{2,4},{4,2},{6,0},{8,14},{10,12},{12,10},{14,8},{16,22},{18,... | collective-permute-start | bytes 1769480 | tf_op jit(solution)/shard_map/ppermute | solution.py:36
  143.6 47.0 %all-to-all-start.2 = ((bf16[8,96,512]{2,1,0:T(8,128)(2,1)}), bf16[8,96,512]{2,1,0:T(8,128)(2,1)S(1)}, u32[]{:S(2)}, u32[]{:S(2)}) async-start(bf16[8,96,512]{2,1,0:T(8,128)(2,1)} %copy-done.12), calls=%async_computation.2 | async-start | bytes 1572864 | tf_op jit(solution)/shard_map/all_to_all | solution.py:50
  147.2 176.5 %all-gather.5.cloned.1.call-start = ((), (), s32[]{:S(2)}) async-start(), calls=%async_computation.8 | async-start | bytes 5013504 | tf_op jit(solution)/shard_map/all_gather | solution.py:590
  196.8 224.4 %reduce-scatter.2.cloned.1.call-start = ((), (), s32[]{:S(2)}) async-start(), calls=%async_computation.9 | async-start | bytes 5898240 | tf_op jit(solution)/shard_map/reduce_scatter | solution.py:623
  228.6 27.8 %collective-permute-start.28 = (bf16[256,1536]{1,0:T(8,128)(2,1)}, bf16[256,1536]{1,0:T(8,128)(2,1)}, u32[]{:S(2)}, u32[]{:S(2)}) collective-permute-start(bf16[256,1536]{1,0:T(8,128)(2,1)} %fusion.6.refs_2_.refs_12_), channel_id=1, source_target_pairs={{0,1},{1,0},{2,3},{3,2},{4,5},{5,4},{6,7},{7,6},{8,9},{9,8},{10,11... | collective-permute-start | bytes 2359304 | tf_op jit(solution)/shard_map/ppermute | solution.py:40
  280.5 28.7 %collective-permute-start.43 = (bf16[256,1536]{1,0:T(8,128)(2,1)}, bf16[256,1536]{1,0:T(8,128)(2,1)}, u32[]{:S(2)}, u32[]{:S(2)}) collective-permute-start(bf16[256,1536]{1,0:T(8,128)(2,1)} %add_convert_fusion.5), channel_id=1, source_target_pairs={{0,4},{2,6},{4,0},{6,2},{8,12},{10,14},{12,8},{14,10},{16,20},{18,... | collective-permute-start | bytes 2359304 | tf_op jit(solution)/shard_map/ppermute | solution.py:36
  338.1 32.9 %all-to-all-start.3 = ((bf16[8,96,512]{2,1,0:T(8,128)(2,1)}), bf16[8,96,512]{2,1,0:T(8,128)(2,1)S(1)}, u32[]{:S(2)}, u32[]{:S(2)}) async-start(bf16[8,96,512]{2,1,0:T(8,128)(2,1)} %bitcast.34), calls=%async_computation.3 | async-start | bytes 1572864 | tf_op jit(solution)/shard_map/all_to_all | solution.py:50
  371.8 49.4 %all-to-all-start.4 = ((bf16[4,384,768]{2,1,0:T(8,128)(2,1)}), bf16[4,384,768]{2,1,0:T(8,128)(2,1)S(1)}, u32[]{:S(2)}, u32[]{:S(2)}) async-start(bf16[4,384,768]{2,1,0:T(8,128)(2,1)} %bitcast.37), calls=%async_computation.4 | async-start | bytes 4718592 | tf_op jit(solution)/shard_map/all_to_all | solution.py:50
  375.5 45.7 %collective-permute-start.52 = (bf16[256,1536]{1,0:T(8,128)(2,1)}, bf16[256,1536]{1,0:T(8,128)(2,1)}, u32[]{:S(2)}, u32[]{:S(2)}) collective-permute-start(bf16[256,1536]{1,0:T(8,128)(2,1)} %add_convert_fusion.1), channel_id=1, source_target_pairs={{0,6},{2,4},{4,2},{6,0},{8,14},{10,12},{12,10},{14,8},{16,22},{18,... | collective-permute-start | bytes 2359304 | tf_op jit(solution)/shard_map/ppermute | solution.py:36
  421.2 61.1 %all-to-all-start.5 = ((bf16[8,288,704]{2,1,0:T(8,128)(2,1)}), bf16[8,288,704]{2,1,0:T(8,128)(2,1)}, u32[]{:S(2)}, u32[]{:S(2)}) async-start(bf16[8,288,704]{2,1,0:T(8,128)(2,1)} %attention_backward.1), calls=%async_computation.6 | async-start | bytes 7077888 | tf_op jit(solution)/shard_map/all_to_all | solution.py:50
  426.1 45.6 %collective-permute-start.53 = (bf16[96,768]{1,0:T(8,128)(2,1)S(1)}, bf16[96,768]{1,0:T(8,128)(2,1)S(1)}, u32[]{:S(2)}, u32[]{:S(2)}) collective-permute-start(bf16[96,768]{1,0:T(8,128)(2,1)S(1)} %get-tuple-element.317), channel_id=1, source_target_pairs={{0,8},{2,10},{4,12},{6,14},{8,0},{10,2},{12,4},{14,6},{16,24},{18,... | collective-permute-start | bytes 442376 | tf_op jit(solution)/shard_map/ppermute | solution.py:36
  427.7 46.6 %collective-permute-start.54 = (bf16[96,768]{1,0:T(8,128)(2,1)S(1)}, bf16[96,768]{1,0:T(8,128)(2,1)S(1)}, u32[]{:S(2)}, u32[]{:S(2)}) collective-permute-start(bf16[96,768]{1,0:T(8,128)(2,1)S(1)} %get-tuple-element.316), channel_id=1, source_target_pairs={{0,16},{2,18},{4,20},{6,22},{8,24},{10,26},{12,28},{14,30},{16,0},... | collective-permute-start | bytes 442376 | tf_op jit(solution)/shard_map/ppermute | solution.py:36
  427.7 53.9 %collective-permute-start.56 = (bf16[96,1536]{1,0:T(8,128)(2,1)S(1)}, bf16[96,1536]{1,0:T(8,128)(2,1)S(1)}, u32[]{:S(2)}, u32[]{:S(2)}) collective-permute-start(bf16[96,1536]{1,0:T(8,128)(2,1)S(1)} %get-tuple-element.313), channel_id=1, source_target_pairs={{0,2},{2,0},{4,6},{6,4},{8,10},{10,8},{12,14},{14,12},{16,18},{18,... | collective-permute-start | bytes 884744 | tf_op jit(solution)/shard_map/ppermute | solution.py:36
  429.0 52.6 %collective-permute-start.57 = (bf16[96,1536]{1,0:T(8,128)(2,1)S(1)}, bf16[96,1536]{1,0:T(8,128)(2,1)S(1)}, u32[]{:S(2)}, u32[]{:S(2)}) collective-permute-start(bf16[96,1536]{1,0:T(8,128)(2,1)S(1)} %get-tuple-element.312), channel_id=1, source_target_pairs={{0,4},{2,6},{4,0},{6,2},{8,12},{10,14},{12,8},{14,10},{16,20},{18,... | collective-permute-start | bytes 884744 | tf_op jit(solution)/shard_map/ppermute | solution.py:36
  430.2 52.1 %collective-permute-start.58 = (bf16[96,1536]{1,0:T(8,128)(2,1)S(1)}, bf16[96,1536]{1,0:T(8,128)(2,1)S(1)}, u32[]{:S(2)}, u32[]{:S(2)}) collective-permute-start(bf16[96,1536]{1,0:T(8,128)(2,1)S(1)} %get-tuple-element.311), channel_id=1, source_target_pairs={{0,6},{2,4},{4,2},{6,0},{8,14},{10,12},{12,10},{14,8},{16,22},{18,... | collective-permute-start | bytes 884744 | tf_op jit(solution)/shard_map/ppermute | solution.py:36
  (112 other events, 1341.7 us)
Sparse Core Ops, SparseCore 0:
  111.9 93.8 all-gather.2
  209.2 96.4 all-gather.4
  323.8 91.1 reduce-scatter.1

commit v4 on v3

--- a/solution.py
+++ b/solution.py
@@ -11,6 +11,7 @@
 HEAD_SIZE = 96
 HALF = HEAD_SIZE // 2
 SPANS = 8
+KV_HEADS = SPANS // 2
 PLANE = 4
 PACKED_LENGTH = 4096
 SPAN = PACKED_LENGTH // SPANS
@@ -48,6 +49,32 @@
 def exchange(value, size):
     groups = None if size == lax.axis_size("fsdp") else groups_of(size)
     return lax.all_to_all(value, "fsdp", 0, 0, axis_index_groups=groups)
+
+
+def head_cut_kernel(q_ref, k_ref, v_ref, gain_ref, out_ref):
+    gains = gain_ref[...].astype(f32)
+    for place in range(SPANS):
+        parts = []
+        for ref in (q_ref, k_ref, v_ref):
+            head = place * ref.shape[1] // (SPANS * HEAD_SIZE)
+            parts.append(ref[:, head * HEAD_SIZE:(head + 1) * HEAD_SIZE].astype(f32))
+        cut = jnp.concatenate(parts + [gains], axis=1).astype(bf16)
+        for first in range(0, out_ref.shape[0], SPANS):
+            out_ref[first + place] = cut
+
+
+def head_cut(count, q_weight, k_weight, v_weight, gains):
+    vmem = pl.BlockSpec(memory_space=pltpu.VMEM)
+    shard = q_weight.shape[0]
+    return pl.pallas_call(
+        head_cut_kernel,
+        in_specs=[vmem] * 4,
+        out_specs=vmem,
+        out_shape=jax.ShapeDtypeStruct((count, shard, 3 * HEAD_SIZE + 2), bf16),
+        compiler_params=pltpu.CompilerParams(vmem_limit_bytes=32 * 2**20),
+        cost_estimate=brief,
+        name="head_cut",
+    )(q_weight, k_weight, v_weight, gains)
 
 
 def project_kernel(*refs):
@@ -206,8 +233,8 @@
     )(q_t, k, v_t, id_row, id_col)
 
 
-def backward_kernel(cubes, q_t_ref, q_ref, k_t_ref, k_ref, v_ref, dout_ref, out_ref, lse_ref, id_row_ref, id_col_ref,
-                    cos_ref, sin_ref, normed_ref, grad_ref, delta_ref, dout_n_ref, dq_ref, sum_ref):
+def backward_kernel(q_t_ref, q_ref, k_t_ref, k_ref, v_ref, dout_ref, out_ref, lse_ref, id_row_ref, id_col_ref,
+                    cos_ref, sin_ref, normed_ref, grad_ref, weight_grad_ref, delta_ref, dout_n_ref, dq_ref, sum_ref):
     block = pl.program_id(0)
 
     @pl.when(block == 0)
@@ -248,22 +275,16 @@
         turned = jnp.concatenate(
             [first * cosine + second * sine, second * cosine - first * sine], axis=0
         )
-        grad_ref[block, number * HEAD_SIZE:(number + 1) * HEAD_SIZE, :SPAN] = turned.astype(bf16)
-    grad_ref[block, 2 * HEAD_SIZE:, :SPAN] = dvalue.T.astype(bf16)
-    sum_ref[...] += dot(grad_ref[block, :, :SPAN], normed_ref[0])
+        grad_ref[0, number * HEAD_SIZE:(number + 1) * HEAD_SIZE, :] = turned.astype(bf16)
+    grad_ref[0, 2 * HEAD_SIZE:, :] = dvalue.T.astype(bf16)
+    sum_ref[...] += dot(grad_ref[0], normed_ref[0])
 
     @pl.when(block == SPANS - 1)
     def _():
-        part = sum_ref.shape[1] // SPANS
-        shard = part // cubes
-        for place in range(SPANS):
-            pieces = [
-                sum_ref[:, (cube * SPANS + place) * shard:(cube * SPANS + place + 1) * shard] for cube in range(cubes)
-            ]
-            grad_ref[place, :, SPAN:] = jnp.concatenate(pieces, axis=1).astype(bf16)
-
-
-def attention_backward(q_t, q, k_t, k, v, dout, out, lse, id_row, id_col, cosine, sine, normed, cubes):
+        weight_grad_ref[...] = sum_ref[...].T.astype(bf16)
+
+
+def attention_backward(q_t, q, k_t, k, v, dout, out, lse, id_row, id_col, cosine, sine, normed):
     tokens = k.shape[0]
     width = normed.shape[2]
     whole = lambda array: pl.BlockSpec(array.shape, lambda i: (0,) * array.ndim)
@@ -271,15 +292,21 @@
     tall = pl.BlockSpec((SPAN, HEAD_SIZE), lambda i: (i, 0))
     table = pl.BlockSpec((HALF, SPAN), lambda i: (0, i))
     return pl.pallas_call(
-        functools.partial(backward_kernel, cubes),
+        backward_kernel,
         grid=(SPANS,),
         in_specs=[
             whole(q_t), whole(q), wide, tall, tall, whole(dout), whole(out), whole(lse), whole(id_row),
             pl.BlockSpec((SPAN, id_col.shape[1]), lambda i: (i, 0)), table, table,
             pl.BlockSpec((1, SPAN, width), lambda i: (i, 0, 0)),
         ],
-        out_specs=pl.BlockSpec((SPANS, 3 * HEAD_SIZE, SPAN + width // SPANS), lambda i: (0, 0, 0)),
-        out_shape=jax.ShapeDtypeStruct((SPANS, 3 * HEAD_SIZE, SPAN + width // SPANS), bf16),
+        out_specs=[
+            pl.BlockSpec((1, 3 * HEAD_SIZE, SPAN), lambda i: (i, 0, 0)),
+            pl.BlockSpec((width, 3 * HEAD_SIZE), lambda i: (0, 0)),
+        ],
+        out_shape=[
+            jax.ShapeDtypeStruct((SPANS, 3 * HEAD_SIZE, SPAN), bf16),
+            jax.ShapeDtypeStruct((width, 3 * HEAD_SIZE), bf16),
+        ],
         scratch_shapes=[
             pltpu.VMEM((1, tokens), f32),
             pltpu.VMEM((tokens, HEAD_SIZE), bf16),
@@ -292,17 +319,18 @@
     )(q_t, q, k_t, k, v, dout, out, lse, id_row, id_col, cosine, sine, normed)
 
 
-def head_finish_kernel(*refs):
-    sum_refs, (q_ref, k_ref, v_ref, q_out, k_out, v_out, product_ref) = refs[:-7], refs[-7:]
-    total = sum_refs[0][...].astype(f32)
-    for ref in sum_refs[1:]:
-        total = total + ref[...].astype(f32)
-    total = total.T
+def head_finish_kernel(sum_ref, q_ref, k_ref, v_ref, q_out, k_out, v_out, product_ref):
     product = jnp.zeros(product_ref.shape, f32)
-    at = 0
-    for ref, out in ((q_ref, q_out), (k_ref, k_out), (v_ref, v_out)):
-        grad = total[:, at:at + out.shape[1]]
-        at += out.shape[1]
+    for number, (ref, out) in enumerate(((q_ref, q_out), (k_ref, k_out), (v_ref, v_out))):
+        heads = out.shape[1] // HEAD_SIZE
+        copies = SPANS // heads
+        grads = []
+        for head in range(heads):
+            grad = sum_ref[head * copies].astype(f32)
+            for other in range(1, copies):
+                grad = grad + sum_ref[head * copies + other].astype(f32)
+            grads.append(grad[:, number * HEAD_SIZE:(number + 1) * HEAD_SIZE])
+        grad = jnp.concatenate(grads, axis=1)
         out[...] = grad
         product = product + jnp.sum(grad * ref[...].astype(f32), axis=1, keepdims=True)
     product_ref[...] = product
@@ -312,13 +340,14 @@
     vmem = pl.BlockSpec(memory_space=pltpu.VMEM)
     return pl.pallas_call(
         head_finish_kernel,
-        in_specs=[vmem] * (len(sums) + 3),
+        in_specs=[vmem] * 4,
         out_specs=[vmem] * 4,
         out_shape=[jax.ShapeDtypeStruct(w.shape, f32) for w in (q_weight, k_weight, v_weight)]
         + [jax.ShapeDtypeStruct((q_weight.shape[0], 1), f32)],
         compiler_params=pltpu.CompilerParams(vmem_limit_bytes=32 * 2**20),
+        cost_estimate=brief,
         name="head_finish",
-    )(*sums, q_weight, k_weight, v_weight)
+    )(sums, q_weight, k_weight, v_weight)
 
 
 def unit_finish_kernel(place_ref, *refs):
@@ -424,26 +453,23 @@
     return [outs[6 * pair:6 * pair + 6] for pair in range(pairs)]
 
 
-def back_kernel(core_ref, back_ref, weight_ref, mine_ref, other_ref, head_ref, table_ref):
+def merged_heads(back_ref):
     heads = back_ref.shape[0]
-    kv_heads = (table_ref.shape[0] // HEAD_SIZE - heads) // 2
-    per_kv = heads // kv_heads
-    cubes, _, shard = head_ref.shape
-
-    def put(at, value):
-        table_ref[at:at + HEAD_SIZE, :] = value[:, :SPAN]
-        for cube in range(cubes):
-            head_ref[cube, at:at + HEAD_SIZE, :] = value[:, SPAN + cube * shard:SPAN + (cube + 1) * shard]
-
-    for head in range(heads):
-        put(head * HEAD_SIZE, back_ref[head, :HEAD_SIZE, :])
-    for number in range(2):
-        here = slice((number + 1) * HEAD_SIZE, (number + 2) * HEAD_SIZE)
-        for head in range(kv_heads):
+    per_kv = heads // KV_HEADS
+    rows = [back_ref[head, :HEAD_SIZE, :] for head in range(heads)]
+    for number in (1, 2):
+        here = slice(number * HEAD_SIZE, (number + 1) * HEAD_SIZE)
+        for head in range(KV_HEADS):
             total = back_ref[head * per_kv, here, :].astype(f32)
             for copy in range(1, per_kv):
                 total = total + back_ref[head * per_kv + copy, here, :].astype(f32)
-            put((heads + number * kv_heads + head) * HEAD_SIZE, total.astype(bf16))
+            rows.append(total.astype(bf16))
+    return rows
+
+
+def back_kernel(core_ref, back_ref, weight_ref, mine_ref, other_ref, table_ref):
+    for at, value in enumerate(merged_heads(back_ref)):
+        table_ref[at * HEAD_SIZE:(at + 1) * HEAD_SIZE, :] = value
     rows = mine_ref.shape[0]
     both = dot(weight_ref[...], table_ref[...])
     low, high = both[:, :rows].T, both[:, rows:].T
@@ -452,19 +478,17 @@
     other_ref[...] = jnp.where(first, high, low)
 
 
-def input_terms(back, weight, core, cubes):
+def input_terms(back, weight, core):
     vmem = pl.BlockSpec(memory_space=pltpu.VMEM)
     width, features = weight.shape
     rows = SPAN // 2
-    shard = (back.shape[2] - SPAN) // cubes
     return pl.pallas_call(
         back_kernel,
         in_specs=[pl.BlockSpec(memory_space=pltpu.SMEM), vmem, vmem],
-        out_specs=[vmem] * 3,
-        out_shape=[jax.ShapeDtypeStruct((rows, width), f32)] * 2
-        + [jax.ShapeDtypeStruct((cubes, features, shard), bf16)],
+        out_specs=[vmem] * 2,
+        out_shape=[jax.ShapeDtypeStruct((rows, width), f32)] * 2,
         scratch_shapes=[pltpu.VMEM((features, SPAN), bf16)],
-        compiler_params=pltpu.CompilerParams(vmem_limit_bytes=56 * 2**20),
+        compiler_params=pltpu.CompilerParams(vmem_limit_bytes=40 * 2**20),
         cost_estimate=brief,
         name="input_terms",
     )(core, back, weight)
@@ -513,21 +537,8 @@
     per_kv = q_heads // kv_heads
     units = gate_weight.shape[2] // PLANE
 
-    def by_head(weight, heads, copies):
-        cut = weight[0].reshape(shard, heads, HEAD_SIZE).transpose(1, 0, 2)
-        return jnp.repeat(cut, copies, axis=0)
-
     gains_own = jnp.stack([attn_gain[0], mlp_gain[0]], axis=-1)
-    sent = jnp.concatenate(
-        [
-            by_head(q_weight, q_heads, 1),
-            by_head(key_matrix, kv_heads, per_kv),
-            by_head(value_matrix, kv_heads, per_kv),
-            jnp.broadcast_to(gains_own[None], (SPANS, shard, 2)),
-        ],
-        axis=-1,
-    )
-    sent = jnp.tile(sent, (count // SPANS, 1, 1))
+    sent = head_cut(count, q_weight[0], key_matrix[0], value_matrix[0], gains_own)
 
     plane_place = f % PLANE
     cubes = count // SPANS
@@ -615,10 +626,12 @@
     results = [first, second, third, fourth]
     dn_got = [swap(first[1])] + dn_got + [swap(fourth[1])]
     dn_pair = [result[0] + got.astype(f32) for result, got in zip(results, dn_got)]
-    dn_far = [dn_pair[0]] + [hop(dn_pair[k].astype(bf16), k) for k in range(1, PLANE)]
+    dn_low = [dn_pair[k].astype(bf16) for k in range(1, PLANE)]
+    dn_low[2], acts = tie((dn_low[2], [result[5] for result in results]))
+    dn_far = [dn_pair[0]] + [hop(low, k) for k, low in enumerate(dn_low, 1)]
     out_pair = [result[2] + swap(result[3]).astype(f32) for result in results]
     out_low = [out_pair[k].astype(bf16) for k in range(1, PLANE)]
-    unit_term = unit_grads(normed_m, [result[4] for result in results], dmlp, [result[5] for result in results])
+    unit_term = unit_grads(normed_m, [result[4] for result in results], dmlp, acts)
     dn_far, out_low, in_part, unit_term = tie((dn_far, out_low, in_part, unit_term))
     unit_sum = lax.psum_scatter(unit_term, "fsdp", scatter_dimension=0, tiled=True, axis_index_groups=lines)
     out_far = [hop(low, k) for k, low in enumerate(out_low[:2], 1)]
@@ -641,10 +654,16 @@
     dout, out_term, out_low, out_far = tie((dout, out_term, out_low, out_far))
     out_term = exchange(out_term.reshape(PLANE, planes * shard, -1), PLANE)
     out_far += [hop(out_low[2], 3)]
-    grads = attention_backward(
-        q_t, q, k_t, key, v, dout, out_full, lse, id_row, id_col, cosine, sine, normed, cubes
-    )
-    grads, out_term, out_far, unit_sum = tie((grads, out_term, out_far, unit_sum))
+    grads, head_low = attention_backward(
+        q_t, q, k_t, key, v, dout, out_full, lse, id_row, id_col, cosine, sine, normed
+    )
+    grads, head_low, out_term, out_far, unit_sum = tie((grads, head_low, out_term, out_far, unit_sum))
+    head_low = head_low.reshape(cubes, SPANS * shard, 3 * HEAD_SIZE)
+    head_sum = lax.dynamic_index_in_dim(head_low, cube_at, 0, keepdims=False).astype(f32)
+    for k in range(1, cubes):
+        far = lax.dynamic_index_in_dim(head_low, cube_at ^ k, 0, keepdims=False)
+        head_sum = head_sum + hop(far, SPANS * k).astype(f32)
+    head_sum = head_sum.astype(bf16).reshape(SPANS, shard, 3 * HEAD_SIZE)
 
     back = exchange(grads, SPANS)
     unit_sum = unit_sum.reshape(PLANE, shard, 3 * units)
@@ -656,22 +675,21 @@
     for k in range(1, planes):
         far = lax.dynamic_index_in_dim(out_term, plane_at ^ k, 0, keepdims=False)
         out_sums.append(hop(far.astype(bf16), PLANE * k))
-    back, out_sums, unit_back = tie((back, out_sums, unit_back))
-    for far in out_sums:
-        out_grad = out_grad + far.astype(f32)
-    mine, other, head_terms = input_terms(back, in_part, t.reshape(1).astype(jnp.int32), cubes)
-    head_sums = [lax.dynamic_index_in_dim(head_terms, cube_at ^ k, 0, keepdims=False) for k in range(cubes)]
-    head_sums = [piece if k == 0 else hop(piece, SPANS * k) for k, piece in enumerate(head_sums)]
-    dnormed_a = mine + swap(other)
-    input_grad = dmid + norm_backward(stream, rms_factor(stream), gain_a, dnormed_a)
-    input_grad, head_sums = tie((input_grad, head_sums))
-
-    q_grad, k_grad, v_grad, gain_a_part = head_finish(head_sums, q_weight[0], key_matrix[0], value_matrix[0])
-
     out_total = out_pair[0]
     for far in out_far:
         out_total = out_total + far.astype(f32)
     output = (mid + out_total).astype(bf16)
+    back, out_sums, unit_back, output, head_sum = tie((back, out_sums, unit_back, output, head_sum))
+    head_sums = exchange(head_sum, SPANS)
+    for far in out_sums:
+        out_grad = out_grad + far.astype(f32)
+    mine, other = input_terms(back, in_part, t.reshape(1).astype(jnp.int32))
+    dnormed_a = mine + swap(other)
+    input_grad = dmid + norm_backward(stream, rms_factor(stream), gain_a, dnormed_a)
+    input_grad, head_sums = tie((input_grad, head_sums))
+
+    q_grad, k_grad, v_grad, gain_a_part = head_finish(head_sums, q_weight[0], key_matrix[0], value_matrix[0])
+
     gate_grad, up_grad, down_grad, gain_m_part = unit_finish(
         plane_place.reshape(1).astype(jnp.int32), unit_back, gate_weight[0], up_weight[0]
     )

time: 537 us -> 518 us (0.965)
  waiting for transfers between devices: 189 us -> 157 us
  local copies, waits for them, and re-layouts: 44.1 us -> 56.5 us
  starting transfers between devices: 80.7 us -> 89.3 us
    ppermute x34, waiting for transfers between devices: 161 us -> 126 us  [hop(): lax.ppermute(value, 'fsdp', [(i, i ^ distance) for i in range(count)])]
    unnamed x131 -> x140, local copies, waits for them, and re-layouts: 11.6 us -> 21.5 us
    all_to_all x6 -> x7, starting transfers between devices: 23.7 us -> 29.4 us  [exchange(): return lax.all_to_all(value, 'fsdp', 0, 0, axis_index_groups=groups)]
    all_to_all x6 -> x7, waiting for transfers between devices: 19.4 us -> 23.6 us  [exchange(): return lax.all_to_all(value, 'fsdp', 0, 0, axis_index_groups=groups)]
    pallas_call x2 -> x3, Pallas kernels: 44.4 us -> 45.1 us  [the longest x1 42.7 us: attention_backward(): pl.pallas_call(backward_kernel, grid=(SPANS,), in_specs=[whole(q_t), whol...]
  transfers between devices with their start and end apart: 71 -> 72, of which waited for: 21 -> 22; matrix products, arithmetic and copies ran while one was open for 17% -> 18% of each run, Pallas kernels for 27% -> 27%
where the time goes in v4:
time: 518 us; the launch traced here: 512 us
  waiting for transfers between devices  157 us (30%)
  Pallas kernels  142 us (27%)
  starting transfers between devices  89.3 us (17%)
  local copies, waits for them, and re-layouts  56.5 us (11%)
  other arithmetic  39.1 us (8%)
  between operations  14.8 us (3%)
  matrix products  13.3 us (3%)
    ppermute x34, waiting for transfers between devices, hop(): lax.ppermute(value, 'fsdp', [(i, i ^ distance) for i in range(count)])  126 us
    pallas_call x1, Pallas kernels, attention_backward(): pl.pallas_call(backward_kernel, grid=(SPANS,), in_specs=[whole(q_t), whol...  42.7 us
    ppermute x34, starting transfers between devices, hop(): lax.ppermute(value, 'fsdp', [(i, i ^ distance) for i in range(count)])  37.9 us
    pallas_call x2, Pallas kernels, feed(): pl.pallas_call(functools.partial(feed_kernel, pairs), in_specs=[vmem] * (...  33.7 us
    all_to_all x7, starting transfers between devices, exchange(): return lax.all_to_all(value, 'fsdp', 0, 0, axis_index_groups=groups)  29.4 us
    all_to_all x7, waiting for transfers between devices, exchange(): return lax.all_to_all(value, 'fsdp', 0, 0, axis_index_groups=groups)  23.6 us
    pallas_call x1, Pallas kernels, attention_forward(): pl.pallas_call(forward_kernel, grid=(SPANS,), in_specs=[pl.BlockSpec((HEA...  22.8 us
    unnamed x140, local copies, waits for them, and re-layouts  21.5 us
  transfers between devices with their start and end apart: 72, of which 22 were waited for; matrix products, arithmetic and copies ran while one was open for 18% of the time, Pallas kernels for 27%

profile of v4, /device:TPU:1, one launch (start us, length us, event | category | flops | bytes accessed | tf_op | source)
XLA Modules:
  0.0 512.1 jit_solution(11113282251835135337)
XLA Ops:
  16.6 3.8 all-to-all-start
  37.8 3.9 multiply_sine_fusion
  43.5 14.8 %collective-permute-done.15.refs_12_ = bf16[256,1536]{1,0:T(8,128)(2,1)} collective-permute-done((bf16[256,1536]{1,0:T(8,128)(2,1)}, bf16[256,1536]{1,0:T(8,128)(2,1)}, u32[]{:S(2)}, u32[]{:S(2)}) %collective-permute-start.15) | collective-permute-done | bytes 786464 | tf_op jit(solution)/shard_map/ppermute | solution.py:37
  63.4 6.6 %collective-permute-done.6 = bf16[128,1536]{1,0:T(8,128)(2,1)S(1)} collective-permute-done((bf16[128,1536]{1,0:T(8,128)(2,1)S(1)}, bf16[128,1536]{1,0:T(8,128)(2,1)S(1)}, u32[]{:S(2)}, u32[]{:S(2)}) %collective-permute-start.6) | collective-permute-done | bytes 393248 | tf_op jit(solution)/shard_map/ppermute | solution.py:37
  75.3 4.3 all-to-all-start.1
  92.9 18.5 %project.1 = (bf16[8,512,1536]{2,1,0:T(8,128)(2,1)}, f32[8,1536]{1,0:T(8,128)}, bf16[96,4096]{1,0:T(8,128)(2,1)}, bf16[96,4096]{1,0:T(8,128)(2,1)}, bf16[96,4096...) custom-call(bf16[256,1536]{1,0:T(8,128)(2,1)} %refs_0_.1, ...), custom_call_target="tpu_custom_call" | custom-call | flops 1024 | bytes 1024 | tf_op jit(solution)/shard_map/project/pallas_call | solution.py:142
  116.5 22.8 %attention_forward.1 = (bf16[8,96,512]{2,1,0:T(8,128)(2,1)S(1)}, f32[96,4096]{1,0:T(8,128)S(1)}, f32[1,4096]{1,0:T(1,128)S(1)}) custom-call(bf16[96,4096]{1,0:T(8,128)(2,1)S(1)} %copy-done.5, bf16[4096,96]{1,0:T(8,128)(2,1)S(1)} %copy-done.4, bf16[96,4096]{1,0:T(8,128)(2,1)S(1)} %copy-done.15, s32[1,4096]{1,0:T(1,128)S(1)} %bitcast.112, ...), custom_call_target="tpu_custom_call" | custom-call | flops 1024 | bytes 1024 | tf_op jit(solution)/shard_map/attention_forward/pallas_call | solution.py:210
  154.3 17.1 %collective-permute-done.25.refs_6_.refs_18_ = bf16[256,1536]{1,0:T(8,128)(2,1)} collective-permute-done((bf16[256,1536]{1,0:T(8,128)(2,1)}, bf16[256,1536]{1,0:T(8,128)(2,1)}, u32[]{:S(2)}, u32[]{:S(2)}) %collective-permute-start.25) | collective-permute-done | bytes 786464 | tf_op jit(solution)/shard_map/ppermute | solution.py:37
  171.3 18.6 %all-to-all-done.2 = bf16[8,96,512]{2,1,0:T(8,128)(2,1)S(1)} async-done(((bf16[8,96,512]{2,1,0:T(8,128)(2,1)}), bf16[8,96,512]{2,1,0:T(8,128)(2,1)S(1)}, u32[]{:S(2)}, u32[]{:S(2)}) %all-to-all-start.2) | async-done | bytes 786464 | tf_op jit(solution)/shard_map/all_to_all | solution.py:51
  206.8 17.1 %collective-permute-done.29.refs_0_.refs_2_ = bf16[256,1536]{1,0:T(8,128)(2,1)S(1)} collective-permute-done((bf16[256,1536]{1,0:T(8,128)(2,1)S(1)}, bf16[256,1536]{1,0:T(8,128)(2,1)S(1)}, u32[]{:S(2)}, u32[]{:S(2)}) %collective-permute-start.29) | collective-permute-done | bytes 786464 | tf_op jit(solution)/shard_map/ppermute | solution.py:37
  230.2 16.6 %feed.2 = (f32[256,1536]{1,0:T(8,128)}, bf16[256,1536]{1,0:T(8,128)(2,1)S(1)}, f32[256,1536]{1,0:T(8,128)}, bf16[256,1536]{1,0:T(8,128)(2,1)S(1)}, bf16[512,1024...) custom-call(bf16[256,1536]{1,0:T(8,128)(2,1)S(1)} %collective-permut, ...), custom_call_target="tpu_custom_call" | custom-call | flops 1024 | bytes 1024 | tf_op jit(solution)/shard_map/feed/pallas_call | solution.py:444
  246.8 5.4 %collective-permute-done.35.refs_4_.refs_6_ = bf16[256,1536]{1,0:T(8,128)(2,1)} collective-permute-done((bf16[256,1536]{1,0:T(8,128)(2,1)S(1)}, bf16[256,1536]{1,0:T(8,128)(2,1)}, u32[]{:S(2)}, u32[]{:S(2)}) %collective-permute-start.35) | collective-permute-done | bytes 786464 | tf_op jit(solution)/shard_map/ppermute | solution.py:37
  259.7 17.1 %feed.3 = (f32[256,1536]{1,0:T(8,128)}, bf16[256,1536]{1,0:T(8,128)(2,1)S(1)}, f32[256,1536]{1,0:T(8,128)}, bf16[256,1536]{1,0:T(8,128)(2,1)}, bf16[512,1024]{1,...) custom-call(bf16[256,1536]{1,0:T(8,128)(2,1)S(1)} %multiply_convert_, ...), custom_call_target="tpu_custom_call" | custom-call | flops 1024 | bytes 1024 | tf_op jit(solution)/shard_map/feed/pallas_call | solution.py:444
  288.7 15.1 %unit_grads.1 = bf16[1536,1536]{1,0:T(8,128)(2,1)} custom-call(bf16[256,1536]{1,0:T(8,128)(2,1)S(1)} %multiply_convert_fusion.refs_0_, bf16[256,1536]{1,0:T(8,128)(2,1)} %collective-permute-done.27.refs_1_, bf16[256,1536]{1,0:T(8,128)(2,1)S(1)} %collective-permute-done.29.refs_0_.refs_2_, bf16[256,1536]{1,0:T(8,128)(2,1)S(1)} %collective-permute-done.31.refs_1_.refs_3_, ...), custom_call_target="tpu_custom_call" | custom-call | flops 1024 | bytes 1024 | tf_op jit(solution)/shard_map/unit_grads/pallas_call | solution.py:397
  305.6 13.3 %collective-permute-done.44 = bf16[256,1536]{1,0:T(8,128)(2,1)} collective-permute-done((bf16[256,1536]{1,0:T(8,128)(2,1)}, bf16[256,1536]{1,0:T(8,128)(2,1)}, u32[]{:S(2)}, u32[]{:S(2)}) %collective-permute-start.44) | collective-permute-done | bytes 786464 | tf_op jit(solution)/shard_map/ppermute | solution.py:37
  321.2 3.9 fusion.22
  328.8 4.4 convolution_convert_fusion.1
  333.2 3.9 all-to-all-start.3
  344.7 19.8 %collective-permute-done.49 = bf16[256,1536]{1,0:T(8,128)(2,1)S(1)} collective-permute-done((bf16[256,1536]{1,0:T(8,128)(2,1)}, bf16[256,1536]{1,0:T(8,128)(2,1)S(1)}, u32[]{:S(2)}, u32[]{:S(2)}) %collective-permute-start.49) | collective-permute-done | bytes 786464 | tf_op jit(solution)/shard_map/ppermute | solution.py:37
  373.0 42.7 %attention_backward.1 = (bf16[8,288,512]{2,1,0:T(8,128)(2,1)}, bf16[1536,288]{1,0:T(8,128)(2,1)}) custom-call(bf16[96,4096]{1,0:T(8,128)(2,1)} %get-tuple-element.168.q_t_ref, bf16[4096,96]{1,0:T(8,128)(2,1)} %get-tuple-element.169.q_ref, bf16[96,4096]{1,0:T(8,128)(2,1)} %get-tuple-element.170.k_t_ref, bf16[4096,96]{1,0:T(8,128)(2,1)} %get-tuple-element.171.k_ref, ...), custom_call_target="tpu_custom_call" | custom-call | flops 1024 | bytes 1024 | tf_op jit(solution)/shard_map/attention_backward/pallas_call | solution.py:294
  439.8 20.5 %collective-permute-done.52 = bf16[96,768]{1,0:T(8,128)(2,1)S(1)} collective-permute-done((bf16[96,768]{1,0:T(8,128)(2,1)}, bf16[96,768]{1,0:T(8,128)(2,1)S(1)}, u32[]{:S(2)}, u32[]{:S(2)}) %collective-permute-start.52) | collective-permute-done | bytes 147488 | tf_op jit(solution)/shard_map/ppermute | solution.py:37
  466.4 6.9 %collective-permute-done.53 = bf16[96,768]{1,0:T(8,128)(2,1)} collective-permute-done((bf16[96,768]{1,0:T(8,128)(2,1)}, bf16[96,768]{1,0:T(8,128)(2,1)}, u32[]{:S(2)}, u32[]{:S(2)}) %collective-permute-start.53) | collective-permute-done | bytes 147488 | tf_op jit(solution)/shard_map/ppermute | solution.py:37
  475.6 4.3 input_terms.1
  484.5 6.6 %all-to-all-start.6 = ((bf16[8,96,288]{2,1,0:T(8,128)(2,1)}), bf16[8,96,288]{2,1,0:T(8,128)(2,1)S(1)}, u32[]{:S(2)}, u32[]{:S(2)}) async-start(bf16[8,96,288]{2,1,0:T(8,128)(2,1)} %bitcast.125), calls=%async_computation.7 | async-start | bytes 1179648 | tf_op jit(solution)/shard_map/all_to_all | solution.py:51
  (347 shorter events, 189.5 us)
Async XLA Ops:
  16.6 55.6 %all-to-all-start = ((bf16[16,96,290]{2,1,0:T(8,128)(2,1)}), bf16[16,96,290]{2,1,0:T(8,128)(2,1)S(1)}, u32[]{:S(2)}, u32[]{:S(2)}) async-start(bf16[16,96,290]{2,1,0:T(8,128)(2,1)} %head_cut.1), calls=%async_computation | async-start | bytes 2359296 | tf_op jit(solution)/shard_map/all_to_all | solution.py:51
  20.4 51.8 %collective-permute-start.10 = (bf16[96,768]{1,0:T(8,128)(2,1)}, bf16[96,768]{1,0:T(8,128)(2,1)}, u32[]{:S(2)}, u32[]{:S(2)}) collective-permute-start(bf16[96,768]{1,0:T(8,128)(2,1)} %bitcast.130), channel_id=1, source_target_pairs={{0,24},{2,26},{4,28},{6,30},{8,16},{10,18},{12,20},{14,22},{16,8},... | collective-permute-start | bytes 442376 | tf_op jit(solution)/shard_map/ppermute | solution.py:37
  36.7 33.2 %collective-permute-start.6 = (bf16[128,1536]{1,0:T(8,128)(2,1)S(1)}, bf16[128,1536]{1,0:T(8,128)(2,1)S(1)}, u32[]{:S(2)}, u32[]{:S(2)}) collective-permute-start(bf16[128,1536]{1,0:T(8,128)(2,1)S(1)} %slice.47), channel_id=1, source_target_pairs={{0,2},{2,0},{4,6},{6,4},{8,10},{10,8},{12,14},{14,12},{16,18},{18,... | collective-permute-start | bytes 1179656 | tf_op jit(solution)/shard_map/ppermute | solution.py:37
  37.3 33.9 %collective-permute-start.7 = (bf16[128,1536]{1,0:T(8,128)(2,1)S(1)}, bf16[128,1536]{1,0:T(8,128)(2,1)S(1)}, u32[]{:S(2)}, u32[]{:S(2)}) collective-permute-start(bf16[128,1536]{1,0:T(8,128)(2,1)S(1)} %slice.48), channel_id=1, source_target_pairs={{0,4},{2,6},{4,0},{6,2},{8,12},{10,14},{12,8},{14,10},{16,20},{18,... | collective-permute-start | bytes 1179656 | tf_op jit(solution)/shard_map/ppermute | solution.py:37
  75.3 36.1 %all-to-all-start.1 = ((bf16[4,96,1536]{2,1,0:T(8,128)(2,1)}), bf16[4,96,1536]{2,1,0:T(8,128)(2,1)}, u32[]{:S(2)}, u32[]{:S(2)}) async-start(bf16[4,96,1536]{2,1,0:T(8,128)(2,1)} %pad_maximum_fusion), calls=%async_computation.1 | async-start | bytes 2359296 | tf_op jit(solution)/shard_map/all_to_all | solution.py:51
  79.6 150.6 %all-gather.3.cloned.1.call-start = ((), (), s32[]{:S(2)}) async-start(), calls=%async_computation.8 | async-start | bytes 5898240 | tf_op jit(solution)/shard_map/all_gather | solution.py:593
  111.5 31.5 %collective-permute-start.22 = (bf16[256,1536]{1,0:T(8,128)(2,1)}, bf16[256,1536]{1,0:T(8,128)(2,1)}, u32[]{:S(2)}, u32[]{:S(2)}) collective-permute-start(bf16[256,1536]{1,0:T(8,128)(2,1)} %fusion.6.refs_2_.refs_12_), channel_id=1, source_target_pairs={{0,2},{2,0},{4,6},{6,4},{8,10},{10,8},{12,14},{14,12},{16,18},{18,... | collective-permute-start | bytes 2359304 | tf_op jit(solution)/shard_map/ppermute | solution.py:37
  111.9 31.1 %collective-permute-start.23 = (bf16[256,1536]{1,0:T(8,128)(2,1)}, bf16[256,1536]{1,0:T(8,128)(2,1)}, u32[]{:S(2)}, u32[]{:S(2)}) collective-permute-start(bf16[256,1536]{1,0:T(8,128)(2,1)} %fusion.6.refs_2_.refs_12_), channel_id=1, source_target_pairs={{0,4},{2,6},{4,0},{6,2},{8,12},{10,14},{12,8},{14,10},{16,20},{18,... | collective-permute-start | bytes 2359304 | tf_op jit(solution)/shard_map/ppermute | solution.py:37
  112.6 30.4 %collective-permute-start.24 = (bf16[4,96,768]{2,1,0:T(8,128)(2,1)}, bf16[4,96,768]{2,1,0:T(8,128)(2,1)}, u32[]{:S(2)}, u32[]{:S(2)}) collective-permute-start(bf16[4,96,768]{2,1,0:T(8,128)(2,1)} %bitcast_dynamic-update-slice_fusion.4), channel_id=1, source_target_pairs={{0,6},{2,4},{4,2},{6,0},{8,14},{10,12},{12,10},{14,8},{16,22},{18,... | collective-permute-start | bytes 1769480 | tf_op jit(solution)/shard_map/ppermute | solution.py:37
  143.0 47.0 %all-to-all-start.2 = ((bf16[8,96,512]{2,1,0:T(8,128)(2,1)}), bf16[8,96,512]{2,1,0:T(8,128)(2,1)S(1)}, u32[]{:S(2)}, u32[]{:S(2)}) async-start(bf16[8,96,512]{2,1,0:T(8,128)(2,1)} %copy-done.16), calls=%async_computation.2 | async-start | bytes 1572864 | tf_op jit(solution)/shard_map/all_to_all | solution.py:51
  146.5 172.3 %all-gather.5.cloned.1.call-start = ((), (), s32[]{:S(2)}) async-start(), calls=%async_computation.9 | async-start | bytes 5013504 | tf_op jit(solution)/shard_map/all_gather | solution.py:601
  196.1 219.6 %reduce-scatter.2.cloned.1.call-start = ((), (), s32[]{:S(2)}) async-start(), calls=%async_computation.10 | async-start | bytes 5898240 | tf_op jit(solution)/shard_map/reduce_scatter | solution.py:636
  228.0 27.6 %collective-permute-start.28 = (bf16[256,1536]{1,0:T(8,128)(2,1)}, bf16[256,1536]{1,0:T(8,128)(2,1)}, u32[]{:S(2)}, u32[]{:S(2)}) collective-permute-start(bf16[256,1536]{1,0:T(8,128)(2,1)} %fusion.6.refs_2_.refs_12_), channel_id=1, source_target_pairs={{0,1},{1,0},{2,3},{3,2},{4,5},{5,4},{6,7},{7,6},{8,9},{9,8},{10,11... | collective-permute-start | bytes 2359304 | tf_op jit(solution)/shard_map/ppermute | solution.py:41
  256.2 27.7 %collective-permute-start.45 = (bf16[256,1536]{1,0:T(8,128)(2,1)S(1)}, bf16[256,1536]{1,0:T(8,128)(2,1)S(1)}, u32[]{:S(2)}, u32[]{:S(2)}) collective-permute-start(bf16[256,1536]{1,0:T(8,128)(2,1)S(1)} %get-tuple-element.233), channel_id=1, source_target_pairs={{0,1},{1,0},{2,3},{3,2},{4,5},{5,4},{6,7},{7,6},{8,9},{9,8},{10,11... | collective-permute-start | bytes 2359304 | tf_op jit(solution)/shard_map/ppermute | solution.py:41
  287.0 31.9 %collective-permute-start.44 = (bf16[256,1536]{1,0:T(8,128)(2,1)}, bf16[256,1536]{1,0:T(8,128)(2,1)}, u32[]{:S(2)}, u32[]{:S(2)}) collective-permute-start(bf16[256,1536]{1,0:T(8,128)(2,1)} %add_convert_fusion.4), channel_id=1, source_target_pairs={{0,6},{2,4},{4,2},{6,0},{8,14},{10,12},{12,10},{14,8},{16,22},{18,... | collective-permute-start | bytes 2359304 | tf_op jit(solution)/shard_map/ppermute | solution.py:37
  333.2 32.8 %all-to-all-start.3 = ((bf16[8,96,512]{2,1,0:T(8,128)(2,1)}), bf16[8,96,512]{2,1,0:T(8,128)(2,1)S(1)}, u32[]{:S(2)}, u32[]{:S(2)}) async-start(bf16[8,96,512]{2,1,0:T(8,128)(2,1)} %bitcast.28), calls=%async_computation.3 | async-start | bytes 1572864 | tf_op jit(solution)/shard_map/all_to_all | solution.py:51
  337.1 27.4 %collective-permute-start.49 = (bf16[256,1536]{1,0:T(8,128)(2,1)}, bf16[256,1536]{1,0:T(8,128)(2,1)S(1)}, u32[]{:S(2)}, u32[]{:S(2)}) collective-permute-start(bf16[256,1536]{1,0:T(8,128)(2,1)} %add_convert_fusion.3), channel_id=1, source_target_pairs={{0,2},{2,0},{4,6},{6,4},{8,10},{10,8},{12,14},{14,12},{16,18},{18,... | collective-permute-start | bytes 2359304 | tf_op jit(solution)/shard_map/ppermute | solution.py:37
  367.0 48.7 %all-to-all-start.4 = ((bf16[4,384,768]{2,1,0:T(8,128)(2,1)}), bf16[4,384,768]{2,1,0:T(8,128)(2,1)S(1)}, u32[]{:S(2)}, u32[]{:S(2)}) async-start(bf16[4,384,768]{2,1,0:T(8,128)(2,1)} %bitcast.117), calls=%async_computation.4 | async-start | bytes 4718592 | tf_op jit(solution)/shard_map/all_to_all | solution.py:51
  370.6 45.1 %collective-permute-start.51 = (bf16[256,1536]{1,0:T(8,128)(2,1)}, bf16[256,1536]{1,0:T(8,128)(2,1)}, u32[]{:S(2)}, u32[]{:S(2)}) collective-permute-start(bf16[256,1536]{1,0:T(8,128)(2,1)} %add_convert_fusion.1), channel_id=1, source_target_pairs={{0,6},{2,4},{4,2},{6,0},{8,14},{10,12},{12,10},{14,8},{16,22},{18,... | collective-permute-start | bytes 2359304 | tf_op jit(solution)/shard_map/ppermute | solution.py:37
  417.1 56.2 %all-to-all-start.5 = ((bf16[8,288,512]{2,1,0:T(8,128)(2,1)}), bf16[8,288,512]{2,1,0:T(8,128)(2,1)S(1)}, u32[]{:S(2)}, u32[]{:S(2)}) async-start(bf16[8,288,512]{2,1,0:T(8,128)(2,1)} %get-tuple-element.265), calls=%async_computation.6 | async-start | bytes 4718592 | tf_op jit(solution)/shard_map/all_to_all | solution.py:51
  425.7 35.0 %collective-permute-start.59 = (bf16[768,288]{0,1:T(8,128)(2,1)}, bf16[768,288]{0,1:T(8,128)(2,1)}, u32[]{:S(2)}, u32[]{:S(2)}) collective-permute-start(bf16[768,288]{0,1:T(8,128)(2,1)} %bitcast.129), channel_id=1, source_target_pairs={{0,16},{2,18},{4,20},{6,22},{8,24},{10,26},{12,28},{14,30},{16,0},... | collective-permute-start | bytes 1327112 | tf_op jit(solution)/shard_map/ppermute | solution.py:37
  429.1 44.2 %collective-permute-start.55 = (bf16[96,1536]{1,0:T(8,128)(2,1)}, bf16[96,1536]{1,0:T(8,128)(2,1)S(1)}, u32[]{:S(2)}, u32[]{:S(2)}) collective-permute-start(bf16[96,1536]{1,0:T(8,128)(2,1)} %get-tuple-element.331), channel_id=1, source_target_pairs={{0,2},{2,0},{4,6},{6,4},{8,10},{10,8},{12,14},{14,12},{16,18},{18,... | collective-permute-start | bytes 884744 | tf_op jit(solution)/shard_map/ppermute | solution.py:37
  430.7 42.6 %collective-permute-start.56 = (bf16[96,1536]{1,0:T(8,128)(2,1)}, bf16[96,1536]{1,0:T(8,128)(2,1)}, u32[]{:S(2)}, u32[]{:S(2)}) collective-permute-start(bf16[96,1536]{1,0:T(8,128)(2,1)} %get-tuple-element.330), channel_id=1, source_target_pairs={{0,4},{2,6},{4,0},{6,2},{8,12},{10,14},{12,8},{14,10},{16,20},{18,... | collective-permute-start | bytes 884744 | tf_op jit(solution)/shard_map/ppermute | solution.py:37
  431.9 41.4 %collective-permute-start.57 = (bf16[96,1536]{1,0:T(8,128)(2,1)}, bf16[96,1536]{1,0:T(8,128)(2,1)}, u32[]{:S(2)}, u32[]{:S(2)}) collective-permute-start(bf16[96,1536]{1,0:T(8,128)(2,1)} %get-tuple-element.329), channel_id=1, source_target_pairs={{0,6},{2,4},{4,2},{6,0},{8,14},{10,12},{12,10},{14,8},{16,22},{18,... | collective-permute-start | bytes 884744 | tf_op jit(solution)/shard_map/ppermute | solution.py:37
  (117 other events, 1272.6 us)
Sparse Core Ops, SparseCore 0:
  111.6 93.6 all-gather.2
  208.7 95.6 all-gather.4
  319.0 92.9 reduce-scatter.1

commit v5 on v4

--- a/solution.py
+++ b/solution.py
@@ -674,12 +674,15 @@
     out_sums = []
     for k in range(1, planes):
         far = lax.dynamic_index_in_dim(out_term, plane_at ^ k, 0, keepdims=False)
-        out_sums.append(hop(far.astype(bf16), PLANE * k))
+        out_sums.append(far.astype(bf16))
     out_total = out_pair[0]
     for far in out_far:
         out_total = out_total + far.astype(f32)
     output = (mid + out_total).astype(bf16)
-    back, out_sums, unit_back, output, head_sum = tie((back, out_sums, unit_back, output, head_sum))
+    back, _, unit_back, output, head_sum, first_sum = tie(
+        (back, out_sums, unit_back, output, head_sum, hop(out_sums[0], PLANE))
+    )
+    out_sums = [first_sum] + [hop(far, PLANE * k) for k, far in enumerate(out_sums[1:], 2)]
     head_sums = exchange(head_sum, SPANS)
     for far in out_sums:
         out_grad = out_grad + far.astype(f32)

time: 518 us -> 511 us (0.986)
  waiting for transfers between devices: 157 us -> 148 us
    ppermute x34, waiting for transfers between devices: 126 us -> 118 us  [hop(): lax.ppermute(value, 'fsdp', [(i, i ^ distance) for i in range(count)])]
  transfers between devices with their start and end apart: 72 -> 72, of which waited for: 22 -> 23; matrix products, arithmetic and copies ran while one was open for 18% -> 18% of each run, Pallas kernels for 27% -> 27%
where the time goes in v5:
time: 511 us; the launch traced here: 505 us
  waiting for transfers between devices  148 us (29%)
  Pallas kernels  142 us (28%)
  starting transfers between devices  90.6 us (18%)
  local copies, waits for them, and re-layouts  56.5 us (11%)
  other arithmetic  39.1 us (8%)
  between operations  14.8 us (3%)
  matrix products  13.3 us (3%)
    ppermute x34, waiting for transfers between devices, hop(): lax.ppermute(value, 'fsdp', [(i, i ^ distance) for i in range(count)])  118 us
    pallas_call x1, Pallas kernels, attention_backward(): pl.pallas_call(backward_kernel, grid=(SPANS,), in_specs=[whole(q_t), whol...  42.7 us
    ppermute x34, starting transfers between devices, hop(): lax.ppermute(value, 'fsdp', [(i, i ^ distance) for i in range(count)])  39.1 us
    pallas_call x2, Pallas kernels, feed(): pl.pallas_call(functools.partial(feed_kernel, pairs), in_specs=[vmem] * (...  33.7 us
    all_to_all x7, starting transfers between devices, exchange(): return lax.all_to_all(value, 'fsdp', 0, 0, axis_index_groups=groups)  28 us
    all_to_all x7, waiting for transfers between devices, exchange(): return lax.all_to_all(value, 'fsdp', 0, 0, axis_index_groups=groups)  23.2 us
    pallas_call x1, Pallas kernels, attention_forward(): pl.pallas_call(forward_kernel, grid=(SPANS,), in_specs=[pl.BlockSpec((HEA...  22.8 us
    ppermute x28, starting transfers between devices, swap(): return lax.ppermute(value, 'tp', [(0, 1), (1, 0)])  22.7 us
  transfers between devices with their start and end apart: 72, of which 23 were waited for; matrix products, arithmetic and copies ran while one was open for 18% of the time, Pallas kernels for 27%

profile of v5, /device:TPU:1, one launch (start us, length us, event | category | flops | bytes accessed | tf_op | source)
XLA Modules:
  0.0 504.9 jit_solution(7191960250860870780)
XLA Ops:
  16.6 3.8 all-to-all-start
  37.8 3.9 multiply_sine_fusion
  43.5 14.8 %collective-permute-done.15.refs_12_ = bf16[256,1536]{1,0:T(8,128)(2,1)} collective-permute-done((bf16[256,1536]{1,0:T(8,128)(2,1)}, bf16[256,1536]{1,0:T(8,128)(2,1)}, u32[]{:S(2)}, u32[]{:S(2)}) %collective-permute-start.15) | collective-permute-done | bytes 786464 | tf_op jit(solution)/shard_map/ppermute | solution.py:37
  63.4 6.6 %collective-permute-done.6 = bf16[128,1536]{1,0:T(8,128)(2,1)S(1)} collective-permute-done((bf16[128,1536]{1,0:T(8,128)(2,1)S(1)}, bf16[128,1536]{1,0:T(8,128)(2,1)S(1)}, u32[]{:S(2)}, u32[]{:S(2)}) %collective-permute-start.6) | collective-permute-done | bytes 393248 | tf_op jit(solution)/shard_map/ppermute | solution.py:37
  75.3 4.3 all-to-all-start.1
  92.9 18.5 %project.1 = (bf16[8,512,1536]{2,1,0:T(8,128)(2,1)}, f32[8,1536]{1,0:T(8,128)}, bf16[96,4096]{1,0:T(8,128)(2,1)}, bf16[96,4096]{1,0:T(8,128)(2,1)}, bf16[96,4096...) custom-call(bf16[256,1536]{1,0:T(8,128)(2,1)} %refs_0_.1, ...), custom_call_target="tpu_custom_call" | custom-call | flops 1024 | bytes 1024 | tf_op jit(solution)/shard_map/project/pallas_call | solution.py:142
  116.5 22.8 %attention_forward.1 = (bf16[8,96,512]{2,1,0:T(8,128)(2,1)S(1)}, f32[96,4096]{1,0:T(8,128)S(1)}, f32[1,4096]{1,0:T(1,128)S(1)}) custom-call(bf16[96,4096]{1,0:T(8,128)(2,1)S(1)} %copy-done.5, bf16[4096,96]{1,0:T(8,128)(2,1)S(1)} %copy-done.4, bf16[96,4096]{1,0:T(8,128)(2,1)S(1)} %copy-done.15, s32[1,4096]{1,0:T(1,128)S(1)} %bitcast.112, ...), custom_call_target="tpu_custom_call" | custom-call | flops 1024 | bytes 1024 | tf_op jit(solution)/shard_map/attention_forward/pallas_call | solution.py:210
  154.3 17.1 %collective-permute-done.25.refs_6_.refs_18_ = bf16[256,1536]{1,0:T(8,128)(2,1)} collective-permute-done((bf16[256,1536]{1,0:T(8,128)(2,1)}, bf16[256,1536]{1,0:T(8,128)(2,1)}, u32[]{:S(2)}, u32[]{:S(2)}) %collective-permute-start.25) | collective-permute-done | bytes 786464 | tf_op jit(solution)/shard_map/ppermute | solution.py:37
  171.3 18.6 %all-to-all-done.2 = bf16[8,96,512]{2,1,0:T(8,128)(2,1)S(1)} async-done(((bf16[8,96,512]{2,1,0:T(8,128)(2,1)}), bf16[8,96,512]{2,1,0:T(8,128)(2,1)S(1)}, u32[]{:S(2)}, u32[]{:S(2)}) %all-to-all-start.2) | async-done | bytes 786464 | tf_op jit(solution)/shard_map/all_to_all | solution.py:51
  206.8 17.1 %collective-permute-done.29.refs_0_.refs_2_ = bf16[256,1536]{1,0:T(8,128)(2,1)S(1)} collective-permute-done((bf16[256,1536]{1,0:T(8,128)(2,1)S(1)}, bf16[256,1536]{1,0:T(8,128)(2,1)S(1)}, u32[]{:S(2)}, u32[]{:S(2)}) %collective-permute-start.29) | collective-permute-done | bytes 786464 | tf_op jit(solution)/shard_map/ppermute | solution.py:37
  230.2 16.6 %feed.2 = (f32[256,1536]{1,0:T(8,128)}, bf16[256,1536]{1,0:T(8,128)(2,1)S(1)}, f32[256,1536]{1,0:T(8,128)}, bf16[256,1536]{1,0:T(8,128)(2,1)S(1)}, bf16[512,1024...) custom-call(bf16[256,1536]{1,0:T(8,128)(2,1)S(1)} %collective-permut, ...), custom_call_target="tpu_custom_call" | custom-call | flops 1024 | bytes 1024 | tf_op jit(solution)/shard_map/feed/pallas_call | solution.py:444
  246.8 5.4 %collective-permute-done.35.refs_4_.refs_6_ = bf16[256,1536]{1,0:T(8,128)(2,1)} collective-permute-done((bf16[256,1536]{1,0:T(8,128)(2,1)S(1)}, bf16[256,1536]{1,0:T(8,128)(2,1)}, u32[]{:S(2)}, u32[]{:S(2)}) %collective-permute-start.35) | collective-permute-done | bytes 786464 | tf_op jit(solution)/shard_map/ppermute | solution.py:37
  259.7 17.1 %feed.3 = (f32[256,1536]{1,0:T(8,128)}, bf16[256,1536]{1,0:T(8,128)(2,1)S(1)}, f32[256,1536]{1,0:T(8,128)}, bf16[256,1536]{1,0:T(8,128)(2,1)}, bf16[512,1024]{1,...) custom-call(bf16[256,1536]{1,0:T(8,128)(2,1)S(1)} %multiply_convert_, ...), custom_call_target="tpu_custom_call" | custom-call | flops 1024 | bytes 1024 | tf_op jit(solution)/shard_map/feed/pallas_call | solution.py:444
  288.7 15.1 %unit_grads.1 = bf16[1536,1536]{1,0:T(8,128)(2,1)} custom-call(bf16[256,1536]{1,0:T(8,128)(2,1)S(1)} %multiply_convert_fusion.refs_0_, bf16[256,1536]{1,0:T(8,128)(2,1)} %collective-permute-done.27.refs_1_, bf16[256,1536]{1,0:T(8,128)(2,1)S(1)} %collective-permute-done.29.refs_0_.refs_2_, bf16[256,1536]{1,0:T(8,128)(2,1)S(1)} %collective-permute-done.31.refs_1_.refs_3_, ...), custom_call_target="tpu_custom_call" | custom-call | flops 1024 | bytes 1024 | tf_op jit(solution)/shard_map/unit_grads/pallas_call | solution.py:397
  305.6 13.3 %collective-permute-done.44 = bf16[256,1536]{1,0:T(8,128)(2,1)} collective-permute-done((bf16[256,1536]{1,0:T(8,128)(2,1)}, bf16[256,1536]{1,0:T(8,128)(2,1)}, u32[]{:S(2)}, u32[]{:S(2)}) %collective-permute-start.44) | collective-permute-done | bytes 786464 | tf_op jit(solution)/shard_map/ppermute | solution.py:37
  321.2 3.9 fusion.22
  328.8 4.4 convolution_convert_fusion.1
  333.2 3.9 all-to-all-start.3
  344.7 19.8 %collective-permute-done.49 = bf16[256,1536]{1,0:T(8,128)(2,1)S(1)} collective-permute-done((bf16[256,1536]{1,0:T(8,128)(2,1)}, bf16[256,1536]{1,0:T(8,128)(2,1)S(1)}, u32[]{:S(2)}, u32[]{:S(2)}) %collective-permute-start.49) | collective-permute-done | bytes 786464 | tf_op jit(solution)/shard_map/ppermute | solution.py:37
  367.0 3.6 all-to-all-start.4
  373.0 42.7 %attention_backward.1 = (bf16[8,288,512]{2,1,0:T(8,128)(2,1)}, bf16[1536,288]{1,0:T(8,128)(2,1)}) custom-call(bf16[96,4096]{1,0:T(8,128)(2,1)} %get-tuple-element.166.q_t_ref, bf16[4096,96]{1,0:T(8,128)(2,1)} %get-tuple-element.167.q_ref, bf16[96,4096]{1,0:T(8,128)(2,1)} %get-tuple-element.168.k_t_ref, bf16[4096,96]{1,0:T(8,128)(2,1)} %get-tuple-element.169.k_ref, ...), custom_call_target="tpu_custom_call" | custom-call | flops 1024 | bytes 1024 | tf_op jit(solution)/shard_map/attention_backward/pallas_call | solution.py:294
  439.8 14.6 %collective-permute-done.56 = bf16[768,288]{0,1:T(8,128)(2,1)} collective-permute-done((bf16[768,288]{0,1:T(8,128)(2,1)}, bf16[768,288]{0,1:T(8,128)(2,1)}, u32[]{:S(2)}, u32[]{:S(2)}) %collective-permute-start.56) | collective-permute-done | bytes 442400 | tf_op jit(solution)/shard_map/ppermute | solution.py:37
  465.5 4.3 input_terms.1
  478.4 5.2 %all-to-all-start.6 = ((bf16[8,96,288]{2,1,0:T(8,128)(2,1)}), bf16[8,96,288]{2,1,0:T(8,128)(2,1)S(1)}, u32[]{:S(2)}, u32[]{:S(2)}) async-start(bf16[8,96,288]{2,1,0:T(8,128)(2,1)} %bitcast.125), calls=%async_computation.7 | async-start | bytes 1179648 | tf_op jit(solution)/shard_map/all_to_all | solution.py:51
  (347 shorter events, 192.7 us)
Async XLA Ops:
  16.6 55.6 %all-to-all-start = ((bf16[16,96,290]{2,1,0:T(8,128)(2,1)}), bf16[16,96,290]{2,1,0:T(8,128)(2,1)S(1)}, u32[]{:S(2)}, u32[]{:S(2)}) async-start(bf16[16,96,290]{2,1,0:T(8,128)(2,1)} %head_cut.1), calls=%async_computation | async-start | bytes 2359296 | tf_op jit(solution)/shard_map/all_to_all | solution.py:51
  20.4 51.8 %collective-permute-start.10 = (bf16[96,768]{1,0:T(8,128)(2,1)}, bf16[96,768]{1,0:T(8,128)(2,1)}, u32[]{:S(2)}, u32[]{:S(2)}) collective-permute-start(bf16[96,768]{1,0:T(8,128)(2,1)} %bitcast.130), channel_id=1, source_target_pairs={{0,24},{2,26},{4,28},{6,30},{8,16},{10,18},{12,20},{14,22},{16,8},... | collective-permute-start | bytes 442376 | tf_op jit(solution)/shard_map/ppermute | solution.py:37
  36.7 33.2 %collective-permute-start.6 = (bf16[128,1536]{1,0:T(8,128)(2,1)S(1)}, bf16[128,1536]{1,0:T(8,128)(2,1)S(1)}, u32[]{:S(2)}, u32[]{:S(2)}) collective-permute-start(bf16[128,1536]{1,0:T(8,128)(2,1)S(1)} %slice.47), channel_id=1, source_target_pairs={{0,2},{2,0},{4,6},{6,4},{8,10},{10,8},{12,14},{14,12},{16,18},{18,... | collective-permute-start | bytes 1179656 | tf_op jit(solution)/shard_map/ppermute | solution.py:37
  37.3 33.9 %collective-permute-start.7 = (bf16[128,1536]{1,0:T(8,128)(2,1)S(1)}, bf16[128,1536]{1,0:T(8,128)(2,1)S(1)}, u32[]{:S(2)}, u32[]{:S(2)}) collective-permute-start(bf16[128,1536]{1,0:T(8,128)(2,1)S(1)} %slice.48), channel_id=1, source_target_pairs={{0,4},{2,6},{4,0},{6,2},{8,12},{10,14},{12,8},{14,10},{16,20},{18,... | collective-permute-start | bytes 1179656 | tf_op jit(solution)/shard_map/ppermute | solution.py:37
  75.3 36.1 %all-to-all-start.1 = ((bf16[4,96,1536]{2,1,0:T(8,128)(2,1)}), bf16[4,96,1536]{2,1,0:T(8,128)(2,1)}, u32[]{:S(2)}, u32[]{:S(2)}) async-start(bf16[4,96,1536]{2,1,0:T(8,128)(2,1)} %pad_maximum_fusion), calls=%async_computation.1 | async-start | bytes 2359296 | tf_op jit(solution)/shard_map/all_to_all | solution.py:51
  79.6 150.6 %all-gather.3.cloned.1.call-start = ((), (), s32[]{:S(2)}) async-start(), calls=%async_computation.8 | async-start | bytes 5898240 | tf_op jit(solution)/shard_map/all_gather | solution.py:593
  111.5 31.5 %collective-permute-start.22 = (bf16[256,1536]{1,0:T(8,128)(2,1)}, bf16[256,1536]{1,0:T(8,128)(2,1)}, u32[]{:S(2)}, u32[]{:S(2)}) collective-permute-start(bf16[256,1536]{1,0:T(8,128)(2,1)} %fusion.6.refs_2_.refs_12_), channel_id=1, source_target_pairs={{0,2},{2,0},{4,6},{6,4},{8,10},{10,8},{12,14},{14,12},{16,18},{18,... | collective-permute-start | bytes 2359304 | tf_op jit(solution)/shard_map/ppermute | solution.py:37
  111.9 31.1 %collective-permute-start.23 = (bf16[256,1536]{1,0:T(8,128)(2,1)}, bf16[256,1536]{1,0:T(8,128)(2,1)}, u32[]{:S(2)}, u32[]{:S(2)}) collective-permute-start(bf16[256,1536]{1,0:T(8,128)(2,1)} %fusion.6.refs_2_.refs_12_), channel_id=1, source_target_pairs={{0,4},{2,6},{4,0},{6,2},{8,12},{10,14},{12,8},{14,10},{16,20},{18,... | collective-permute-start | bytes 2359304 | tf_op jit(solution)/shard_map/ppermute | solution.py:37
  112.6 30.4 %collective-permute-start.24 = (bf16[4,96,768]{2,1,0:T(8,128)(2,1)}, bf16[4,96,768]{2,1,0:T(8,128)(2,1)}, u32[]{:S(2)}, u32[]{:S(2)}) collective-permute-start(bf16[4,96,768]{2,1,0:T(8,128)(2,1)} %bitcast_dynamic-update-slice_fusion.4), channel_id=1, source_target_pairs={{0,6},{2,4},{4,2},{6,0},{8,14},{10,12},{12,10},{14,8},{16,22},{18,... | collective-permute-start | bytes 1769480 | tf_op jit(solution)/shard_map/ppermute | solution.py:37
  143.0 47.0 %all-to-all-start.2 = ((bf16[8,96,512]{2,1,0:T(8,128)(2,1)}), bf16[8,96,512]{2,1,0:T(8,128)(2,1)S(1)}, u32[]{:S(2)}, u32[]{:S(2)}) async-start(bf16[8,96,512]{2,1,0:T(8,128)(2,1)} %copy-done.16), calls=%async_computation.2 | async-start | bytes 1572864 | tf_op jit(solution)/shard_map/all_to_all | solution.py:51
  146.5 172.3 %all-gather.5.cloned.1.call-start = ((), (), s32[]{:S(2)}) async-start(), calls=%async_computation.9 | async-start | bytes 5013504 | tf_op jit(solution)/shard_map/all_gather | solution.py:601
  196.1 219.6 %reduce-scatter.2.cloned.1.call-start = ((), (), s32[]{:S(2)}) async-start(), calls=%async_computation.10 | async-start | bytes 5898240 | tf_op jit(solution)/shard_map/reduce_scatter | solution.py:636
  228.0 27.6 %collective-permute-start.28 = (bf16[256,1536]{1,0:T(8,128)(2,1)}, bf16[256,1536]{1,0:T(8,128)(2,1)}, u32[]{:S(2)}, u32[]{:S(2)}) collective-permute-start(bf16[256,1536]{1,0:T(8,128)(2,1)} %fusion.6.refs_2_.refs_12_), channel_id=1, source_target_pairs={{0,1},{1,0},{2,3},{3,2},{4,5},{5,4},{6,7},{7,6},{8,9},{9,8},{10,11... | collective-permute-start | bytes 2359304 | tf_op jit(solution)/shard_map/ppermute | solution.py:41
  256.2 27.7 %collective-permute-start.45 = (bf16[256,1536]{1,0:T(8,128)(2,1)S(1)}, bf16[256,1536]{1,0:T(8,128)(2,1)S(1)}, u32[]{:S(2)}, u32[]{:S(2)}) collective-permute-start(bf16[256,1536]{1,0:T(8,128)(2,1)S(1)} %get-tuple-element.231), channel_id=1, source_target_pairs={{0,1},{1,0},{2,3},{3,2},{4,5},{5,4},{6,7},{7,6},{8,9},{9,8},{10,11... | collective-permute-start | bytes 2359304 | tf_op jit(solution)/shard_map/ppermute | solution.py:41
  287.0 31.9 %collective-permute-start.44 = (bf16[256,1536]{1,0:T(8,128)(2,1)}, bf16[256,1536]{1,0:T(8,128)(2,1)}, u32[]{:S(2)}, u32[]{:S(2)}) collective-permute-start(bf16[256,1536]{1,0:T(8,128)(2,1)} %add_convert_fusion.4), channel_id=1, source_target_pairs={{0,6},{2,4},{4,2},{6,0},{8,14},{10,12},{12,10},{14,8},{16,22},{18,... | collective-permute-start | bytes 2359304 | tf_op jit(solution)/shard_map/ppermute | solution.py:37
  333.2 32.8 %all-to-all-start.3 = ((bf16[8,96,512]{2,1,0:T(8,128)(2,1)}), bf16[8,96,512]{2,1,0:T(8,128)(2,1)S(1)}, u32[]{:S(2)}, u32[]{:S(2)}) async-start(bf16[8,96,512]{2,1,0:T(8,128)(2,1)} %bitcast.28), calls=%async_computation.3 | async-start | bytes 1572864 | tf_op jit(solution)/shard_map/all_to_all | solution.py:51
  337.1 27.4 %collective-permute-start.49 = (bf16[256,1536]{1,0:T(8,128)(2,1)}, bf16[256,1536]{1,0:T(8,128)(2,1)S(1)}, u32[]{:S(2)}, u32[]{:S(2)}) collective-permute-start(bf16[256,1536]{1,0:T(8,128)(2,1)} %add_convert_fusion.3), channel_id=1, source_target_pairs={{0,2},{2,0},{4,6},{6,4},{8,10},{10,8},{12,14},{14,12},{16,18},{18,... | collective-permute-start | bytes 2359304 | tf_op jit(solution)/shard_map/ppermute | solution.py:37
  367.0 48.7 %all-to-all-start.4 = ((bf16[4,384,768]{2,1,0:T(8,128)(2,1)}), bf16[4,384,768]{2,1,0:T(8,128)(2,1)S(1)}, u32[]{:S(2)}, u32[]{:S(2)}) async-start(bf16[4,384,768]{2,1,0:T(8,128)(2,1)} %bitcast.117), calls=%async_computation.4 | async-start | bytes 4718592 | tf_op jit(solution)/shard_map/all_to_all | solution.py:51
  370.6 45.1 %collective-permute-start.51 = (bf16[256,1536]{1,0:T(8,128)(2,1)}, bf16[256,1536]{1,0:T(8,128)(2,1)}, u32[]{:S(2)}, u32[]{:S(2)}) collective-permute-start(bf16[256,1536]{1,0:T(8,128)(2,1)} %add_convert_fusion.1), channel_id=1, source_target_pairs={{0,6},{2,4},{4,2},{6,0},{8,14},{10,12},{12,10},{14,8},{16,22},{18,... | collective-permute-start | bytes 2359304 | tf_op jit(solution)/shard_map/ppermute | solution.py:37
  417.1 46.1 %all-to-all-start.5 = ((bf16[8,288,512]{2,1,0:T(8,128)(2,1)}), bf16[8,288,512]{2,1,0:T(8,128)(2,1)S(1)}, u32[]{:S(2)}, u32[]{:S(2)}) async-start(bf16[8,288,512]{2,1,0:T(8,128)(2,1)} %get-tuple-element.263), calls=%async_computation.6 | async-start | bytes 4718592 | tf_op jit(solution)/shard_map/all_to_all | solution.py:51
  425.7 28.7 %collective-permute-start.56 = (bf16[768,288]{0,1:T(8,128)(2,1)}, bf16[768,288]{0,1:T(8,128)(2,1)}, u32[]{:S(2)}, u32[]{:S(2)}) collective-permute-start(bf16[768,288]{0,1:T(8,128)(2,1)} %bitcast.129), channel_id=1, source_target_pairs={{0,16},{2,18},{4,20},{6,22},{8,24},{10,26},{12,28},{14,30},{16,0},... | collective-permute-start | bytes 1327112 | tf_op jit(solution)/shard_map/ppermute | solution.py:37
  429.1 31.2 %collective-permute-start.52 = (bf16[96,1536]{1,0:T(8,128)(2,1)}, bf16[96,1536]{1,0:T(8,128)(2,1)S(1)}, u32[]{:S(2)}, u32[]{:S(2)}) collective-permute-start(bf16[96,1536]{1,0:T(8,128)(2,1)} %get-tuple-element.327), channel_id=1, source_target_pairs={{0,2},{2,0},{4,6},{6,4},{8,10},{10,8},{12,14},{14,12},{16,18},{18,... | collective-permute-start | bytes 884744 | tf_op jit(solution)/shard_map/ppermute | solution.py:37
  430.7 32.5 %collective-permute-start.53 = (bf16[96,1536]{1,0:T(8,128)(2,1)}, bf16[96,1536]{1,0:T(8,128)(2,1)}, u32[]{:S(2)}, u32[]{:S(2)}) collective-permute-start(bf16[96,1536]{1,0:T(8,128)(2,1)} %get-tuple-element.326), channel_id=1, source_target_pairs={{0,4},{2,6},{4,0},{6,2},{8,12},{10,14},{12,8},{14,10},{16,20},{18,... | collective-permute-start | bytes 884744 | tf_op jit(solution)/shard_map/ppermute | solution.py:37
  431.9 31.3 %collective-permute-start.54 = (bf16[96,1536]{1,0:T(8,128)(2,1)}, bf16[96,1536]{1,0:T(8,128)(2,1)}, u32[]{:S(2)}, u32[]{:S(2)}) collective-permute-start(bf16[96,1536]{1,0:T(8,128)(2,1)} %get-tuple-element.325), channel_id=1, source_target_pairs={{0,6},{2,4},{4,2},{6,0},{8,14},{10,12},{12,10},{14,8},{16,22},{18,... | collective-permute-start | bytes 884744 | tf_op jit(solution)/shard_map/ppermute | solution.py:37
  (117 other events, 1294.4 us)
Sparse Core Ops, SparseCore 0:
  111.6 93.6 all-gather.2
  208.7 95.6 all-gather.4
  319.0 92.9 reduce-scatter.1

commit v6 on v5

--- a/solution.py
+++ b/solution.py
@@ -79,8 +79,8 @@
 
 def project_kernel(*refs):
     pieces, (place_ref, head_ref, cos_ref, sin_ref) = refs[:2 * SPANS], refs[2 * SPANS:2 * SPANS + 4]
-    normed_ref, gain_ref, q_t_ref, k_t_ref, v_t_ref, q_ref, k_ref, v_ref = refs[2 * SPANS + 4:2 * SPANS + 12]
-    in_buf, out_buf, in_sem, out_sem = refs[2 * SPANS + 12:]
+    normed_ref, gain_ref, q_t_ref, k_t_ref, v_t_ref, k_ref, v_ref = refs[2 * SPANS + 4:2 * SPANS + 11]
+    in_buf, out_buf, in_sem, out_sem = refs[2 * SPANS + 11:]
     rows = pieces[0].shape[0]
     place, core = place_ref[0], place_ref[1]
 
@@ -119,14 +119,15 @@
         product = dot(normed, head_ref[:, :3 * HEAD_SIZE]).T
         here = pl.ds(pl.multiple_of((place ^ pair) * 2 * rows, 2 * rows), 2 * rows)
         cosine, sine = cos_ref[:, here], sin_ref[:, here]
-        for number, (t_ref, n_ref) in enumerate(((q_t_ref, q_ref), (k_t_ref, k_ref))):
+        for number, (t_ref, n_ref) in enumerate(((q_t_ref, None), (k_t_ref, k_ref))):
             first = product[number * HEAD_SIZE:number * HEAD_SIZE + HALF]
             second = product[number * HEAD_SIZE + HALF:(number + 1) * HEAD_SIZE]
             turned = jnp.concatenate(
                 [first * cosine - second * sine, second * cosine + first * sine], axis=0
             )
             t_ref[:, here] = turned.astype(bf16)
-            n_ref[here, :] = turned.T.astype(bf16)
+            if n_ref is not None:
+                n_ref[here, :] = turned.T.astype(bf16)
         value = product[2 * HEAD_SIZE:3 * HEAD_SIZE]
         v_t_ref[:, here] = value.astype(bf16)
         v_ref[here, :] = value.T.astype(bf16)
@@ -142,13 +143,13 @@
     return pl.pallas_call(
         project_kernel,
         in_specs=[anywhere] * len(pieces) + [pl.BlockSpec(memory_space=pltpu.SMEM), vmem, vmem, vmem],
-        out_specs=[anywhere] + [vmem] * 7,
+        out_specs=[anywhere] + [vmem] * 6,
         out_shape=[
             jax.ShapeDtypeStruct((SPANS, 2 * rows, width), bf16),
             jax.ShapeDtypeStruct((8, width), f32),
         ]
         + [jax.ShapeDtypeStruct((HEAD_SIZE, tokens), bf16)] * 3
-        + [jax.ShapeDtypeStruct((tokens, HEAD_SIZE), bf16)] * 3,
+        + [jax.ShapeDtypeStruct((tokens, HEAD_SIZE), bf16)] * 2,
         scratch_shapes=[
             pltpu.VMEM((3, 2 * rows, width), bf16),
             pltpu.VMEM((2, 2 * rows, width), bf16),
@@ -233,8 +234,8 @@
     )(q_t, k, v_t, id_row, id_col)
 
 
-def backward_kernel(q_t_ref, q_ref, k_t_ref, k_ref, v_ref, dout_ref, out_ref, lse_ref, id_row_ref, id_col_ref,
-                    cos_ref, sin_ref, normed_ref, grad_ref, weight_grad_ref, delta_ref, dout_n_ref, dq_ref, sum_ref):
+def backward_kernel(q_t_ref, k_t_ref, k_ref, v_ref, dout_ref, out_ref, lse_ref, id_row_ref, id_col_ref,
+                    cos_ref, sin_ref, normed_ref, grad_ref, weight_grad_ref, delta_ref, dq_ref, sum_ref):
     block = pl.program_id(0)
 
     @pl.when(block == 0)
@@ -243,7 +244,6 @@
             dout = dout_ref[at]
             here = slice(at * SPAN, (at + 1) * SPAN)
             delta_ref[:, here] = jnp.sum(dout.astype(f32) * out_ref[:, here], axis=0, keepdims=True)
-            dout_n_ref[here, :] = dout.astype(f32).T.astype(bf16)
         dq_ref[...] = jnp.zeros(dq_ref.shape, f32)
         sum_ref[...] = jnp.zeros(sum_ref.shape, f32)
 
@@ -260,23 +260,23 @@
         probs = jnp.exp2(jnp.where(allowed, scores, masked_score))
         dprobs = dot(value, dout_ref[at])
         dscores = (probs * (dprobs - delta_ref[:, rows])).astype(bf16)
-        dvalue = dvalue + dot(probs.astype(bf16), dout_n_ref[rows, :])
-        dkey = dkey + dot(dscores, q_ref[rows, :])
+        dvalue = dvalue + dot(dout_ref[at], probs.astype(bf16), 1, 1)
+        dkey = dkey + dot(q_t_ref[:, rows], dscores, 1, 1)
         dq_ref[at] += dot(key_t, dscores)
         return dkey, dvalue
 
-    zero = jnp.zeros((SPAN, HEAD_SIZE), f32)
+    zero = jnp.zeros((HEAD_SIZE, SPAN), f32)
     carry = step(block, (zero, zero), True)
     dkey, dvalue = lax.fori_loop(block + 1, SPANS, lambda at, c: step(at, c, False), carry)
     cosine, sine = cos_ref[...], sin_ref[...]
-    for number, grad in enumerate((dq_ref[block], dkey.T)):
+    for number, grad in enumerate((dq_ref[block], dkey)):
         first = grad[:HALF] * scale
         second = grad[HALF:] * scale
         turned = jnp.concatenate(
             [first * cosine + second * sine, second * cosine - first * sine], axis=0
         )
         grad_ref[0, number * HEAD_SIZE:(number + 1) * HEAD_SIZE, :] = turned.astype(bf16)
-    grad_ref[0, 2 * HEAD_SIZE:, :] = dvalue.T.astype(bf16)
+    grad_ref[0, 2 * HEAD_SIZE:, :] = dvalue.astype(bf16)
     sum_ref[...] += dot(grad_ref[0], normed_ref[0])
 
     @pl.when(block == SPANS - 1)
@@ -284,7 +284,7 @@
         weight_grad_ref[...] = sum_ref[...].T.astype(bf16)
 
 
-def attention_backward(q_t, q, k_t, k, v, dout, out, lse, id_row, id_col, cosine, sine, normed):
+def attention_backward(q_t, k_t, k, v, dout, out, lse, id_row, id_col, cosine, sine, normed):
     tokens = k.shape[0]
     width = normed.shape[2]
     whole = lambda array: pl.BlockSpec(array.shape, lambda i: (0,) * array.ndim)
@@ -295,7 +295,7 @@
         backward_kernel,
         grid=(SPANS,),
         in_specs=[
-            whole(q_t), whole(q), wide, tall, tall, whole(dout), whole(out), whole(lse), whole(id_row),
+            whole(q_t), wide, tall, tall, whole(dout), whole(out), whole(lse), whole(id_row),
             pl.BlockSpec((SPAN, id_col.shape[1]), lambda i: (i, 0)), table, table,
             pl.BlockSpec((1, SPAN, width), lambda i: (i, 0, 0)),
         ],
@@ -309,14 +309,13 @@
         ],
         scratch_shapes=[
             pltpu.VMEM((1, tokens), f32),
-            pltpu.VMEM((tokens, HEAD_SIZE), bf16),
             pltpu.VMEM((SPANS, HEAD_SIZE, SPAN), f32),
             pltpu.VMEM((3 * HEAD_SIZE, width), f32),
         ],
         compiler_params=pltpu.CompilerParams(vmem_limit_bytes=56 * 2**20),
         cost_estimate=brief,
         name="attention_backward",
-    )(q_t, q, k_t, k, v, dout, out, lse, id_row, id_col, cosine, sine, normed)
+    )(q_t, k_t, k, v, dout, out, lse, id_row, id_col, cosine, sine, normed)
 
 
 def head_finish_kernel(sum_ref, q_ref, k_ref, v_ref, q_out, k_out, v_out, product_ref):
@@ -587,7 +586,7 @@
 
     places = jnp.stack([place, t]).astype(jnp.int32)
 
-    normed, gains, q_t, k_t, v_t, q, key, v = project(pieces, head_set, places, cosine, sine)
+    normed, gains, q_t, k_t, v_t, key, v = project(pieces, head_set, places, cosine, sine)
     gain_a, gain_m = gains[0:1], gains[1:2]
     q_t, out_0, out_1, out_2, dmlp_own, unit_own = tie((q_t, out_0, out_1, out_2, dmlp_own, unit_own))
     unit_weight = lax.all_gather(unit_own, "fsdp", axis=0, tiled=True, axis_index_groups=lines)
@@ -655,7 +654,7 @@
     out_term = exchange(out_term.reshape(PLANE, planes * shard, -1), PLANE)
     out_far += [hop(out_low[2], 3)]
     grads, head_low = attention_backward(
-        q_t, q, k_t, key, v, dout, out_full, lse, id_row, id_col, cosine, sine, normed
+        q_t, k_t, key, v, dout, out_full, lse, id_row, id_col, cosine, sine, normed
     )
     grads, head_low, out_term, out_far, unit_sum = tie((grads, head_low, out_term, out_far, unit_sum))
     head_low = head_low.reshape(cubes, SPANS * shard, 3 * HEAD_SIZE)

time: 511 us -> 510 us (level)
  transfers between devices with their start and end apart: 72 -> 72, of which waited for: 23 -> 24; matrix products, arithmetic and copies ran while one was open for 18% -> 18% of each run, Pallas kernels for 27% -> 27%
where the time goes in v6:
time: 510 us; the launch traced here: 503 us
  waiting for transfers between devices  149 us (29%)
  Pallas kernels  140 us (27%)
  starting transfers between devices  90.6 us (18%)
  local copies, waits for them, and re-layouts  56.6 us (11%)
  other arithmetic  39.1 us (8%)
  between operations  14.8 us (3%)
  matrix products  13.4 us (3%)
    ppermute x34, waiting for transfers between devices, hop(): lax.ppermute(value, 'fsdp', [(i, i ^ distance) for i in range(count)])  118 us
    pallas_call x1, Pallas kernels, attention_backward(): pl.pallas_call(backward_kernel, grid=(SPANS,), in_specs=[whole(q_t), wide...  40.9 us
    ppermute x34, starting transfers between devices, hop(): lax.ppermute(value, 'fsdp', [(i, i ^ distance) for i in range(count)])  39.2 us
    pallas_call x2, Pallas kernels, feed(): pl.pallas_call(functools.partial(feed_kernel, pairs), in_specs=[vmem] * (...  33.8 us
    all_to_all x7, starting transfers between devices, exchange(): return lax.all_to_all(value, 'fsdp', 0, 0, axis_index_groups=groups)  27.5 us
    all_to_all x7, waiting for transfers between devices, exchange(): return lax.all_to_all(value, 'fsdp', 0, 0, axis_index_groups=groups)  23.2 us
    ppermute x28, starting transfers between devices, swap(): return lax.ppermute(value, 'tp', [(0, 1), (1, 0)])  23.1 us
    pallas_call x1, Pallas kernels, attention_forward(): pl.pallas_call(forward_kernel, grid=(SPANS,), in_specs=[pl.BlockSpec((HEA...  22.8 us
  transfers between devices with their start and end apart: 72, of which 24 were waited for; matrix products, arithmetic and copies ran while one was open for 18% of the time, Pallas kernels for 27%

profile of v6, /device:TPU:1, one launch (start us, length us, event | category | flops | bytes accessed | tf_op | source)
XLA Modules:
  0.0 503.4 jit_solution(12610200981006143493)
XLA Ops:
  16.6 3.8 all-to-all-start
  37.8 3.9 multiply_sine_fusion
  43.5 14.8 %collective-permute-done.15.refs_12_ = bf16[256,1536]{1,0:T(8,128)(2,1)} collective-permute-done((bf16[256,1536]{1,0:T(8,128)(2,1)}, bf16[256,1536]{1,0:T(8,128)(2,1)}, u32[]{:S(2)}, u32[]{:S(2)}) %collective-permute-start.15) | collective-permute-done | bytes 786464 | tf_op jit(solution)/shard_map/ppermute | solution.py:37
  63.4 6.6 %collective-permute-done.6 = bf16[128,1536]{1,0:T(8,128)(2,1)S(1)} collective-permute-done((bf16[128,1536]{1,0:T(8,128)(2,1)S(1)}, bf16[128,1536]{1,0:T(8,128)(2,1)S(1)}, u32[]{:S(2)}, u32[]{:S(2)}) %collective-permute-start.6) | collective-permute-done | bytes 393248 | tf_op jit(solution)/shard_map/ppermute | solution.py:37
  75.3 4.3 all-to-all-start.1
  92.9 18.0 %project.1 = (bf16[8,512,1536]{2,1,0:T(8,128)(2,1)}, f32[8,1536]{1,0:T(8,128)}, bf16[96,4096]{1,0:T(8,128)(2,1)}, bf16[96,4096]{1,0:T(8,128)(2,1)}, bf16[96,4096...) custom-call(bf16[256,1536]{1,0:T(8,128)(2,1)} %refs_0_.1, ...), custom_call_target="tpu_custom_call" | custom-call | flops 1024 | bytes 1024 | tf_op jit(solution)/shard_map/project/pallas_call | solution.py:143
  116.0 22.8 %attention_forward.1 = (bf16[8,96,512]{2,1,0:T(8,128)(2,1)S(1)}, f32[96,4096]{1,0:T(8,128)S(1)}, f32[1,4096]{1,0:T(1,128)S(1)}) custom-call(bf16[96,4096]{1,0:T(8,128)(2,1)S(1)} %copy-done.5, bf16[4096,96]{1,0:T(8,128)(2,1)S(1)} %copy-done.4, bf16[96,4096]{1,0:T(8,128)(2,1)S(1)} %copy-done.15, s32[1,4096]{1,0:T(1,128)S(1)} %bitcast.112, ...), custom_call_target="tpu_custom_call" | custom-call | flops 1024 | bytes 1024 | tf_op jit(solution)/shard_map/attention_forward/pallas_call | solution.py:211
  153.8 17.1 %collective-permute-done.25.refs_6_.refs_18_ = bf16[256,1536]{1,0:T(8,128)(2,1)} collective-permute-done((bf16[256,1536]{1,0:T(8,128)(2,1)}, bf16[256,1536]{1,0:T(8,128)(2,1)}, u32[]{:S(2)}, u32[]{:S(2)}) %collective-permute-start.25) | collective-permute-done | bytes 786464 | tf_op jit(solution)/shard_map/ppermute | solution.py:37
  170.9 18.6 %all-to-all-done.2 = bf16[8,96,512]{2,1,0:T(8,128)(2,1)S(1)} async-done(((bf16[8,96,512]{2,1,0:T(8,128)(2,1)}), bf16[8,96,512]{2,1,0:T(8,128)(2,1)S(1)}, u32[]{:S(2)}, u32[]{:S(2)}) %all-to-all-start.2) | async-done | bytes 786464 | tf_op jit(solution)/shard_map/all_to_all | solution.py:51
  206.3 17.1 %collective-permute-done.29.refs_0_.refs_2_ = bf16[256,1536]{1,0:T(8,128)(2,1)S(1)} collective-permute-done((bf16[256,1536]{1,0:T(8,128)(2,1)S(1)}, bf16[256,1536]{1,0:T(8,128)(2,1)S(1)}, u32[]{:S(2)}, u32[]{:S(2)}) %collective-permute-start.29) | collective-permute-done | bytes 786464 | tf_op jit(solution)/shard_map/ppermute | solution.py:37
  229.7 16.7 %feed.2 = (f32[256,1536]{1,0:T(8,128)}, bf16[256,1536]{1,0:T(8,128)(2,1)S(1)}, f32[256,1536]{1,0:T(8,128)}, bf16[256,1536]{1,0:T(8,128)(2,1)S(1)}, bf16[512,1024...) custom-call(bf16[256,1536]{1,0:T(8,128)(2,1)S(1)} %collective-permut, ...), custom_call_target="tpu_custom_call" | custom-call | flops 1024 | bytes 1024 | tf_op jit(solution)/shard_map/feed/pallas_call | solution.py:443
  246.4 5.4 %collective-permute-done.35.refs_4_.refs_6_ = bf16[256,1536]{1,0:T(8,128)(2,1)} collective-permute-done((bf16[256,1536]{1,0:T(8,128)(2,1)S(1)}, bf16[256,1536]{1,0:T(8,128)(2,1)}, u32[]{:S(2)}, u32[]{:S(2)}) %collective-permute-start.35) | collective-permute-done | bytes 786464 | tf_op jit(solution)/shard_map/ppermute | solution.py:37
  259.1 17.1 %feed.3 = (f32[256,1536]{1,0:T(8,128)}, bf16[256,1536]{1,0:T(8,128)(2,1)S(1)}, f32[256,1536]{1,0:T(8,128)}, bf16[256,1536]{1,0:T(8,128)(2,1)}, bf16[512,1024]{1,...) custom-call(bf16[256,1536]{1,0:T(8,128)(2,1)S(1)} %multiply_convert_, ...), custom_call_target="tpu_custom_call" | custom-call | flops 1024 | bytes 1024 | tf_op jit(solution)/shard_map/feed/pallas_call | solution.py:443
  288.2 15.1 %unit_grads.1 = bf16[1536,1536]{1,0:T(8,128)(2,1)} custom-call(bf16[256,1536]{1,0:T(8,128)(2,1)S(1)} %multiply_convert_fusion.refs_0_, bf16[256,1536]{1,0:T(8,128)(2,1)} %collective-permute-done.27.refs_1_, bf16[256,1536]{1,0:T(8,128)(2,1)S(1)} %collective-permute-done.29.refs_0_.refs_2_, bf16[256,1536]{1,0:T(8,128)(2,1)S(1)} %collective-permute-done.31.refs_1_.refs_3_, ...), custom_call_target="tpu_custom_call" | custom-call | flops 1024 | bytes 1024 | tf_op jit(solution)/shard_map/unit_grads/pallas_call | solution.py:396
  305.1 13.2 %collective-permute-done.44 = bf16[256,1536]{1,0:T(8,128)(2,1)} collective-permute-done((bf16[256,1536]{1,0:T(8,128)(2,1)}, bf16[256,1536]{1,0:T(8,128)(2,1)}, u32[]{:S(2)}, u32[]{:S(2)}) %collective-permute-start.44) | collective-permute-done | bytes 786464 | tf_op jit(solution)/shard_map/ppermute | solution.py:37
  320.7 3.9 fusion.22
  328.3 4.4 convolution_convert_fusion.1
  332.7 3.9 all-to-all-start.3
  344.2 19.8 %collective-permute-done.49 = bf16[256,1536]{1,0:T(8,128)(2,1)S(1)} collective-permute-done((bf16[256,1536]{1,0:T(8,128)(2,1)}, bf16[256,1536]{1,0:T(8,128)(2,1)S(1)}, u32[]{:S(2)}, u32[]{:S(2)}) %collective-permute-start.49) | collective-permute-done | bytes 786464 | tf_op jit(solution)/shard_map/ppermute | solution.py:37
  366.5 3.6 all-to-all-start.4
  372.4 40.9 %attention_backward.1 = (bf16[8,288,512]{2,1,0:T(8,128)(2,1)}, bf16[1536,288]{1,0:T(8,128)(2,1)}) custom-call(bf16[96,4096]{1,0:T(8,128)(2,1)} %get-tuple-element.165.q_t_ref, bf16[96,4096]{1,0:T(8,128)(2,1)} %get-tuple-element.166.k_t_ref, bf16[4096,96]{1,0:T(8,128)(2,1)} %get-tuple-element.167.k_ref, bf16[4096,96]{1,0:T(8,128)(2,1)} %get-tuple-element.168.v_ref, ...), custom_call_target="tpu_custom_call" | custom-call | flops 1024 | bytes 1024 | tf_op jit(solution)/shard_map/attention_backward/pallas_call | solution.py:294
  438.9 14.1 %collective-permute-done.56 = bf16[768,288]{0,1:T(8,128)(2,1)} collective-permute-done((bf16[768,288]{0,1:T(8,128)(2,1)}, bf16[768,288]{0,1:T(8,128)(2,1)}, u32[]{:S(2)}, u32[]{:S(2)}) %collective-permute-start.56) | collective-permute-done | bytes 442400 | tf_op jit(solution)/shard_map/ppermute | solution.py:37
  464.3 4.3 input_terms.1
  477.4 4.7 all-to-all-start.6
  (347 shorter events, 194.6 us)
Async XLA Ops:
  16.6 55.6 %all-to-all-start = ((bf16[16,96,290]{2,1,0:T(8,128)(2,1)}), bf16[16,96,290]{2,1,0:T(8,128)(2,1)S(1)}, u32[]{:S(2)}, u32[]{:S(2)}) async-start(bf16[16,96,290]{2,1,0:T(8,128)(2,1)} %head_cut.1), calls=%async_computation | async-start | bytes 2359296 | tf_op jit(solution)/shard_map/all_to_all | solution.py:51
  20.4 51.8 %collective-permute-start.10 = (bf16[96,768]{1,0:T(8,128)(2,1)}, bf16[96,768]{1,0:T(8,128)(2,1)}, u32[]{:S(2)}, u32[]{:S(2)}) collective-permute-start(bf16[96,768]{1,0:T(8,128)(2,1)} %bitcast.130), channel_id=1, source_target_pairs={{0,24},{2,26},{4,28},{6,30},{8,16},{10,18},{12,20},{14,22},{16,8},... | collective-permute-start | bytes 442376 | tf_op jit(solution)/shard_map/ppermute | solution.py:37
  36.7 33.2 %collective-permute-start.6 = (bf16[128,1536]{1,0:T(8,128)(2,1)S(1)}, bf16[128,1536]{1,0:T(8,128)(2,1)S(1)}, u32[]{:S(2)}, u32[]{:S(2)}) collective-permute-start(bf16[128,1536]{1,0:T(8,128)(2,1)S(1)} %slice.47), channel_id=1, source_target_pairs={{0,2},{2,0},{4,6},{6,4},{8,10},{10,8},{12,14},{14,12},{16,18},{18,... | collective-permute-start | bytes 1179656 | tf_op jit(solution)/shard_map/ppermute | solution.py:37
  37.3 33.9 %collective-permute-start.7 = (bf16[128,1536]{1,0:T(8,128)(2,1)S(1)}, bf16[128,1536]{1,0:T(8,128)(2,1)S(1)}, u32[]{:S(2)}, u32[]{:S(2)}) collective-permute-start(bf16[128,1536]{1,0:T(8,128)(2,1)S(1)} %slice.48), channel_id=1, source_target_pairs={{0,4},{2,6},{4,0},{6,2},{8,12},{10,14},{12,8},{14,10},{16,20},{18,... | collective-permute-start | bytes 1179656 | tf_op jit(solution)/shard_map/ppermute | solution.py:37
  75.3 35.6 %all-to-all-start.1 = ((bf16[4,96,1536]{2,1,0:T(8,128)(2,1)}), bf16[4,96,1536]{2,1,0:T(8,128)(2,1)}, u32[]{:S(2)}, u32[]{:S(2)}) async-start(bf16[4,96,1536]{2,1,0:T(8,128)(2,1)} %pad_maximum_fusion), calls=%async_computation.1 | async-start | bytes 2359296 | tf_op jit(solution)/shard_map/all_to_all | solution.py:51
  79.6 150.1 %all-gather.3.cloned.1.call-start = ((), (), s32[]{:S(2)}) async-start(), calls=%async_computation.8 | async-start | bytes 5898240 | tf_op jit(solution)/shard_map/all_gather | solution.py:592
  110.9 31.5 %collective-permute-start.22 = (bf16[256,1536]{1,0:T(8,128)(2,1)}, bf16[256,1536]{1,0:T(8,128)(2,1)}, u32[]{:S(2)}, u32[]{:S(2)}) collective-permute-start(bf16[256,1536]{1,0:T(8,128)(2,1)} %fusion.6.refs_2_.refs_12_), channel_id=1, source_target_pairs={{0,2},{2,0},{4,6},{6,4},{8,10},{10,8},{12,14},{14,12},{16,18},{18,... | collective-permute-start | bytes 2359304 | tf_op jit(solution)/shard_map/ppermute | solution.py:37
  111.4 31.1 %collective-permute-start.23 = (bf16[256,1536]{1,0:T(8,128)(2,1)}, bf16[256,1536]{1,0:T(8,128)(2,1)}, u32[]{:S(2)}, u32[]{:S(2)}) collective-permute-start(bf16[256,1536]{1,0:T(8,128)(2,1)} %fusion.6.refs_2_.refs_12_), channel_id=1, source_target_pairs={{0,4},{2,6},{4,0},{6,2},{8,12},{10,14},{12,8},{14,10},{16,20},{18,... | collective-permute-start | bytes 2359304 | tf_op jit(solution)/shard_map/ppermute | solution.py:37
  112.1 30.4 %collective-permute-start.24 = (bf16[4,96,768]{2,1,0:T(8,128)(2,1)}, bf16[4,96,768]{2,1,0:T(8,128)(2,1)}, u32[]{:S(2)}, u32[]{:S(2)}) collective-permute-start(bf16[4,96,768]{2,1,0:T(8,128)(2,1)} %bitcast_dynamic-update-slice_fusion.4), channel_id=1, source_target_pairs={{0,6},{2,4},{4,2},{6,0},{8,14},{10,12},{12,10},{14,8},{16,22},{18,... | collective-permute-start | bytes 1769480 | tf_op jit(solution)/shard_map/ppermute | solution.py:37
  142.5 47.0 %all-to-all-start.2 = ((bf16[8,96,512]{2,1,0:T(8,128)(2,1)}), bf16[8,96,512]{2,1,0:T(8,128)(2,1)S(1)}, u32[]{:S(2)}, u32[]{:S(2)}) async-start(bf16[8,96,512]{2,1,0:T(8,128)(2,1)} %copy-done.16), calls=%async_computation.2 | async-start | bytes 1572864 | tf_op jit(solution)/shard_map/all_to_all | solution.py:51
  146.0 172.3 %all-gather.5.cloned.1.call-start = ((), (), s32[]{:S(2)}) async-start(), calls=%async_computation.9 | async-start | bytes 5013504 | tf_op jit(solution)/shard_map/all_gather | solution.py:600
  195.6 218.9 %reduce-scatter.2.cloned.1.call-start = ((), (), s32[]{:S(2)}) async-start(), calls=%async_computation.10 | async-start | bytes 5898240 | tf_op jit(solution)/shard_map/reduce_scatter | solution.py:635
  227.5 27.6 %collective-permute-start.28 = (bf16[256,1536]{1,0:T(8,128)(2,1)}, bf16[256,1536]{1,0:T(8,128)(2,1)}, u32[]{:S(2)}, u32[]{:S(2)}) collective-permute-start(bf16[256,1536]{1,0:T(8,128)(2,1)} %fusion.6.refs_2_.refs_12_), channel_id=1, source_target_pairs={{0,1},{1,0},{2,3},{3,2},{4,5},{5,4},{6,7},{7,6},{8,9},{9,8},{10,11... | collective-permute-start | bytes 2359304 | tf_op jit(solution)/shard_map/ppermute | solution.py:41
  255.6 27.7 %collective-permute-start.45 = (bf16[256,1536]{1,0:T(8,128)(2,1)S(1)}, bf16[256,1536]{1,0:T(8,128)(2,1)S(1)}, u32[]{:S(2)}, u32[]{:S(2)}) collective-permute-start(bf16[256,1536]{1,0:T(8,128)(2,1)S(1)} %get-tuple-element.229), channel_id=1, source_target_pairs={{0,1},{1,0},{2,3},{3,2},{4,5},{5,4},{6,7},{7,6},{8,9},{9,8},{10,11... | collective-permute-start | bytes 2359304 | tf_op jit(solution)/shard_map/ppermute | solution.py:41
  286.5 31.8 %collective-permute-start.44 = (bf16[256,1536]{1,0:T(8,128)(2,1)}, bf16[256,1536]{1,0:T(8,128)(2,1)}, u32[]{:S(2)}, u32[]{:S(2)}) collective-permute-start(bf16[256,1536]{1,0:T(8,128)(2,1)} %add_convert_fusion.4), channel_id=1, source_target_pairs={{0,6},{2,4},{4,2},{6,0},{8,14},{10,12},{12,10},{14,8},{16,22},{18,... | collective-permute-start | bytes 2359304 | tf_op jit(solution)/shard_map/ppermute | solution.py:37
  332.7 32.8 %all-to-all-start.3 = ((bf16[8,96,512]{2,1,0:T(8,128)(2,1)}), bf16[8,96,512]{2,1,0:T(8,128)(2,1)S(1)}, u32[]{:S(2)}, u32[]{:S(2)}) async-start(bf16[8,96,512]{2,1,0:T(8,128)(2,1)} %bitcast.28), calls=%async_computation.3 | async-start | bytes 1572864 | tf_op jit(solution)/shard_map/all_to_all | solution.py:51
  336.6 27.4 %collective-permute-start.49 = (bf16[256,1536]{1,0:T(8,128)(2,1)}, bf16[256,1536]{1,0:T(8,128)(2,1)S(1)}, u32[]{:S(2)}, u32[]{:S(2)}) collective-permute-start(bf16[256,1536]{1,0:T(8,128)(2,1)} %add_convert_fusion.3), channel_id=1, source_target_pairs={{0,2},{2,0},{4,6},{6,4},{8,10},{10,8},{12,14},{14,12},{16,18},{18,... | collective-permute-start | bytes 2359304 | tf_op jit(solution)/shard_map/ppermute | solution.py:37
  366.5 48.1 %all-to-all-start.4 = ((bf16[4,384,768]{2,1,0:T(8,128)(2,1)}), bf16[4,384,768]{2,1,0:T(8,128)(2,1)S(1)}, u32[]{:S(2)}, u32[]{:S(2)}) async-start(bf16[4,384,768]{2,1,0:T(8,128)(2,1)} %bitcast.117), calls=%async_computation.4 | async-start | bytes 4718592 | tf_op jit(solution)/shard_map/all_to_all | solution.py:51
  370.1 44.4 %collective-permute-start.51 = (bf16[256,1536]{1,0:T(8,128)(2,1)}, bf16[256,1536]{1,0:T(8,128)(2,1)}, u32[]{:S(2)}, u32[]{:S(2)}) collective-permute-start(bf16[256,1536]{1,0:T(8,128)(2,1)} %add_convert_fusion.1), channel_id=1, source_target_pairs={{0,6},{2,4},{4,2},{6,0},{8,14},{10,12},{12,10},{14,8},{16,22},{18,... | collective-permute-start | bytes 2359304 | tf_op jit(solution)/shard_map/ppermute | solution.py:37
  415.9 46.0 %all-to-all-start.5 = ((bf16[8,288,512]{2,1,0:T(8,128)(2,1)}), bf16[8,288,512]{2,1,0:T(8,128)(2,1)S(1)}, u32[]{:S(2)}, u32[]{:S(2)}) async-start(bf16[8,288,512]{2,1,0:T(8,128)(2,1)} %get-tuple-element.261), calls=%async_computation.6 | async-start | bytes 4718592 | tf_op jit(solution)/shard_map/all_to_all | solution.py:51
  424.8 28.1 %collective-permute-start.56 = (bf16[768,288]{0,1:T(8,128)(2,1)}, bf16[768,288]{0,1:T(8,128)(2,1)}, u32[]{:S(2)}, u32[]{:S(2)}) collective-permute-start(bf16[768,288]{0,1:T(8,128)(2,1)} %bitcast.129), channel_id=1, source_target_pairs={{0,16},{2,18},{4,20},{6,22},{8,24},{10,26},{12,28},{14,30},{16,0},... | collective-permute-start | bytes 1327112 | tf_op jit(solution)/shard_map/ppermute | solution.py:37
  428.2 30.1 %collective-permute-start.52 = (bf16[96,1536]{1,0:T(8,128)(2,1)}, bf16[96,1536]{1,0:T(8,128)(2,1)S(1)}, u32[]{:S(2)}, u32[]{:S(2)}) collective-permute-start(bf16[96,1536]{1,0:T(8,128)(2,1)} %get-tuple-element.325), channel_id=1, source_target_pairs={{0,2},{2,0},{4,6},{6,4},{8,10},{10,8},{12,14},{14,12},{16,18},{18,... | collective-permute-start | bytes 884744 | tf_op jit(solution)/shard_map/ppermute | solution.py:37
  429.8 32.2 %collective-permute-start.53 = (bf16[96,1536]{1,0:T(8,128)(2,1)}, bf16[96,1536]{1,0:T(8,128)(2,1)}, u32[]{:S(2)}, u32[]{:S(2)}) collective-permute-start(bf16[96,1536]{1,0:T(8,128)(2,1)} %get-tuple-element.324), channel_id=1, source_target_pairs={{0,4},{2,6},{4,0},{6,2},{8,12},{10,14},{12,8},{14,10},{16,20},{18,... | collective-permute-start | bytes 884744 | tf_op jit(solution)/shard_map/ppermute | solution.py:37
  431.0 31.0 %collective-permute-start.54 = (bf16[96,1536]{1,0:T(8,128)(2,1)}, bf16[96,1536]{1,0:T(8,128)(2,1)}, u32[]{:S(2)}, u32[]{:S(2)}) collective-permute-start(bf16[96,1536]{1,0:T(8,128)(2,1)} %get-tuple-element.323), channel_id=1, source_target_pairs={{0,6},{2,4},{4,2},{6,0},{8,14},{10,12},{12,10},{14,8},{16,22},{18,... | collective-permute-start | bytes 884744 | tf_op jit(solution)/shard_map/ppermute | solution.py:37
  (117 other events, 1289.4 us)
Sparse Core Ops, SparseCore 0:
  111.1 93.6 all-gather.2
  208.2 95.4 all-gather.4
  318.5 92.9 reduce-scatter.1
